TPU v7x, 32 devices: a whole 2x2x4 slice. The times are simulated.
32 devices in a mesh: seq: 8 (over z, x), head: 4 (over y, core).
Axes of the slice: x: 2, y: 2, z: 4, core: 2. Of those that a mesh axis runs over, the one named last changes fastest.
Arguments:
- tokens: bfloat16 [2, 2048, 768], P(None, ('seq', 'head')), may hold values from -6 to 6
- positions: int32 [2, 2048], P(None, 'seq'), may hold values from 0 to 2047, each once within a row
- w_qkv: bfloat16 [768, 2304], P(('seq', 'head')), may hold values from -0.21875 to 0.21875
- qv_bias: bfloat16 [2, 768], P(None, ('seq', 'head')), may hold values from -3 to 3
- w_attn_out: bfloat16 [768, 768], P(('seq', 'head')), may hold values from -0.875 to 0.875
- attn_out_bias: bfloat16 [768], P(('seq', 'head')), may hold values from -3 to 3
- norm1_gain: bfloat16 [768], P(('seq', 'head')), may hold values from 0.5 to 1.5
- norm1_bias: bfloat16 [768], P(('seq', 'head')), may hold values from -3 to 3
- w_in: bfloat16 [768, 6144], P(('seq', 'head')), may hold values from -0.21875 to 0.21875
- in_bias: bfloat16 [6144], P(('seq', 'head')), may hold values from -3 to 3
- w_out: bfloat16 [3072, 768], P(('seq', 'head')), may hold values from -0.109375 to 0.109375
- out_bias: bfloat16 [768], P(('seq', 'head')), may hold values from -3 to 3
- norm2_gain: bfloat16 [768], P(('seq', 'head')), may hold values from 0.5 to 1.5
- norm2_bias: bfloat16 [768], P(('seq', 'head')), may hold values from -3 to 3
- cotangent: bfloat16 [2, 2048, 768], P(None, ('seq', 'head')), may hold values from -6 to 6
Outputs:
- output: bfloat16 [2, 2048, 768], P(None, ('seq', 'head'))
- input_grad: float32 [2, 2048, 768], P(None, ('seq', 'head'))
- grad_w_qkv: float32 [768, 2304], P(('seq', 'head'))
- grad_qv_bias: float32 [2, 768], P(None, ('seq', 'head'))
- grad_w_attn_out: float32 [768, 768], P(('seq', 'head'))
- grad_attn_out_bias: float32 [768], P(('seq', 'head'))
- grad_norm1_gain: float32 [768], P(('seq', 'head'))
- grad_norm1_bias: float32 [768], P(('seq', 'head'))
- grad_w_in: float32 [768, 6144], P(('seq', 'head'))
- grad_in_bias: float32 [6144], P(('seq', 'head'))
- grad_w_out: float32 [3072, 768], P(('seq', 'head'))
- grad_out_bias: float32 [768], P(('seq', 'head'))
- grad_norm2_gain: float32 [768], P(('seq', 'head'))
- grad_norm2_bias: float32 [768], P(('seq', 'head'))
Inputs may be any that keep to these rules, and one draw needn't show every extreme that they name: `positions`: each row holds every position 0 to 2047 exactly once.
All inputs are finite; a program needn't handle non-finite values.
Results may differ from a plain program's by a relative error of at most 0.039.
Values may be sent and summed in bfloat16 or wider, within the bound.
No kernel may reach another device: no remote copies, remote signals or barrier semaphores. Data moves between devices by JAX's collectives and lax.ppermute only.
A program may use at most 192 MiB of HBM per device.

v0:
```python
import functools

import jax
import jax.numpy as jnp
from jax import lax
from jax.experimental import pallas as pl
from jax.experimental.pallas import tpu as pltpu
from jax.sharding import Mesh
from jax.sharding import PartitionSpec as P

HEADS = 12
HEAD_DIM = 64
GROUPS = 4
GROUP_HEADS = HEADS // GROUPS
GROUP_WIDTH = GROUP_HEADS * HEAD_DIM
EPSILON = 1e-12
SCORE_SCALE = 0.125
LOG2E = 1.4426950408889634
LOWEST = -1e30
GRAD_TILE = 256
KEY_BLOCK = 512
FF_TILE = 256
SEQ_GROUP = ("s", "r", "x")
CHUNKS = ("e", "y", "c")
RING = ("s", "e", "r")
PLANE = ("x", "y")
SEQ_AXIS = ("s", "e", "r", "x")
EVERY = ("s", "e", "r", "x", "y", "c")
SWAP = ((0, 1), (1, 0))
BF16 = jnp.bfloat16
F32 = jnp.float32
VMEM_BYTES = 60 * 2**20


def nt(a, b):
    return lax.dot_general(a, b, (((1,), (1,)), ((), ())), preferred_element_type=F32)


def tn(a, b):
    return lax.dot_general(a, b, (((0,), (0,)), ((), ())), preferred_element_type=F32)


def nn(a, b):
    return lax.dot_general(a, b, (((1,), (0,)), ((), ())), preferred_element_type=F32)


def head_cols(head, base=0):
    return slice(base + head * HEAD_DIM, base + (head + 1) * HEAD_DIM)


def log2_scores(keys, queries, slope, key_pos, query_pos):
    products = nt(keys, queries)
    distances = jnp.abs(key_pos * slope - query_pos * slope)
    return products * (SCORE_SCALE * LOG2E) - distances


def column(row):
    return jnp.broadcast_to(row, (8, row.shape[1])).T[:, :1]


def key_blocks(kv_refs):
    start = 0
    for piece in kv_refs:
        yield piece, start
        start += piece.shape[0]


def turn_positions(pk_ref, column_ref):
    length = pk_ref.shape[1]

    def turn(row, carry):
        at = pl.ds(pl.multiple_of(row * length, length), length)
        column_ref[at, :] = column(pk_ref[pl.ds(row, 1), :])
        return carry

    lax.fori_loop(0, pk_ref.shape[0], turn, 0)


def attend_kernel(deps, count, first, last, slopes_ref, q_ref, pq_ref, pk_ref, *refs):
    refs = refs[deps:]
    kv_refs, refs = refs[:count], refs[count:]
    if not first:
        (sum_in_ref, stat_in_ref), refs = refs[:2], refs[2:]
    sum_ref, stat_ref = refs[:2]
    column_ref = refs[-1]
    rows = q_ref.shape[0]
    query_pos = pq_ref[...]
    turn_positions(pk_ref, column_ref)
    for head in range(GROUP_HEADS):
        slope = slopes_ref[head]
        queries = q_ref[:, head_cols(head)]
        if first:
            carry = (
                jnp.full((1, rows), LOWEST, F32),
                jnp.zeros((1, rows), F32),
                jnp.zeros((HEAD_DIM, rows), F32),
            )
        else:
            carry = (
                stat_in_ref[head : head + 1, :],
                stat_in_ref[GROUP_HEADS + head : GROUP_HEADS + head + 1, :],
                sum_in_ref[head_cols(head), :],
            )
        for kv_ref, start in key_blocks(kv_refs):

            def visit(block, carry, kv_ref=kv_ref, start=start):
                top, total, summed = carry
                at = pl.ds(pl.multiple_of(block * KEY_BLOCK, KEY_BLOCK), KEY_BLOCK)
                pos_at = pl.ds(
                    pl.multiple_of(start + block * KEY_BLOCK, KEY_BLOCK), KEY_BLOCK
                )
                keys = kv_ref[at, head_cols(head)]
                values = kv_ref[at, head_cols(head, GROUP_WIDTH)]
                scores = log2_scores(keys, queries, slope, column_ref[pos_at, :], query_pos)
                new_top = jnp.maximum(top, jnp.max(scores, axis=0, keepdims=True))
                weights = jnp.exp2(scores - new_top)
                shrink = jnp.exp2(top - new_top)
                total = total * shrink + jnp.sum(weights, axis=0, keepdims=True)
                summed = summed * shrink + tn(values, weights.astype(BF16))
                return new_top, total, summed

            carry = lax.fori_loop(0, kv_ref.shape[0] // KEY_BLOCK, visit, carry)
        top, total, summed = carry
        if last:
            attended = summed / total
            sum_ref[head_cols(head), :] = attended
            refs[2][:, head_cols(head)] = attended.T.astype(BF16)
            stat_ref[head : head + 1, :] = top + jnp.log2(total)
        else:
            sum_ref[head_cols(head), :] = summed
            stat_ref[head : head + 1, :] = top
            stat_ref[GROUP_HEADS + head : GROUP_HEADS + head + 1, :] = total


def attend(slopes, queries, query_pos, key_pos, key_values, state, last, earlier):
    rows, length = queries.shape[0], key_pos.size
    vmem = pl.BlockSpec(memory_space=pltpu.VMEM)
    count = len(key_values)
    first = state is None
    state = () if first else state
    outs = [
        jax.ShapeDtypeStruct((GROUP_WIDTH, rows), F32),
        jax.ShapeDtypeStruct((GROUP_HEADS * (1 if last else 2), rows), F32),
    ]
    if last:
        outs.append(jax.ShapeDtypeStruct((rows, GROUP_WIDTH), BF16))
    return pl.pallas_call(
        functools.partial(attend_kernel, len(earlier), count, first, last),
        out_shape=tuple(outs),
        in_specs=[pl.BlockSpec(memory_space=pltpu.SMEM)]
        + [vmem] * 3
        + [pl.BlockSpec(memory_space=pl.ANY)] * len(earlier)
        + [vmem] * (count + len(state)),
        out_specs=(vmem,) * len(outs),
        scratch_shapes=[pltpu.VMEM((length, 1), F32)],
        compiler_params=pltpu.CompilerParams(vmem_limit_bytes=VMEM_BYTES),
        cost_estimate=pl.CostEstimate(
            flops=64 * rows * length * GROUP_WIDTH,
            bytes_accessed=rows * length,
            transcendentals=rows * length * GROUP_HEADS,
        ),
        name="attend",
    )(slopes, queries, query_pos, key_pos, *earlier, *key_values, *state)


def attend_back_kernel(
    deps, count, first, last, slopes_ref, q_ref, pq_ref, pk_ref, do_ref, out_ref, lse_ref, *refs
):
    refs = refs[deps:]
    kv_refs, refs = refs[:count], refs[count:]
    if not first:
        dq_in_ref, refs = refs[0], refs[1:]
    dq_ref, dkv_refs, column_ref = refs[0], refs[1 : count + 1], refs[-1]
    rows = q_ref.shape[0]
    query_pos = pq_ref[...]
    turn_positions(pk_ref, column_ref)
    for head in range(GROUP_HEADS):
        slope = slopes_ref[head]
        queries = q_ref[:, head_cols(head)]
        out_grads = do_ref[:, head_cols(head)]
        log_sum = lse_ref[head : head + 1, :]
        delta = jnp.sum(
            out_grads.astype(F32).T * out_ref[head_cols(head), :], axis=0, keepdims=True
        )
        if first:
            query_grads = jnp.zeros((HEAD_DIM, rows), F32)
        else:
            query_grads = dq_in_ref[head_cols(head), :]
        for (kv_ref, start), dkv_ref in zip(key_blocks(kv_refs), dkv_refs):

            def visit(block, query_grads, kv_ref=kv_ref, start=start, dkv_ref=dkv_ref):
                at = pl.ds(pl.multiple_of(block * KEY_BLOCK, KEY_BLOCK), KEY_BLOCK)
                pos_at = pl.ds(
                    pl.multiple_of(start + block * KEY_BLOCK, KEY_BLOCK), KEY_BLOCK
                )
                keys = kv_ref[at, head_cols(head)]
                values = kv_ref[at, head_cols(head, GROUP_WIDTH)]
                scores = log2_scores(keys, queries, slope, column_ref[pos_at, :], query_pos)
                probs = jnp.exp2(scores - log_sum)
                prob_grads = nt(values, out_grads)
                score_grads = (probs * (prob_grads - delta)).astype(BF16)
                dkv_ref[at, head_cols(head, GROUP_WIDTH)] = nn(
                    probs.astype(BF16), out_grads
                ).astype(BF16)
                dkv_ref[at, head_cols(head)] = (nn(score_grads, queries) * SCORE_SCALE).astype(
                    BF16
                )
                return query_grads + tn(keys, score_grads)

            query_grads = lax.fori_loop(0, kv_ref.shape[0] // KEY_BLOCK, visit, query_grads)
        if last:
            dq_ref[:, head_cols(head)] = (query_grads * SCORE_SCALE).T.astype(BF16)
        else:
            dq_ref[head_cols(head), :] = query_grads


def attend_back(
    slopes,
    queries,
    query_pos,
    key_pos,
    out_grads,
    attended,
    log_sums,
    key_values,
    state,
    last,
    earlier,
):
    rows, length = queries.shape[0], key_pos.size
    vmem = pl.BlockSpec(memory_space=pltpu.VMEM)
    count = len(key_values)
    first = state is None
    state = () if first else (state,)
    query_out = (
        jax.ShapeDtypeStruct((rows, GROUP_WIDTH), BF16)
        if last
        else jax.ShapeDtypeStruct((GROUP_WIDTH, rows), F32)
    )
    return pl.pallas_call(
        functools.partial(attend_back_kernel, len(earlier), count, first, last),
        out_shape=(query_out,)
        + tuple(jax.ShapeDtypeStruct(piece.shape, BF16) for piece in key_values),
        in_specs=[pl.BlockSpec(memory_space=pltpu.SMEM)]
        + [vmem] * 6
        + [pl.BlockSpec(memory_space=pl.ANY)] * len(earlier)
        + [vmem] * (count + len(state)),
        out_specs=(vmem,) * (1 + count),
        scratch_shapes=[pltpu.VMEM((length, 1), F32)],
        compiler_params=pltpu.CompilerParams(vmem_limit_bytes=VMEM_BYTES),
        cost_estimate=pl.CostEstimate(
            flops=84 * rows * length * GROUP_WIDTH,
            bytes_accessed=rows * length,
            transcendentals=rows * length * GROUP_HEADS,
        ),
        name="attend_back",
    )(
        slopes,
        queries,
        query_pos,
        key_pos,
        out_grads,
        attended,
        log_sums,
        *earlier,
        *key_values,
        *state,
    )


def assemble(core_ref, own_ref, swap_ref, columns, target, sems):
    core = core_ref[0]
    copies = []
    for which, (piece, half) in enumerate(((own_ref, core), (swap_ref, 1 - core))):
        copy = pltpu.make_async_copy(piece.at[:, columns], target.at[half], sems.at[which])
        copy.start()
        copies.append(copy)
    return copies


def merged(parts_ref):
    return jnp.concatenate(
        [
            jnp.concatenate(
                [parts_ref[seq * GROUPS + group] for group in range(GROUPS)], axis=1
            )
            for seq in range(2)
        ]
    )


def first_norm_kernel(
    columns,
    core_ref,
    mixed_ref,
    rows_ref,
    vec_ref,
    own_ref,
    swap_ref,
    low_ref,
    hidden_ref,
    normal_ref,
    scale_ref,
    weight_ref,
    sems,
):
    for copy in assemble(core_ref, own_ref, swap_ref, columns, weight_ref, sems):
        copy.wait()
    mixed = merged(mixed_ref)
    lin = jnp.concatenate([nn(mixed, weight_ref[0]), nn(mixed, weight_ref[1])], axis=1)
    total = rows_ref[...].astype(F32) + (lin + vec_ref[2:3, :])
    normal, scale = normalised(total)
    hidden = normal * vec_ref[3:4, :] + vec_ref[4:5, :]
    low_ref[...] = hidden.astype(BF16)
    hidden_ref[...] = hidden
    normal_ref[...] = normal
    scale_ref[...] = scale


def normalised(values):
    centred = values - jnp.mean(values, axis=1, keepdims=True)
    variance = jnp.mean(centred * centred, axis=1, keepdims=True)
    scale = lax.rsqrt(variance + EPSILON)
    return centred * scale, scale


def norm_back(grads, normal, scale, gain):
    scaled = grads * gain
    return (
        scaled
        - jnp.mean(scaled, axis=1, keepdims=True)
        - normal * jnp.mean(scaled * normal, axis=1, keepdims=True)
    ) * scale


def column_sum(values):
    return jnp.sum(values, axis=0, keepdims=True)


def first_norm(core, mixed, rows, vectors, own, swap, columns):
    tokens, width = rows.shape
    vmem = pl.BlockSpec(memory_space=pltpu.VMEM)
    half = columns.stop - columns.start
    return pl.pallas_call(
        functools.partial(first_norm_kernel, columns),
        out_shape=(
            jax.ShapeDtypeStruct((tokens, width), BF16),
            jax.ShapeDtypeStruct((tokens, width), F32),
            jax.ShapeDtypeStruct((tokens, width), F32),
            jax.ShapeDtypeStruct((tokens, 1), F32),
            jax.ShapeDtypeStruct((2, width, half), BF16),
        ),
        in_specs=[pl.BlockSpec(memory_space=pltpu.SMEM)]
        + [vmem] * 3
        + [pl.BlockSpec(memory_space=pl.ANY)] * 2,
        out_specs=(vmem,) * 5,
        scratch_shapes=[pltpu.SemaphoreType.DMA((2,))],
        compiler_params=pltpu.CompilerParams(vmem_limit_bytes=VMEM_BYTES),
        cost_estimate=pl.CostEstimate(
            flops=64 * tokens * width * width, bytes_accessed=4 * width * width, transcendentals=0
        ),
        name="first_norm",
    )(core, mixed, rows, vectors, own, swap)


def ff_forward_kernel(
    in_columns,
    out_columns,
    core_ref,
    hidden_ref,
    bias_ref,
    own_ref,
    swap_ref,
    act_ref,
    slope_ref,
    gelu_ref,
    parts_ref,
    w_in_ref,
    w_out_ref,
    sems,
):
    in_copies = assemble(core_ref, own_ref, swap_ref, in_columns, w_in_ref, sems.at[0])
    out_copies = assemble(core_ref, own_ref, swap_ref, out_columns, w_out_ref, sems.at[1])
    for copy in in_copies:
        copy.wait()
    tokens = hidden_ref.shape[0]

    def expand(tile, carry):
        at = pl.ds(pl.multiple_of(tile * FF_TILE, FF_TILE), FF_TILE)
        rows = hidden_ref[at, :]
        gate = nn(rows, w_in_ref[0]) + bias_ref[0:1, :]
        up = nn(rows, w_in_ref[1]) + bias_ref[1:2, :]
        cdf = 0.5 * (1.0 + lax.erf(gate * (0.5**0.5)))
        density = jnp.exp(-0.5 * gate * gate) * 0.3989422804014327
        gelu = gate * cdf
        act_ref[at, :] = (gelu * up).astype(BF16)
        gelu_ref[at, :] = gelu.astype(BF16)
        slope_ref[at, :] = (up * (cdf + gate * density)).astype(BF16)
        return carry

    lax.fori_loop(0, tokens // FF_TILE, expand, 0)
    for copy in out_copies:
        copy.wait()

    def contract(tile, carry):
        at = pl.ds(pl.multiple_of(tile * FF_TILE, FF_TILE), FF_TILE)
        rows = act_ref[at, :]
        parts_ref[at, :] = jnp.concatenate(
            [nn(rows, w_out_ref[0]), nn(rows, w_out_ref[1])], axis=1
        ).astype(BF16)
        return carry

    lax.fori_loop(0, tokens // FF_TILE, contract, 0)


def ff_forward(core, hidden, bias, own, swap, in_columns, out_columns):
    tokens, width = hidden.shape
    units = bias.shape[1]
    vmem = pl.BlockSpec(memory_space=pltpu.VMEM)
    return pl.pallas_call(
        functools.partial(ff_forward_kernel, in_columns, out_columns),
        out_shape=(
            jax.ShapeDtypeStruct((tokens, units), BF16),
            jax.ShapeDtypeStruct((tokens, units), BF16),
            jax.ShapeDtypeStruct((tokens, units), BF16),
            jax.ShapeDtypeStruct((tokens, width), BF16),
            jax.ShapeDtypeStruct((2, width, units), BF16),
            jax.ShapeDtypeStruct((2, units, width // 2), BF16),
        ),
        in_specs=[pl.BlockSpec(memory_space=pltpu.SMEM)]
        + [vmem] * 2
        + [pl.BlockSpec(memory_space=pl.ANY)] * 2,
        out_specs=(vmem,) * 6,
        scratch_shapes=[pltpu.SemaphoreType.DMA((2, 2))],
        compiler_params=pltpu.CompilerParams(vmem_limit_bytes=VMEM_BYTES),
        cost_estimate=pl.CostEstimate(
            flops=32 * tokens * width * units,
            bytes_accessed=6 * width * units,
            transcendentals=2 * tokens * units,
        ),
        name="ff_forward",
    )(core, hidden, bias, own, swap)


def second_norm_kernel(
    parts_ref, hidden_ref, cotangent_ref, vec_ref, result_ref, grad_ref, low_ref, sums_ref
):
    lin = jnp.sum(parts_ref[...].astype(F32), axis=0) + vec_ref[5:6, :]
    normal, scale = normalised(hidden_ref[...] + lin)
    gain = vec_ref[6:7, :]
    result_ref[...] = (normal * gain + vec_ref[7:8, :]).astype(BF16)
    grads = cotangent_ref[...].astype(F32)
    back = norm_back(grads, normal, scale, gain)
    low = back.astype(BF16)
    grad_ref[...] = back
    low_ref[...] = low
    sums_ref[...] = jnp.concatenate(
        [
            column_sum(low.astype(F32)),
            column_sum(grads * normal),
            column_sum(grads),
            jnp.zeros((5, back.shape[1]), F32),
        ]
    )


def second_norm(parts, hidden, cotangent, vectors):
    tokens, width = hidden.shape
    vmem = pl.BlockSpec(memory_space=pltpu.VMEM)
    return pl.pallas_call(
        second_norm_kernel,
        out_shape=(
            jax.ShapeDtypeStruct((tokens, width), BF16),
            jax.ShapeDtypeStruct((tokens, width), F32),
            jax.ShapeDtypeStruct((tokens, width), BF16),
            jax.ShapeDtypeStruct((8, width), F32),
        ),
        in_specs=[vmem] * 4,
        out_specs=(vmem,) * 4,
        compiler_params=pltpu.CompilerParams(vmem_limit_bytes=VMEM_BYTES),
        cost_estimate=pl.CostEstimate(
            flops=20000 * tokens * width, bytes_accessed=20 * tokens * width, transcendentals=0
        ),
        name="second_norm",
    )(parts, hidden, cotangent, vectors)


def ff_backward_kernel(
    grad_ref, slope_ref, gelu_ref, w_in_ref, w_out_ref, joined_ref, parts_ref, bias_ref, half_ref
):
    tokens, width = grad_ref.shape
    half = width // 2
    bias_ref[...] = jnp.zeros_like(bias_ref)

    def visit(tile, carry):
        at = pl.ds(pl.multiple_of(tile * FF_TILE, FF_TILE), FF_TILE)
        left, right = grad_ref[at, :half], grad_ref[at, half:]
        half_ref[0, at, :] = left
        half_ref[1, at, :] = right
        act_grad = nt(left, w_out_ref[0]) + nt(right, w_out_ref[1])
        for which, factor in ((0, slope_ref), (1, gelu_ref)):
            joined = (act_grad * factor[at, :].astype(F32)).astype(BF16)
            joined_ref[which, at, :] = joined
            bias_ref[which : which + 1, :] += column_sum(joined.astype(F32))
        parts_ref[at, :] = (
            nt(joined_ref[0, at, :], w_in_ref[0]) + nt(joined_ref[1, at, :], w_in_ref[1])
        ).astype(BF16)
        return carry

    lax.fori_loop(0, tokens // FF_TILE, visit, 0)


def ff_backward(grads, slope, gelu, w_in, w_out):
    tokens, width = grads.shape
    units = slope.shape[1]
    vmem = pl.BlockSpec(memory_space=pltpu.VMEM)
    return pl.pallas_call(
        ff_backward_kernel,
        out_shape=(
            jax.ShapeDtypeStruct((2, tokens, units), BF16),
            jax.ShapeDtypeStruct((tokens, width), BF16),
            jax.ShapeDtypeStruct((2, units), F32),
            jax.ShapeDtypeStruct((2, tokens, width // 2), BF16),
        ),
        in_specs=[vmem] * 5,
        out_specs=(vmem,) * 4,
        compiler_params=pltpu.CompilerParams(vmem_limit_bytes=VMEM_BYTES),
        cost_estimate=pl.CostEstimate(
            flops=32 * tokens * width * units,
            bytes_accessed=6 * width * units,
            transcendentals=0,
        ),
        name="ff_backward",
    )(grads, slope, gelu, w_in, w_out)


def ff_grads_kernel(core_ref, act_ref, half_ref, hidden_ref, joined_ref, keep_ref, give_ref):
    core = core_ref[0]
    units = joined_ref.shape[2]

    def visit(tile, carry):
        at = pl.ds(pl.multiple_of(tile * GRAD_TILE, GRAD_TILE), GRAD_TILE)
        hidden = hidden_ref[:, at]
        act = act_ref[:, at]
        give_ref[at, :units] = tn(hidden, joined_ref[1 - core]).astype(BF16)
        give_ref[at, units:] = tn(act, half_ref[1 - core]).astype(BF16)
        keep_ref[at, :units] = tn(hidden, joined_ref[core]).astype(BF16)
        keep_ref[at, units:] = tn(act, half_ref[core]).astype(BF16)
        return carry

    lax.fori_loop(0, hidden_ref.shape[1] // GRAD_TILE, visit, 0)


def ff_grads_of(core, act, halves, hidden, joined):
    width = hidden.shape[1]
    cols = joined.shape[2] + halves.shape[2]
    vmem = pl.BlockSpec(memory_space=pltpu.VMEM)
    return pl.pallas_call(
        ff_grads_kernel,
        out_shape=(jax.ShapeDtypeStruct((width, cols), BF16),) * 2,
        in_specs=[pl.BlockSpec(memory_space=pltpu.SMEM)] + [vmem] * 4,
        out_specs=(vmem,) * 2,
        compiler_params=pltpu.CompilerParams(vmem_limit_bytes=VMEM_BYTES),
        cost_estimate=pl.CostEstimate(flops=6 * 10**9, bytes_accessed=10**4, transcendentals=0),
        name="ff_grads",
    )(core, act, halves, hidden, joined)


def first_back_kernel(
    core_ref,
    parts_ref,
    second_ref,
    normal_ref,
    scale_ref,
    vec_ref,
    weight_ref,
    sums_ref,
    mixed_ref,
    _,
    grad_ref,
    out_ref,
    keep_ref,
    give_ref,
):
    tokens, width = second_ref.shape
    half, count = width // 2, tokens // 2
    normal = normal_ref[...]
    grads = second_ref[...] + jnp.sum(parts_ref[...].astype(F32), axis=0)
    back = norm_back(grads, normal, scale_ref[...], vec_ref[3:4, :])
    low = back.astype(BF16)
    grad_ref[...] = back
    out_grad = nt(low[:, :half], weight_ref[0]) + nt(low[:, half:], weight_ref[1])
    for seq in range(2):
        for group in range(GROUPS):
            out_ref[seq * GROUPS + group] = out_grad[
                seq * count : (seq + 1) * count, group * GROUP_WIDTH : (group + 1) * GROUP_WIDTH
            ].astype(BF16)
    rows = jnp.concatenate(
        [
            column_sum(low.astype(F32)),
            column_sum(grads * normal),
            column_sum(grads),
            sums_ref[0:3, :],
            jnp.zeros((122, width), F32),
        ]
    )
    turned = rows.T.astype(BF16)
    keep_ref[:, half:] = turned
    give_ref[:, half:] = turned
    mixed = merged(mixed_ref)
    left = tn(mixed, low[:, :half]).astype(BF16)
    right = tn(mixed, low[:, half:]).astype(BF16)
    own_left = core_ref[0] == 0
    keep_ref[:, :half] = jnp.where(own_left, left, right)
    give_ref[:, :half] = jnp.where(own_left, right, left)


def first_back(core, parts, second_grad, normal, scale, vectors, weight, sums, mixed, earlier):
    tokens, width = second_grad.shape
    vmem = pl.BlockSpec(memory_space=pltpu.VMEM)
    return pl.pallas_call(
        first_back_kernel,
        out_shape=(
            jax.ShapeDtypeStruct((tokens, width), F32),
            jax.ShapeDtypeStruct((2 * GROUPS, tokens // 2, GROUP_WIDTH), BF16),
            jax.ShapeDtypeStruct((width, width // 2 + 128), BF16),
            jax.ShapeDtypeStruct((width, width // 2 + 128), BF16),
        ),
        in_specs=[pl.BlockSpec(memory_space=pltpu.SMEM)]
        + [vmem] * 8
        + [pl.BlockSpec(memory_space=pl.ANY)],
        out_specs=(vmem,) * 4,
        compiler_params=pltpu.CompilerParams(vmem_limit_bytes=VMEM_BYTES),
        cost_estimate=pl.CostEstimate(
            flops=64 * tokens * width * width, bytes_accessed=4 * width * width, transcendentals=0
        ),
        name="first_back",
    )(core, parts, second_grad, normal, scale, vectors, weight, sums, mixed, earlier)


def input_back_kernel(
    place_ref, dq_ref, own_ref, c_ref, y_ref, weight_ref, keep_ref, give_ref, grad_ref
):
    kv_grad = own_ref[...].astype(F32) + c_ref[...].astype(F32) + y_ref[...].astype(F32)
    grads = jnp.concatenate([dq_ref[...], kv_grad.astype(BF16)], axis=1)
    grad_ref[...] = grads
    inputs = nt(grads, weight_ref[...]).astype(BF16)
    pairs, count = keep_ref.shape[0], keep_ref.shape[1]
    own_first = place_ref[2] == 0
    for pair in range(pairs):
        first = inputs[2 * pair * count : (2 * pair + 1) * count]
        second = inputs[(2 * pair + 1) * count : (2 * pair + 2) * count]
        keep_ref[pair] = jnp.where(own_first, first, second)
        give_ref[pair] = jnp.where(own_first, second, first)


def input_back(place, query_grads, own, from_c, from_y, weight):
    tokens = query_grads.shape[0]
    width, cols = weight.shape
    vmem = pl.BlockSpec(memory_space=pltpu.VMEM)
    return pl.pallas_call(
        input_back_kernel,
        out_shape=(
            jax.ShapeDtypeStruct((4, tokens // 8, width), BF16),
            jax.ShapeDtypeStruct((4, tokens // 8, width), BF16),
            jax.ShapeDtypeStruct((tokens, cols), BF16),
        ),
        in_specs=[pl.BlockSpec(memory_space=pltpu.SMEM)] + [vmem] * 5,
        out_specs=(vmem,) * 3,
        compiler_params=pltpu.CompilerParams(vmem_limit_bytes=VMEM_BYTES),
        cost_estimate=pl.CostEstimate(
            flops=10 * tokens * width * cols, bytes_accessed=4 * tokens * width, transcendentals=0
        ),
        name="input_back",
    )(place, query_grads, own, from_c, from_y, weight)


def qkv_weight_kernel(place_ref, chunk_ref, grad_ref, shift_ref, keep_ref, give_ref):
    grads = grad_ref[...]
    weights = tn(chunk_ref[...], grads)
    cols = weights.shape[1]
    owners, shifts = shift_ref.shape
    shard = weights.shape[0] // (4 * owners)
    sums = column_sum(grads.astype(F32))
    for y_side in range(2):
        blocks = []
        for c_side in range(2):
            first = (y_side * 2 + c_side) * shard
            here = (place_ref[1] == c_side) & (place_ref[2] == y_side)
            shift = jnp.where(here, shift_ref[...], 0.0)
            blocks.append(
                jnp.concatenate(
                    [
                        *(
                            weights[at : at + shard]
                            for at in range(first, weights.shape[0], 4 * shard)
                        ),
                        jnp.concatenate([shift, jnp.zeros((owners, cols - shifts), F32)], axis=1),
                        jnp.broadcast_to(sums, (8, cols)),
                    ]
                ).astype(BF16)
            )
        own_first = place_ref[0] == 0
        keep_ref[y_side] = jnp.where(own_first, blocks[0], blocks[1])
        give_ref[y_side] = jnp.where(own_first, blocks[1], blocks[0])


def qkv_weight(place, chunk, grads, shifts):
    tokens, width = chunk.shape
    cols = grads.shape[1]
    rows = width // 4 + shifts.shape[0] + 8
    vmem = pl.BlockSpec(memory_space=pltpu.VMEM)
    return pl.pallas_call(
        qkv_weight_kernel,
        out_shape=(jax.ShapeDtypeStruct((2, rows, cols), BF16),) * 2,
        in_specs=[pl.BlockSpec(memory_space=pltpu.SMEM)] + [vmem] * 3,
        out_specs=(vmem,) * 2,
        compiler_params=pltpu.CompilerParams(vmem_limit_bytes=VMEM_BYTES),
        cost_estimate=pl.CostEstimate(
            flops=14 * tokens * width * cols, bytes_accessed=4 * tokens * width, transcendentals=0
        ),
        name="qkv_weight",
    )(place, chunk, grads, shifts)


def unpack_kernel(half, ring, parts_ref, in_ref, attn_ref, vec_ref):
    start = half + 128
    units = parts_ref.shape[3] - start
    piece = units // ring
    for side in range(2):
        for place in range(ring):
            at = start + place * piece
            to = (side * ring + place) * 4 * piece
            in_ref[:, to : to + 4 * piece] = jnp.concatenate(
                [parts_ref[plane, side, :, at : at + piece].astype(F32) for plane in range(4)],
                axis=1,
            )
        attn_ref[:, side * half : (side + 1) * half] = sum(
            parts_ref[plane, side, :, :half].astype(F32) for plane in range(4)
        )
    vectors = sum(parts_ref[plane, 0, :, half:start].astype(F32) for plane in range(4))
    vec_ref[...] = vectors.T[:8]


def unpack(parts, half, ring):
    shard, cols = parts.shape[2:]
    units = cols - half - 128
    vmem = pl.BlockSpec(memory_space=pltpu.VMEM)
    return pl.pallas_call(
        functools.partial(unpack_kernel, half, ring),
        out_shape=(
            jax.ShapeDtypeStruct((shard, 8 * units), F32),
            jax.ShapeDtypeStruct((shard, 2 * half), F32),
            jax.ShapeDtypeStruct((8, shard), F32),
        ),
        in_specs=[vmem],
        out_specs=(vmem,) * 3,
        compiler_params=pltpu.CompilerParams(vmem_limit_bytes=VMEM_BYTES),
        name="unpack",
    )(parts)


def swap_sum(keep, give, axis):
    return keep.astype(F32) + lax.ppermute(give.astype(BF16), axis, SWAP).astype(F32)


def gather_plane(block):
    return lax.all_gather(block, PLANE, axis=0, tiled=True)


def spread_plane(parts):
    return lax.all_to_all(parts.reshape(4, -1, parts.shape[1]), PLANE, 0, 0, tiled=True)


def after(array, earlier):
    first = earlier[(slice(0, 1),) * earlier.ndim].reshape((1,) * array.ndim)
    return array + (first.astype(F32) * 0.0).astype(array.dtype)


def hold_kernel(*refs):
    del refs


def hold(array, earlier, cost=1):
    anywhere = pl.BlockSpec(memory_space=pl.ANY)
    return pl.pallas_call(
        hold_kernel,
        out_shape=jax.ShapeDtypeStruct(array.shape, array.dtype),
        in_specs=[anywhere] * 2,
        out_specs=anywhere,
        input_output_aliases={0: 0},
        cost_estimate=pl.CostEstimate(flops=cost, bytes_accessed=1, transcendentals=0),
        name="hold",
    )(array, earlier)


def pick_at(parts, index, axis):
    return lax.dynamic_index_in_dim(parts, index, axis, keepdims=False)


def pick(parts, index):
    return lax.dynamic_index_in_dim(parts, index, 0, keepdims=False)


def two(own, other, index):
    return jnp.where(index == 0, jnp.stack([own, other]), jnp.stack([other, own]))


def body(
    tokens,
    positions,
    w_qkv,
    qv_bias,
    w_attn_out,
    attn_out_bias,
    norm1_gain,
    norm1_bias,
    w_in,
    in_bias,
    w_out,
    out_bias,
    norm2_gain,
    norm2_bias,
    cotangent,
):
    seq_count, row_count, width = tokens.shape
    outer = lax.axis_size("e")
    seq_size = 2 * outer * GROUPS
    devices = seq_size * 4
    shard = w_qkv.shape[0]
    ff_shard = w_out.shape[0]
    ring = 4 * outer
    group = lax.axis_index(("r", "x"))
    place = lax.axis_index(("y", "c"))
    units = 2 * ring * ff_shard
    y_at, c_at = lax.axis_index("y"), lax.axis_index("c")
    qkv_cols = 3 * GROUP_WIDTH

    half = width // 2

    with jax.named_scope("gather_ff_weights"):
        in_cols = (
            w_in.reshape(shard, 2, ring, 4, 2 * ff_shard)
            .transpose(3, 1, 0, 2, 4)
            .reshape(4, 2, shard, units)
        )
        attn_cols = w_attn_out.reshape(shard, 2, half).transpose(1, 0, 2)
        in_parts = jnp.concatenate(
            [in_cols, jnp.broadcast_to(attn_cols, (4, 2, shard, half))], axis=3
        ).reshape(8, shard, units + half)
        in_parts = lax.all_to_all(
            in_parts, ("x", "y", "c"), 0, 0, tiled=True
        ).reshape(8 * shard, units + half)
        out_halves = w_out.reshape(ff_shard, 2, half).transpose(1, 0, 2)
        out_cols = two(
            pick(out_halves, c_at), lax.ppermute(pick(out_halves, 1 - c_at), "c", SWAP), c_at
        ).reshape(2 * ff_shard, half)
        packed = jnp.concatenate([in_parts, out_cols], axis=1)

    with jax.named_scope("gather_qkv_weights"):
        own_pos = lax.dynamic_slice_in_dim(positions, place * row_count, row_count, 1)
        shorts = jnp.stack(
            [
                qv_bias[0],
                qv_bias[1],
                attn_out_bias,
                norm1_gain,
                norm1_bias,
                out_bias,
                norm2_gain,
                norm2_bias,
            ]
        )
        spare = 64
        wide = qkv_cols + spare
        high = max(shard, 16)
        shift_rows = -(-2 * ff_shard // spare)
        smalls = jnp.concatenate(
            [
                jnp.broadcast_to(jnp.pad(shorts, ((0, 0), (0, spare - shard))), (2, 8, spare)),
                (own_pos >> 7).astype(BF16)[:, None],
                (own_pos & 127).astype(BF16)[:, None],
                jnp.broadcast_to(
                    jnp.pad(in_bias, (0, shift_rows * spare - 2 * ff_shard)).reshape(
                        shift_rows, spare
                    ),
                    (2, shift_rows, spare),
                ),
                jnp.zeros((2, high - 10 - shift_rows, spare), BF16),
            ],
            axis=1,
        )
        columns = (
            w_qkv.reshape(shard, 3, GROUPS, GROUP_WIDTH)
            .transpose(2, 0, 1, 3)
            .reshape(1, GROUPS, shard, qkv_cols)
        )
        columns = jnp.pad(columns, ((0, 0), (0, 0), (0, high - shard), (0, 0)))
        parcel = jnp.concatenate(
            [
                jnp.broadcast_to(columns, (2, GROUPS, high, qkv_cols)),
                jnp.broadcast_to(smalls[:, None], (2, GROUPS, high, spare)),
            ],
            axis=3,
        ).reshape(8, high, wide)
        parcel = lax.all_to_all(after(parcel, in_parts), SEQ_GROUP, 0, 0, tiled=True)

    with jax.named_scope("gather_tokens"):
        s_at, r_at, x_at = (lax.axis_index(name) for name in SEQ_GROUP)
        chunk = two(
            pick(tokens, s_at), lax.ppermute(pick(tokens, 1 - s_at), "s", SWAP), s_at
        )
        chunk = two(chunk, lax.ppermute(chunk, "r", SWAP), r_at)
        chunk = hold(chunk, packed)
        chunk = two(chunk, lax.ppermute(chunk, "x", SWAP), x_at)
        chunk = chunk.transpose(2, 1, 0, 3, 4).reshape(8 * row_count, width)

    with jax.named_scope("gather_qkv_weights"):
        parcels = lax.all_gather(hold(parcel, chunk), CHUNKS, axis=0, tiled=False)
        parcels = parcels.reshape(outer, 2, 2, 2, 2, 2, high, wide)
        order = (3, 0, 4, 5, 1, 2)
        qkv_slice = (
            parcels[..., :shard, :qkv_cols].transpose(*order, 6, 7).reshape(width, qkv_cols)
        )
        smalls = parcels[..., qkv_cols:]
        vectors = (
            smalls[..., :8, :shard].transpose(6, *order, 7).reshape(8, width).astype(F32)
        )
        pos_parts = smalls[..., 8:10, :row_count].astype(F32)
        chunk_pos = (pos_parts[..., 0, :] * 128.0 + pos_parts[..., 1, :]).reshape(
            outer, 2, 2, 8 * row_count
        )
        in_shift = pick_at(
            pick_at(smalls[..., 10 : 10 + shift_rows, :], x_at, 1), y_at, 1
        )
        in_shift = (
            in_shift.transpose(1, 0, 2, 3, 4, 5)
            .reshape(seq_size, shift_rows * spare)[:, : 2 * ff_shard]
            .reshape(2, units)
            .astype(F32)
        )

    with jax.named_scope("gather_ff_weights"):
        packed = lax.all_gather(packed, RING, axis=0, tiled=True)
        core = c_at.reshape(1).astype(jnp.int32)

    with jax.named_scope("project"):
        qv_slice = lax.dynamic_slice_in_dim(vectors[:2], group * GROUP_WIDTH, GROUP_WIDTH, 1)
        column_bias = jnp.concatenate(
            [qv_slice[0], jnp.zeros((GROUP_WIDTH,), F32), qv_slice[1]]
        )
        queries = (
            jnp.dot(chunk, qkv_slice[:, :GROUP_WIDTH], preferred_element_type=F32)
            + column_bias[:GROUP_WIDTH]
        ).astype(BF16)
        own_kv = (
            jnp.dot(chunk, qkv_slice[:, GROUP_WIDTH:], preferred_element_type=F32)
            + column_bias[GROUP_WIDTH:]
        ).astype(BF16)
    with jax.named_scope("gather_kv"):
        if outer > 1:
            own_kv = lax.all_gather(own_kv, "e", axis=0, tiled=True)
        y_kv = lax.ppermute(own_kv, "y", SWAP)
        key_values = [own_kv, lax.ppermute(own_kv, "c", SWAP)]
    ordered_pos = jnp.stack(
        [
            lax.dynamic_index_in_dim(
                lax.dynamic_index_in_dim(chunk_pos, y_at ^ ky, 1, keepdims=False),
                c_at ^ kc,
                1,
                keepdims=False,
            )
            for ky in (0, 1)
            for kc in (0, 1)
        ]
    )
    query_pos = lax.dynamic_index_in_dim(ordered_pos[0], lax.axis_index("e"), 0, keepdims=True)
    key_pos = ordered_pos.reshape(4 * outer, 8 * row_count)
    head_ids = group * GROUP_HEADS + jnp.arange(GROUP_HEADS)
    slopes = 2.0 ** (-8.0 * (head_ids + 1).astype(F32) / HEADS) * LOG2E

    with jax.named_scope("attention"):
        span = outer
        parts = ((0, 2), (2, 3), (3, 4))
        state = None
        for number, (first, last) in enumerate(parts):
            state = attend(
                slopes,
                queries,
                query_pos,
                key_pos[first * span : last * span],
                key_values[first:last],
                state,
                last=last == 4,
                earlier=(vectors, in_shift) if number == 1 else (),
            )
            if number == 0:
                y_kv = hold(y_kv, state[0])
                key_values += [y_kv, lax.ppermute(y_kv, "c", SWAP)]
        attended, log_sums, attended_low = state

    with jax.named_scope("return_attended"):
        returned = lax.all_to_all(
            attended_low.reshape(8, row_count, GROUP_WIDTH), SEQ_GROUP, 0, 0, tiled=True
        )
    with jax.named_scope("first_norm"):
        packed = hold(packed, returned)
        attn_own = packed[:, units : units + half]
        attn_swap = lax.ppermute(attn_own, "c", SWAP)
        hidden_low, hidden, normal, scale, attn_full = first_norm(
            core,
            returned,
            tokens.reshape(2 * row_count, width),
            vectors,
            attn_own,
            attn_swap,
            slice(0, half),
        )
        packed = hold(packed, hidden_low)
        swapped = lax.ppermute(packed, "c", SWAP)
    with jax.named_scope("gather_hidden"):
        hidden_group = gather_plane(hidden_low)
    with jax.named_scope("ff_forward"):
        activated_low, slope, gelu, ff_parts, in_slice, out_slice = ff_forward(
            core,
            hidden_group,
            in_shift,
            packed,
            swapped,
            slice(0, units),
            slice(units + half, units + width),
        )
    with jax.named_scope("sum_ff"):
        ff_parts = spread_plane(ff_parts)
    with jax.named_scope("second_norm"):
        result, second_grad, ff_grad, sums = second_norm(
            ff_parts, hidden, cotangent.reshape(2 * row_count, width), vectors
        )
    with jax.named_scope("gather_ff_grad"):
        ff_grads = gather_plane(ff_grad)
    with jax.named_scope("ff_backward"):
        joined_grad, hidden_parts, grad_in_shift, grad_halves = ff_backward(
            ff_grads, slope, gelu, in_slice, out_slice
        )
    with jax.named_scope("sum_hidden_grad"):
        hidden_parts = spread_plane(hidden_parts)
    with jax.named_scope("ff_weight_grads"):
        keep, give = ff_grads_of(core, activated_low, grad_halves, hidden_group, joined_grad)
        ff_keep, ff_give = keep, give
    with jax.named_scope("first_norm_back"):
        first_grad, out_grad, keep, give = first_back(
            core,
            hidden_parts,
            second_grad,
            normal,
            scale,
            vectors,
            attn_full,
            sums,
            returned,
            ff_keep,
        )
    with jax.named_scope("send_out_grad"):
        out_grads = lax.all_to_all(out_grad, SEQ_GROUP, 0, 0, tiled=True).reshape(
            8 * row_count, GROUP_WIDTH
        )
    with jax.named_scope("attn_weight_grad"):
        rows = jnp.concatenate(
            [swap_sum(keep, give, "c"), swap_sum(ff_keep, ff_give, "c")], axis=1
        ).astype(BF16)
        rows = hold(rows, out_grads)
        row_sums = lax.psum_scatter(rows, RING, scatter_dimension=0, tiled=True)

    with jax.named_scope("attention_back"):
        state, c_part, y_part, cy_part = attend_back(
            slopes,
            queries,
            query_pos,
            key_pos[span:],
            out_grads,
            attended,
            log_sums,
            key_values[1:],
            None,
            last=False,
            earlier=(rows,),
        )
        y_sum = swap_sum(y_part, cy_part, "c").astype(BF16)
        query_grads, own_part = attend_back(
            slopes,
            queries,
            query_pos,
            key_pos[:span],
            out_grads,
            attended,
            log_sums,
            key_values[:1],
            state,
            last=True,
            earlier=(y_sum,),
        )
    with jax.named_scope("sum_kv_grads"):
        from_c = lax.ppermute(c_part, "c", SWAP)
        from_y = lax.ppermute(y_sum, "y", SWAP)
        if outer > 1:
            total = own_part.astype(F32) + from_c.astype(F32) + from_y.astype(F32)
            own_part = lax.psum_scatter(
                total, "e", scatter_dimension=0, tiled=True
            ).astype(BF16)
            from_c = from_y = jnp.zeros_like(own_part)

    with jax.named_scope("input_back"):
        spot = jnp.stack([c_at, y_at, x_at]).astype(jnp.int32)
        input_keep, input_give, qkv_grad = input_back(
            spot, query_grads, own_part, from_c, from_y, qkv_slice
        )
    with jax.named_scope("qkv_weight_grad"):
        keep, give = qkv_weight(
            spot,
            chunk,
            qkv_grad,
            grad_in_shift.reshape(seq_size, 2 * ff_shard),
        )
        bundle = swap_sum(keep, give, "c").astype(BF16)
        from_x = lax.ppermute(input_give, "x", SWAP)
        parts = (hold(input_keep, bundle).astype(F32) + from_x.astype(F32)).reshape(
            2, 2, row_count, width
        )
        bundle = swap_sum(pick(bundle, y_at), pick(bundle, 1 - y_at), "y").astype(BF16)
        ends = width // 4 + seq_size
        shares = jnp.concatenate(
            [
                bundle[: width // 4].reshape(seq_size, shard, qkv_cols),
                jnp.broadcast_to(bundle[ends : ends + 1], (seq_size, 1, qkv_cols)),
                bundle[width // 4 : ends][:, None],
                jnp.zeros((seq_size, 6, qkv_cols), BF16),
            ],
            axis=1,
        )
    with jax.named_scope("input_grad"):
        from_r = lax.ppermute(pick_at(parts, 1 - r_at, 1).astype(BF16), "r", SWAP)
        parts = hold(pick_at(parts, r_at, 1), shares) + from_r.astype(F32)
        input_grad = first_grad.reshape(2, row_count, width) + two(
            pick(parts, s_at),
            lax.ppermute(pick(parts, 1 - s_at).astype(BF16), "s", SWAP).astype(F32),
            s_at,
        )
    with jax.named_scope("qkv_weight_grad"):
        shares = lax.all_to_all(shares, SEQ_AXIS, 0, 0, tiled=True)
    with jax.named_scope("ff_weight_grads"):
        own_cols = half + 128 + units
        row_sums = hold(row_sums, shares)
        exchanged = lax.all_to_all(
            row_sums[:, :own_cols].reshape(8, shard, own_cols), ("x", "y", "c"), 0, 0, tiled=True
        ).reshape(4, 2, shard, own_cols)
        out_sums = row_sums[:, own_cols:].reshape(2, ff_shard, half)
        grad_w_out = (
            two(
                pick(out_sums, c_at),
                lax.ppermute(pick(out_sums, 1 - c_at), "c", SWAP),
                c_at,
            )
            .transpose(1, 0, 2)
            .reshape(ff_shard, width)
            .astype(F32)
        )
        if outer == 1:
            grad_w_in, grad_w_attn, vector_grads = unpack(exchanged, half, ring)
        else:
            grad_w_in = (
                exchanged[..., half + 128 :]
                .reshape(4, 2, shard, ring, 2 * ff_shard)
                .transpose(2, 1, 3, 0, 4)
                .reshape(shard, 2 * devices * ff_shard)
                .astype(F32)
            )
            grad_w_attn = (
                jnp.sum(exchanged[..., :half].astype(F32), axis=0)
                .transpose(1, 0, 2)
                .reshape(shard, width)
            )
            vector_grads = jnp.sum(exchanged[:, 0, :, half : half + 8].astype(F32), axis=0).T
    with jax.named_scope("qkv_weight_grad"):
        shares = shares.astype(F32)
        totals = jnp.sum(shares.reshape(2 * outer, GROUPS, shard + 8, qkv_cols), axis=0)
        grad_w_qkv = (
            totals[:, :shard]
            .reshape(GROUPS, shard, 3, GROUP_WIDTH)
            .transpose(1, 2, 0, 3)
            .reshape(shard, 3 * width)
        )
        sums = totals[:, shard].reshape(GROUPS, 3, GROUP_WIDTH).transpose(1, 0, 2).reshape(3, width)
        grad_qv = lax.dynamic_slice_in_dim(sums[0::2], lax.axis_index(EVERY) * shard, shard, 1)
        grad_in_bias = jnp.sum(totals[:, shard + 1, : 2 * ff_shard], axis=0)

    return (
        result.reshape(2, row_count, width).astype(BF16),
        input_grad,
        grad_w_qkv,
        grad_qv,
        grad_w_attn,
        vector_grads[0],
        vector_grads[1],
        vector_grads[2],
        grad_w_in,
        grad_in_bias,
        grad_w_out,
        vector_grads[3],
        vector_grads[4],
        vector_grads[5],
    )


def solution(mesh):
    seq_size = mesh.shape["seq"]
    split = Mesh(mesh.devices.reshape(2, seq_size // 8, 2, 2, 2, 2), EVERY)
    tokens_at = P(None, EVERY, None)
    rows_at = P(EVERY, None)
    vector_at = P(EVERY)
    return jax.shard_map(
        body,
        mesh=split,
        in_specs=(
            tokens_at,
            P(None, SEQ_AXIS),
            rows_at,
            P(None, EVERY),
            rows_at,
            vector_at,
            vector_at,
            vector_at,
            rows_at,
            vector_at,
            rows_at,
            vector_at,
            vector_at,
            vector_at,
            tokens_at,
        ),
        out_specs=(
            tokens_at,
            tokens_at,
            rows_at,
            P(None, EVERY),
            rows_at,
            vector_at,
            vector_at,
            vector_at,
            rows_at,
            vector_at,
            rows_at,
            vector_at,
            vector_at,
            vector_at,
        ),
        check_vma=False,
    )
```

profile of v0, /device:TPU:0, one launch (start us, length us, event | category | flops | bytes accessed | tf_op | source)
XLA Modules:
  0.0 289.7 jit_solution(6964589070830189837)
XLA Ops:
  7.2 1.0 constant_dynamic-slice_fusion.11
  8.2 4.1 %collective-permute-start = (bf16[64,768]{1,0:T(8,128)(2,1)S(1)}, bf16[64,768]{1,0:T(8,128)(2,1)S(1)}, u32[]{:S(2)}, u32[]{:S(2)}) collective-permute-start(bf16[64,768]{1,0:T(8,128)(2,1)S(1)} %get-tuple-element.107), channel_id=1, source_target_pairs={{0,16},{16,0},{1,17},{17,1},{2,18},{18,2},{3,19},{19,3},{4,20},{20... | collective-permute-start | bytes 294920 | tf_op jit(solution)/shard_map/gather_tokens/ppermute | solution.py:911
  12.3 0.9 reshape.262
  13.6 1.4 reshape.259
  16.6 3.8 %all-to-all-start = ((bf16[8,24,1152]{2,1,0:T(8,128)(2,1)}), bf16[8,24,1152]{2,1,0:T(8,128)(2,1)S(1)}, u32[]{:S(2)}, u32[]{:S(2)}) async-start(bf16[8,24,1152]{2,1,0:T(8,128)(2,1)} %pad_maximum_fusion.2), calls=%async_computation | async-start | bytes 884736 | tf_op jit(solution)/shard_map/gather_ff_weights/all_to_all | solution.py:851
  21.4 1.6 collective-permute-start.1
  23.1 5.7 %collective-permute-done.1 = bf16[2,64,768]{2,1,0:T(8,128)(2,1)S(1)} collective-permute-done((bf16[2,64,768]{2,1,0:T(8,128)(2,1)S(1)}, bf16[2,64,768]{2,1,0:T(8,128)(2,1)S(1)}, u32[]{:S(2)}, u32[]{:S(2)}) %collective-permute-start.1) | collective-permute-done | bytes 196640 | tf_op jit(solution)/shard_map/gather_tokens/ppermute | solution.py:913
  30.9 1.7 collective-permute-start.3
  34.1 3.4 %all-to-all-start.1 = ((bf16[8,24,640]{2,1,0:T(8,128)(2,1)}), bf16[8,24,640]{2,1,0:T(8,128)(2,1)S(1)}, u32[]{:S(2)}, u32[]{:S(2)}) async-start(bf16[8,24,640]{2,1,0:T(8,128)(2,1)} %bitcast.26), calls=%async_computation.1 | async-start | bytes 491520 | tf_op jit(solution)/shard_map/gather_qkv_weights/all_to_all | solution.py:906
  38.3 4.7 %collective-permute-done.3 = bf16[2,2,64,768]{3,2,1,0:T(8,128)(2,1)S(1)} collective-permute-done((bf16[2,2,64,768]{3,2,1,0:T(8,128)(2,1)}, bf16[2,2,64,768]{3,2,1,0:T(8,128)(2,1)S(1)}, u32[]{:S(2)}, u32[]{:S(2)}) %collective-permute-start.3) | collective-permute-done | bytes 393248 | tf_op jit(solution)/shard_map/gather_tokens/ppermute | solution.py:915
  43.1 1.0 copy.77
  44.1 1.6 all-to-all-done.1.refs_0_
  46.4 10.0 %all-gather = bf16[32,24,640]{2,1,0:T(8,128)(2,1)S(1)} all-gather(bf16[8,24,640]{2,1,0:T(8,128)(2,1)} %hold.10), channel_id=2, replica_groups=mesh['s'=2,'e'=1,'r'=2,'x'=2,'y'=2,'c'=2] {'e','y','c'}, dimensions={0}, use_global_device_ids=true | all-gather | bytes 1228800 | tf_op jit(solution)/shard_map/gather_qkv_weights/all_gather | solution.py:919
  57.6 1.4 fusion.refs_0_.refs_1_
  62.4 1.1 fusion.1.q_ref
  63.5 5.4 %attend.3 = (f32[192,512]{1,0:T(8,128)}, f32[6,512]{1,0:T(8,128)}) custom-call(f32[3]{0:T(128)} %power_multiply_fusion.slopes_ref, bf16[512,192]{1,0:T(8,128)(2,1)} %fusion.1.q_ref, f32[1,512]{1,0:T(1,128)} %get-tuple-element.118.pq_ref.pk_ref, f32[2,512]{1,0:T(2,128)} %maximum_bitcast_fusion.1.pk_ref, bf16[512,384]{1,0:T(8,128)(2,1)} %fusion.refs_0_.refs_1_, ...), custom_call_target="tpu_custom_call" | custom-call | flops 6442450944 | bytes 524288 | tf_op jit(solution)/shard_map/attention/attend/pallas_call | solution.py:147
  68.9 1.9 collective-permute-done.4.refs_0_
  72.2 3.7 %attend.4 = (f32[192,512]{1,0:T(8,128)}, f32[6,512]{1,0:T(8,128)}) custom-call(f32[3]{0:T(128)} %power_multiply_fusion.slopes_ref, bf16[512,192]{1,0:T(8,128)(2,1)} %fusion.1.q_ref, f32[1,512]{1,0:T(1,128)} %get-tuple-element.118.pq_ref.pk_ref, f32[1,512]{1,0:T(1,128)} %get-tuple-element.115.pk_ref, f32[8,768]{1,0:T(8,128)} %convert_element_type.125.refs_0_.vec_ref, ...), custom_call_target="tpu_custom_call" | custom-call | flops 3221225472 | bytes 262144 | tf_op jit(solution)/shard_map/attention/attend/pallas_call | solution.py:147
  76.7 4.0 %attend.5 = (f32[192,512]{1,0:T(8,128)}, f32[3,512]{1,0:T(4,128)}, bf16[512,192]{1,0:T(8,128)(2,1)}) custom-call(f32[3]{0:T(128)} %power_multiply_fusion.slopes_ref, bf16[512,192]{1,0:T(8,128)(2,1)} %fusion.1.q_ref, f32[1,512]{1,0:T(1,128)} %get-tuple-element.118.pq_ref.pk_ref, f32[1,512]{1,0:T(1,128)} %get-tuple-element.117.pk_ref, ...), custom_call_target="tpu_custom_call" | custom-call | flops 3221225472 | bytes 262144 | tf_op jit(solution)/shard_map/attention/attend/pallas_call | solution.py:147
  80.8 16.9 %all_to_all.40.refs_1_.mixed_ref = bf16[8,64,192]{2,1,0:T(8,128)(2,1)} all-to-all(bf16[8,64,192]{2,1,0:T(8,128)(2,1)} %bitcast.163), channel_id=1, replica_groups=mesh['s'=2,'e'=1,'r'=2,'x'=2,'y'=2,'c'=2] {'s','r','x'}, dimensions={0} | all-to-all | bytes 393216 | tf_op jit(solution)/shard_map/return_attended/all_to_all | solution.py:1003
  97.7 1.1 slice.160.own_ref
  98.9 2.0 collective-permute-done.7.swap_ref
  101.7 4.3 %first_norm.1 = (bf16[128,768]{1,0:T(8,128)(2,1)}, f32[128,768]{1,0:T(8,128)}, f32[128,768]{1,0:T(8,128)}, f32[128,1]{1,0:T(8,128)}, bf16[2,768,384]{2,1,0:T(8,128)(2,1)}) custom-call(s32[1]{0:T(128)} %bitcast.core_ref, bf16[8,64,192]{2,1,0:T(8,128)(2,1)} %all_to_all.40.refs_1_.mixed_ref, bf16[128,768]{1,0:T(8,128)(2,1)} %bitcast.164, ...), custom_call_target="tpu_custom_call" | custom-call | flops 4831838208 | bytes 2359296 | tf_op jit(solution)/shard_map/first_norm/first_norm/pallas_call | solution.py:344
  106.9 13.3 %all_gather.18.hidden_ref = bf16[512,768]{1,0:T(8,128)(2,1)} all-gather(bf16[128,768]{1,0:T(8,128)(2,1)S(1)} %copy-done.9), channel_id=1, replica_groups=mesh['s'=2,'e'=1,'r'=2,'x'=2,'y'=2,'c'=2] {'x','y'}, dimensions={0}, use_global_device_ids=true | all-gather | bytes 983040 | tf_op jit(solution)/shard_map/gather_hidden/all_gather | solution.py:768
  120.3 1.4 copy-done.26
  121.7 7.8 %ff_forward.1 = (bf16[512,768]{1,0:T(8,128)(2,1)}, bf16[512,768]{1,0:T(8,128)(2,1)}, bf16[512,768]{1,0:T(8,128)(2,1)}, bf16[512,768]{1,0:T(8,128)(2,1)}, bf16[2,...) custom-call(s32[1]{0:T(128)} %bitcast.core_ref, bf16[512,768]{1,0:T(8,128)(2,1)} %all_gather.18.hidden_ref, ...), custom_call_target="tpu_custom_call" | custom-call | flops 9663676416 | bytes 3538944 | tf_op jit(solution)/shard_map/ff_forward/ff_forward/pallas_call | solution.py:420
  129.4 15.1 %all_to_all.41.parts_ref = bf16[4,128,768]{2,1,0:T(8,128)(2,1)} all-to-all(bf16[4,128,768]{2,1,0:T(8,128)(2,1)} %bitcast.152), channel_id=1, replica_groups=mesh['s'=2,'e'=1,'r'=2,'x'=2,'y'=2,'c'=2] {'x','y'}, dimensions={0} | all-to-all | bytes 1572864 | tf_op jit(solution)/shard_map/sum_ff/all_to_all | solution.py:772
  144.5 2.5 second_norm.1
  147.1 12.4 %all_gather.19.grad_ref = bf16[512,768]{1,0:T(8,128)(2,1)} all-gather(bf16[128,768]{1,0:T(8,128)(2,1)} %get-tuple-element.69), channel_id=1, replica_groups=mesh['s'=2,'e'=1,'r'=2,'x'=2,'y'=2,'c'=2] {'x','y'}, dimensions={0}, use_global_device_ids=true | all-gather | bytes 983040 | tf_op jit(solution)/shard_map/gather_ff_grad/all_gather | solution.py:768
  159.4 6.8 %ff_backward.1 = (bf16[2,512,768]{2,1,0:T(8,128)(2,1)}, bf16[512,768]{1,0:T(8,128)(2,1)}, f32[2,768]{1,0:T(2,128)}, bf16[2,512,384]{2,1,0:T(8,128)(2,1)}) custom-call(bf16[512,768]{1,0:T(8,128)(2,1)} %all_gather.19.grad_ref, bf16[512,768]{1,0:T(8,128)(2,1)} %get-tuple-element.70.slope_ref, bf16[512,768]{1,0:T(8,128)(2,1)} %get-tuple-element.71.gelu_ref, ...), custom_call_target="tpu_custom_call" | custom-call | flops 9663676416 | bytes 3538944 | tf_op jit(solution)/shard_map/ff_backward/ff_backward/pallas_call | solution.py:517
  166.3 3.5 %all-to-all-start.4 = ((bf16[4,128,768]{2,1,0:T(8,128)(2,1)}), bf16[4,128,768]{2,1,0:T(8,128)(2,1)S(1)}, u32[]{:S(2)}, u32[]{:S(2)}) async-start(bf16[4,128,768]{2,1,0:T(8,128)(2,1)} %bitcast.151), calls=%async_computation.4 | async-start | bytes 1572864 | tf_op jit(solution)/shard_map/sum_hidden_grad/all_to_all | solution.py:772
  169.8 6.3 %ff_grads.1 = (bf16[768,1152]{1,0:T(8,128)(2,1)}, bf16[768,1152]{1,0:T(8,128)(2,1)}) custom-call(s32[1]{0:T(128)} %bitcast.core_ref, bf16[512,768]{1,0:T(8,128)(2,1)} %get-tuple-element.80.act_ref, bf16[2,512,384]{2,1,0:T(8,128)(2,1)} %get-tuple-element.81.half_ref, bf16[512,768]{1,0:T(8,128)(2,1)} %all_gather.18.hidden_ref, ...), custom_call_target="tpu_custom_call" | custom-call | flops 6000000000 | bytes 10000 | tf_op jit(solution)/shard_map/ff_weight_grads/ff_grads/pallas_call | solution.py:558
  176.0 1.7 all-to-all-done.4.parts_ref
  177.8 0.9 copy-done.10
  178.7 4.1 %first_back.1 = (f32[128,768]{1,0:T(8,128)}, bf16[8,64,192]{2,1,0:T(8,128)(2,1)}, bf16[768,512]{1,0:T(8,128)(2,1)}, bf16[768,512]{1,0:T(8,128)(2,1)}) custom-call(s32[1]{0:T(128)} %bitcast.core_ref, bf16[4,128,768]{2,1,0:T(8,128)(2,1)} %copy-done.10, f32[128,768]{1,0:T(8,128)} %get-tuple-element.75.second_ref, f32[128,768]{1,0:T(8,128)} %get-tuple-element.76.normal_ref, ...), custom_call_target="tpu_custom_call" | custom-call | flops 4831838208 | bytes 2359296 | tf_op jit(solution)/shard_map/first_norm_back/first_back/pallas_call | solution.py:621
  183.4 4.0 %all-to-all-start.5 = ((bf16[8,64,192]{2,1,0:T(8,128)(2,1)}), bf16[8,64,192]{2,1,0:T(8,128)(2,1)}, u32[]{:S(2)}, u32[]{:S(2)}) async-start(bf16[8,64,192]{2,1,0:T(8,128)(2,1)} %get-tuple-element.85), calls=%async_computation.5 | async-start | bytes 524288 | tf_op jit(solution)/shard_map/send_out_grad/all_to_all | solution.py:1064
  187.5 1.6 add_convert_fusion.1
  189.5 1.7 pad_maximum_fusion.refs_0_
  191.2 6.1 %all-to-all-done.5 = bf16[8,64,192]{2,1,0:T(8,128)(2,1)} async-done(((bf16[8,64,192]{2,1,0:T(8,128)(2,1)}), bf16[8,64,192]{2,1,0:T(8,128)(2,1)}, u32[]{:S(2)}, u32[]{:S(2)}) %all-to-all-start.5) | async-done | bytes 196640 | tf_op jit(solution)/shard_map/send_out_grad/all_to_all | solution.py:1064
  197.3 9.5 %attend_back.2 = (f32[192,512]{1,0:T(8,128)}, bf16[512,384]{1,0:T(8,128)(2,1)}, bf16[512,384]{1,0:T(8,128)(2,1)}, bf16[512,384]{1,0:T(8,128)(2,1)}) custom-call(f32[3]{0:T(128)} %power_multiply_fusion.slopes_ref, bf16[512,192]{1,0:T(8,128)(2,1)} %fusion.1.q_ref, f32[1,512]{1,0:T(1,128)} %get-tuple-element.118.pq_ref.pk_ref, ...), custom_call_target="tpu_custom_call" | custom-call | flops 12683575296 | bytes 786432 | tf_op jit(solution)/shard_map/attention_back/attend_back/pallas_call | solution.py:240
  208.8 1.1 add_convert_fusion.3.refs_0_
  209.9 1.5 collective-permute-start.13
  211.4 4.9 %attend_back.3 = (bf16[512,192]{1,0:T(8,128)(2,1)}, bf16[512,384]{1,0:T(8,128)(2,1)}) custom-call(f32[3]{0:T(128)} %power_multiply_fusion.slopes_ref, bf16[512,192]{1,0:T(8,128)(2,1)} %fusion.1.q_ref, f32[1,512]{1,0:T(1,128)} %get-tuple-element.118.pq_ref.pk_ref, f32[1,512]{1,0:T(1,128)} %get-tuple-element.118.pq_ref.pk_ref, ...), custom_call_target="tpu_custom_call" | custom-call | flops 4227858432 | bytes 262144 | tf_op jit(solution)/shard_map/attention_back/attend_back/pallas_call | solution.py:240
  216.3 4.8 %collective-permute-done.13.y_ref = bf16[512,384]{1,0:T(8,128)(2,1)S(1)} collective-permute-done((bf16[512,384]{1,0:T(8,128)(2,1)S(1)}, bf16[512,384]{1,0:T(8,128)(2,1)S(1)}, u32[]{:S(2)}, u32[]{:S(2)}) %collective-permute-start.13) | collective-permute-done | bytes 393248 | tf_op jit(solution)/shard_map/sum_kv_grads/ppermute | solution.py:1104
  221.9 3.7 %input_back.1 = (bf16[4,64,768]{2,1,0:T(8,128)(2,1)}, bf16[4,64,768]{2,1,0:T(8,128)(2,1)}, bf16[512,576]{1,0:T(8,128)(2,1)}) custom-call(s32[3]{0:T(128)} %pad_add_fusion.place_ref, bf16[512,192]{1,0:T(8,128)(2,1)} %get-tuple-element.94.dq_ref, bf16[512,384]{1,0:T(8,128)(2,1)} %get-tuple-element.95.own_ref, bf16[512,384]{1,0:T(8,128)(2,1)} %copy-done.30, ...), custom_call_target="tpu_custom_call" | custom-call | flops 2264924160 | bytes 1572864 | tf_op jit(solution)/shard_map/input_back/input_back/pallas_call | solution.py:661
  225.5 3.2 %qkv_weight.1 = (bf16[2,208,576]{2,1,0:T(8,128)(2,1)}, bf16[2,208,576]{2,1,0:T(8,128)(2,1)}) custom-call(s32[3]{0:T(128)} %pad_add_fusion.place_ref, bf16[512,768]{1,0:T(8,128)(2,1)} %bitcast.135, bf16[512,576]{1,0:T(8,128)(2,1)} %get-tuple-element.98.grad_ref, f32[8,192]{1,0:T(8,128)} %reshape.276.shift_ref), custom_call_target="tpu_custom_call" | custom-call | flops 3170893824 | bytes 1572864 | tf_op jit(solution)/shard_map/qkv_weight_grad/qkv_weight/pallas_call | solution.py:713
  228.7 1.5 collective-permute-start.15
  230.8 1.2 add_convert_fusion.2.refs_1_
  232.1 1.5 collective-permute-start.16
  233.6 6.6 %collective-permute-done.15 = bf16[4,64,768]{2,1,0:T(8,128)(2,1)S(1)} collective-permute-done((bf16[4,64,768]{2,1,0:T(8,128)(2,1)S(1)}, bf16[4,64,768]{2,1,0:T(8,128)(2,1)S(1)}, u32[]{:S(2)}, u32[]{:S(2)}) %collective-permute-start.15) | collective-permute-done | bytes 393248 | tf_op jit(solution)/shard_map/qkv_weight_grad/ppermute | solution.py:1125
  240.2 1.1 convert_add_fusion
  241.4 1.1 collective-permute-start.17
  244.3 3.6 %all-to-all-start.6 = ((bf16[8,32,576]{2,1,0:T(8,128)(2,1)}), bf16[8,32,576]{2,1,0:T(8,128)(2,1)S(1)}, u32[]{:S(2)}, u32[]{:S(2)}) async-start(bf16[8,32,576]{2,1,0:T(8,128)(2,1)} %maximum_maximum_fusion.refs_1_), calls=%async_computation.6 | async-start | bytes 655360 | tf_op jit(solution)/shard_map/qkv_weight_grad/all_to_all | solution.py:1149
  247.9 1.8 collective-permute-done.17
  249.7 1.0 convert_add_fusion.2
  250.8 3.1 %collective-permute-start.18 = (bf16[64,768]{1,0:T(8,128)(2,1)S(1)}, bf16[64,768]{1,0:T(8,128)(2,1)S(1)}, u32[]{:S(2)}, u32[]{:S(2)}) collective-permute-start(bf16[64,768]{1,0:T(8,128)(2,1)S(1)} %fusion.8), channel_id=1, source_target_pairs={{0,16},{16,0},{1,17},{17,1},{2,18},{18,2},{3,19},{19,3},{4,20},{20... | collective-permute-start | bytes 294920 | tf_op jit(solution)/shard_map/input_grad/ppermute | solution.py:1145
  253.8 8.4 %collective-permute-done.18 = bf16[64,768]{1,0:T(8,128)(2,1)S(1)} collective-permute-done((bf16[64,768]{1,0:T(8,128)(2,1)S(1)}, bf16[64,768]{1,0:T(8,128)(2,1)S(1)}, u32[]{:S(2)}, u32[]{:S(2)}) %collective-permute-start.18) | collective-permute-done | bytes 98336 | tf_op jit(solution)/shard_map/input_grad/ppermute | solution.py:1145
  263.5 0.9 reshape.282
  264.7 1.8 slice.166
  266.5 3.6 %all-to-all-start.7 = ((bf16[8,24,1280]{2,1,0:T(8,128)(2,1)}), bf16[8,24,1280]{2,1,0:T(8,128)(2,1)S(1)}, u32[]{:S(2)}, u32[]{:S(2)}) async-start(bf16[8,24,1280]{2,1,0:T(8,128)(2,1)} %bitcast.65), calls=%async_computation.8 | async-start | bytes 983040 | tf_op jit(solution)/shard_map/ff_weight_grads/all_to_all | solution.py:1153
  270.7 0.9 slice.168
  274.0 4.7 %all-to-all-done.7 = bf16[8,24,1280]{2,1,0:T(8,128)(2,1)S(1)} async-done(((bf16[8,24,1280]{2,1,0:T(8,128)(2,1)}), bf16[8,24,1280]{2,1,0:T(8,128)(2,1)S(1)}, u32[]{:S(2)}, u32[]{:S(2)}) %all-to-all-start.7) | async-done | bytes 491552 | tf_op jit(solution)/shard_map/ff_weight_grads/all_to_all | solution.py:1153
  279.5 2.0 unpack.1
  281.4 1.4 slice_bitcast_fusion.2
  (190 shorter events, 27.3 us)
Async XLA Ops:
  7.2 8.4 %copy-start.16 = (bf16[24,768]{1,0:T(8,128)(2,1)S(1)}, bf16[24,768]{1,0:T(8,128)(2,1)}, u32[]{:S(2)}) copy-start(bf16[24,768]{1,0:T(8,128)(2,1)} %param.19) | copy-start | bytes 110596
  8.2 13.2 %collective-permute-start = (bf16[64,768]{1,0:T(8,128)(2,1)S(1)}, bf16[64,768]{1,0:T(8,128)(2,1)S(1)}, u32[]{:S(2)}, u32[]{:S(2)}) collective-permute-start(bf16[64,768]{1,0:T(8,128)(2,1)S(1)} %get-tuple-element.107), channel_id=1, source_target_pairs={{0,16},{16,0},{1,17},{17,1},{2,18},{18,2},{3,19},{19,3},{4,20},{20... | collective-permute-start | bytes 294920 | tf_op jit(solution)/shard_map/gather_tokens/ppermute | solution.py:911
  13.6 9.5 %collective-permute-start.2 = (bf16[96,384]{1,0:T(8,128)(2,1)S(1)}, bf16[96,384]{1,0:T(8,128)(2,1)S(1)}, u32[]{:S(2)}, u32[]{:S(2)}) collective-permute-start(bf16[96,384]{1,0:T(8,128)(2,1)S(1)} %bitcast.167), channel_id=1, source_target_pairs={{0,1},{1,0},{2,3},{3,2},{4,5},{5,4},{6,7},{7,6},{8,9},{9,8},{10,11... | collective-permute-start | bytes 221192 | tf_op jit(solution)/shard_map/gather_ff_weights/ppermute | solution.py:856
  15.1 5.3 %copy-start.18 = (s32[2,256]{1,0:T(2,128)S(1)}, s32[2,256]{1,0:T(2,128)}, u32[]{:S(2)}) copy-start(s32[2,256]{1,0:T(2,128)} %param.16) | copy-start | bytes 6148
  15.1 5.4 %copy-start.32 = (bf16[192]{0:T(256)(128)(2,1)S(1)}, bf16[192]{0:T(256)(128)(2,1)}, u32[]{:S(2)}) copy-start(bf16[192]{0:T(256)(128)(2,1)} %param.24) | copy-start | bytes 1156
  15.1 5.5 %copy-start.15 = (bf16[24,2304]{1,0:T(8,128)(2,1)S(1)}, bf16[24,2304]{1,0:T(8,128)(2,1)}, u32[]{:S(2)}) copy-start(bf16[24,2304]{1,0:T(8,128)(2,1)} %param.17) | copy-start | bytes 331780
  15.6 5.4 %copy-start.19 = (bf16[2,24]{1,0:T(2,128)(2,1)S(1)}, bf16[2,24]{1,0:T(2,128)(2,1)}, u32[]{:S(2)}) copy-start(bf16[2,24]{1,0:T(2,128)(2,1)} %param.18) | copy-start | bytes 292
  15.6 5.4 %copy-start.20 = (bf16[24]{0:T(256)(128)(2,1)S(1)}, bf16[24]{0:T(256)(128)(2,1)}, u32[]{:S(2)}) copy-start(bf16[24]{0:T(256)(128)(2,1)} %param.20) | copy-start | bytes 148
  15.7 5.4 %copy-start.21 = (bf16[24]{0:T(256)(128)(2,1)S(1)}, bf16[24]{0:T(256)(128)(2,1)}, u32[]{:S(2)}) copy-start(bf16[24]{0:T(256)(128)(2,1)} %param.21) | copy-start | bytes 148
  15.7 5.4 %copy-start.22 = (bf16[24]{0:T(256)(128)(2,1)S(1)}, bf16[24]{0:T(256)(128)(2,1)}, u32[]{:S(2)}) copy-start(bf16[24]{0:T(256)(128)(2,1)} %param.22) | copy-start | bytes 148
  15.7 5.4 %copy-start.23 = (bf16[24]{0:T(256)(128)(2,1)S(1)}, bf16[24]{0:T(256)(128)(2,1)}, u32[]{:S(2)}) copy-start(bf16[24]{0:T(256)(128)(2,1)} %param.26) | copy-start | bytes 148
  15.7 5.4 %copy-start.24 = (bf16[24]{0:T(256)(128)(2,1)S(1)}, bf16[24]{0:T(256)(128)(2,1)}, u32[]{:S(2)}) copy-start(bf16[24]{0:T(256)(128)(2,1)} %param.27) | copy-start | bytes 148
  15.7 5.4 %copy-start.25 = (bf16[24]{0:T(256)(128)(2,1)S(1)}, bf16[24]{0:T(256)(128)(2,1)}, u32[]{:S(2)}) copy-start(bf16[24]{0:T(256)(128)(2,1)} %param.28) | copy-start | bytes 148
  16.6 13.0 %all-to-all-start = ((bf16[8,24,1152]{2,1,0:T(8,128)(2,1)}), bf16[8,24,1152]{2,1,0:T(8,128)(2,1)S(1)}, u32[]{:S(2)}, u32[]{:S(2)}) async-start(bf16[8,24,1152]{2,1,0:T(8,128)(2,1)} %pad_maximum_fusion.2), calls=%async_computation | async-start | bytes 884736 | tf_op jit(solution)/shard_map/gather_ff_weights/all_to_all | solution.py:851
  21.4 7.4 %collective-permute-start.1 = (bf16[2,64,768]{2,1,0:T(8,128)(2,1)S(1)}, bf16[2,64,768]{2,1,0:T(8,128)(2,1)S(1)}, u32[]{:S(2)}, u32[]{:S(2)}) collective-permute-start(bf16[2,64,768]{2,1,0:T(8,128)(2,1)S(1)} %maximum_select_fusion.4), channel_id=1, source_target_pairs={{0,8},{8,0},{1,9},{9,1},{2,10},{10,2},{3,11},{11,3},{4,12},{12,4},... | collective-permute-start | bytes 589832 | tf_op jit(solution)/shard_map/gather_tokens/ppermute | solution.py:913
  30.9 12.0 %copy-start.2 = (bf16[2,2,64,768]{3,2,1,0:T(8,128)(2,1)S(1)}, bf16[2,2,64,768]{3,2,1,0:T(8,128)(2,1)}, u32[]{:S(2)}) copy-start(bf16[2,2,64,768]{3,2,1,0:T(8,128)(2,1)} %hold.9) | copy-start | bytes 1179652
  30.9 12.0 %collective-permute-start.3 = (bf16[2,2,64,768]{3,2,1,0:T(8,128)(2,1)}, bf16[2,2,64,768]{3,2,1,0:T(8,128)(2,1)S(1)}, u32[]{:S(2)}, u32[]{:S(2)}) collective-permute-start(bf16[2,2,64,768]{3,2,1,0:T(8,128)(2,1)} %hold.9), channel_id=1, source_target_pairs={{0,4},{4,0},{1,5},{5,1},{2,6},{6,2},{3,7},{7,3},{8,12},{12,8},{9,1... | collective-permute-start | bytes 1179656 | tf_op jit(solution)/shard_map/gather_tokens/ppermute | solution.py:915
  34.1 11.6 %all-to-all-start.1 = ((bf16[8,24,640]{2,1,0:T(8,128)(2,1)}), bf16[8,24,640]{2,1,0:T(8,128)(2,1)S(1)}, u32[]{:S(2)}, u32[]{:S(2)}) async-start(bf16[8,24,640]{2,1,0:T(8,128)(2,1)} %bitcast.26), calls=%async_computation.1 | async-start | bytes 491520 | tf_op jit(solution)/shard_map/gather_qkv_weights/all_to_all | solution.py:906
  37.5 60.2 %all-gather.3.cloned.1.call-start = ((), (), s32[]{:S(2)}) async-start(), calls=%async_computation.9 | async-start | bytes 2949120 | tf_op jit(solution)/shard_map/gather_ff_weights/all_gather | solution.py:944
  45.7 0.7 copy-start.5
  56.4 1.2 copy-start.3
  56.6 6.9 %copy-start.8 = (bf16[2,1,2,2,2,2,24,576]{7,6,5,4,3,2,0,1:T(8,128)(2,1)}, bf16[2,1,2,2,2,2,24,576]{7,6,5,4,3,2,0,1:T(8,128)(2,1)S(1)}, u32[]{:S(2)}) copy-start(bf16[2,1,2,2,2,2,24,576]{7,6,5,4,3,2,0,1:T(8,128)(2,1)S(1)} %copy.81) | copy-start | bytes 2654212
  59.0 4.5 %collective-permute-start.5 = (bf16[512,384]{1,0:T(8,128)(2,1)}, bf16[512,384]{1,0:T(8,128)(2,1)}, u32[]{:S(2)}, u32[]{:S(2)}) collective-permute-start(bf16[512,384]{1,0:T(8,128)(2,1)} %fusion.refs_0_.refs_1_), channel_id=1, source_target_pairs={{0,1},{1,0},{2,3},{3,2},{4,5},{5,4},{6,7},{7,6},{8,9},{9,8},{10,11... | collective-permute-start | bytes 1179656 | tf_op jit(solution)/shard_map/gather_kv/ppermute | solution.py:964
  59.4 11.4 %collective-permute-start.4 = (bf16[512,384]{1,0:T(8,128)(2,1)}, bf16[512,384]{1,0:T(8,128)(2,1)S(1)}, u32[]{:S(2)}, u32[]{:S(2)}) collective-permute-start(bf16[512,384]{1,0:T(8,128)(2,1)} %fusion.refs_0_.refs_1_), channel_id=1, source_target_pairs={{0,2},{2,0},{1,3},{3,1},{4,6},{6,4},{5,7},{7,5},{8,10},{10,8},{9,1... | collective-permute-start | bytes 1179656 | tf_op jit(solution)/shard_map/gather_kv/ppermute | solution.py:963
  70.8 0.7 copy-start.13
  71.5 4.4 %collective-permute-start.6 = (bf16[512,384]{1,0:T(8,128)(2,1)}, bf16[512,384]{1,0:T(8,128)(2,1)S(1)}, u32[]{:S(2)}, u32[]{:S(2)}) collective-permute-start(bf16[512,384]{1,0:T(8,128)(2,1)} %hold.11.refs_2_), channel_id=1, source_target_pairs={{0,1},{1,0},{2,3},{3,2},{4,5},{5,4},{6,7},{7,6},{8,9},{9,8},{10,11... | collective-permute-start | bytes 1179656 | tf_op jit(solution)/shard_map/attention/ppermute | solution.py:999
  76.0 0.7 copy-start.28
  98.8 2.1 copy-start.11
  98.8 2.1 collective-permute-start.7
  100.9 0.8 copy-start.27
  106.0 0.9 copy-start.9
  106.0 14.2 %collective-permute-start.8 = (bf16[768,1536]{1,0:T(8,128)(2,1)}, bf16[768,1536]{1,0:T(8,128)(2,1)S(1)}, u32[]{:S(2)}, u32[]{:S(2)}) collective-permute-start(bf16[768,1536]{1,0:T(8,128)(2,1)} %hold.13.own_ref), channel_id=1, source_target_pairs={{0,1},{1,0},{2,3},{3,2},{4,5},{5,4},{6,7},{7,6},{8,9},{9,8},{10,11... | collective-permute-start | bytes 7077896 | tf_op jit(solution)/shard_map/first_norm/ppermute | solution.py:1020
  120.2 1.4 copy-start.26
  166.3 11.5 %all-to-all-start.4 = ((bf16[4,128,768]{2,1,0:T(8,128)(2,1)}), bf16[4,128,768]{2,1,0:T(8,128)(2,1)S(1)}, u32[]{:S(2)}, u32[]{:S(2)}) async-start(bf16[4,128,768]{2,1,0:T(8,128)(2,1)} %bitcast.151), calls=%async_computation.4 | async-start | bytes 1572864 | tf_op jit(solution)/shard_map/sum_hidden_grad/all_to_all | solution.py:772
  176.0 13.0 %collective-permute-start.10 = (bf16[768,1152]{1,0:T(8,128)(2,1)}, bf16[768,1152]{1,0:T(8,128)(2,1)S(1)}, u32[]{:S(2)}, u32[]{:S(2)}) collective-permute-start(bf16[768,1152]{1,0:T(8,128)(2,1)} %get-tuple-element.90), channel_id=1, source_target_pairs={{0,1},{1,0},{2,3},{3,2},{4,5},{5,4},{6,7},{7,6},{8,9},{9,8},{10,11... | collective-permute-start | bytes 5308424 | tf_op jit(solution)/shard_map/attn_weight_grad/ppermute | solution.py:764
  177.8 0.9 copy-start.10
  182.8 6.3 %copy-start.7 = (bf16[768,1152]{1,0:T(8,128)(2,1)S(1)}, bf16[768,1152]{1,0:T(8,128)(2,1)}, u32[]{:S(2)}) copy-start(bf16[768,1152]{1,0:T(8,128)(2,1)} %get-tuple-element.83._) | copy-start | bytes 5308420
  182.8 4.7 %collective-permute-start.9 = (bf16[768,512]{1,0:T(8,128)(2,1)}, bf16[768,512]{1,0:T(8,128)(2,1)}, u32[]{:S(2)}, u32[]{:S(2)}) collective-permute-start(bf16[768,512]{1,0:T(8,128)(2,1)} %get-tuple-element.89), channel_id=1, source_target_pairs={{0,1},{1,0},{2,3},{3,2},{4,5},{5,4},{6,7},{7,6},{8,9},{9,8},{10,11... | collective-permute-start | bytes 2359304 | tf_op jit(solution)/shard_map/attn_weight_grad/ppermute | solution.py:764
  183.4 13.9 %all-to-all-start.5 = ((bf16[8,64,192]{2,1,0:T(8,128)(2,1)}), bf16[8,64,192]{2,1,0:T(8,128)(2,1)}, u32[]{:S(2)}, u32[]{:S(2)}) async-start(bf16[8,64,192]{2,1,0:T(8,128)(2,1)} %get-tuple-element.85), calls=%async_computation.5 | async-start | bytes 524288 | tf_op jit(solution)/shard_map/send_out_grad/all_to_all | solution.py:1064
  187.4 77.2 %reduce-scatter.2.cloned.1.call-start = ((), (), s32[]{:S(2)}) async-start(), calls=%async_computation.10 | async-start | bytes 3194880 | tf_op jit(solution)/shard_map/attn_weight_grad/reduce_scatter | solution.py:1072
  197.3 10.1 %copy-start.17 = (f32[2,768]{1,0:T(2,128)S(1)}, f32[2,768]{1,0:T(2,128)}, u32[]{:S(2)}) copy-start(f32[2,768]{1,0:T(2,128)} %get-tuple-element.99) | copy-start | bytes 18436
  206.8 1.9 collective-permute-start.11
  208.1 8.2 %collective-permute-start.12 = (bf16[512,384]{1,0:T(8,128)(2,1)}, bf16[512,384]{1,0:T(8,128)(2,1)S(1)}, u32[]{:S(2)}, u32[]{:S(2)}) collective-permute-start(bf16[512,384]{1,0:T(8,128)(2,1)} %get-tuple-element.96), channel_id=1, source_target_pairs={{0,1},{1,0},{2,3},{3,2},{4,5},{5,4},{6,7},{7,6},{8,9},{9,8},{10,11... | collective-permute-start | bytes 1179656 | tf_op jit(solution)/shard_map/sum_kv_grads/ppermute | solution.py:1103
  209.9 1.5 copy-start.14
  209.9 11.2 %collective-permute-start.13 = (bf16[512,384]{1,0:T(8,128)(2,1)S(1)}, bf16[512,384]{1,0:T(8,128)(2,1)S(1)}, u32[]{:S(2)}, u32[]{:S(2)}) collective-permute-start(bf16[512,384]{1,0:T(8,128)(2,1)S(1)} %add_convert_fusion.3.refs_0_), channel_id=1, source_target_pairs={{0,2},{2,0},{1,3},{3,1},{4,6},{6,4},{5,7},{7,5},{8,10},{10,8},{9,1... | collective-permute-start | bytes 1179656 | tf_op jit(solution)/shard_map/sum_kv_grads/ppermute | solution.py:1104
  216.3 4.8 %copy-start.30 = (bf16[512,384]{1,0:T(8,128)(2,1)}, bf16[512,384]{1,0:T(8,128)(2,1)S(1)}, u32[]{:S(2)}) copy-start(bf16[512,384]{1,0:T(8,128)(2,1)S(1)} %collective-permute-done.12.c_ref) | copy-start | bytes 1179652
  221.1 0.7 copy-start.31
  225.5 3.2 %copy-start.29 = (bf16[4,64,768]{2,1,0:T(8,128)(2,1)S(1)}, bf16[4,64,768]{2,1,0:T(8,128)(2,1)}, u32[]{:S(2)}) copy-start(bf16[4,64,768]{2,1,0:T(8,128)(2,1)} %get-tuple-element.102) | copy-start | bytes 1179652
  228.7 2.1 collective-permute-start.14
  228.7 11.5 %collective-permute-start.15 = (bf16[4,64,768]{2,1,0:T(8,128)(2,1)S(1)}, bf16[4,64,768]{2,1,0:T(8,128)(2,1)S(1)}, u32[]{:S(2)}, u32[]{:S(2)}) collective-permute-start(bf16[4,64,768]{2,1,0:T(8,128)(2,1)S(1)} %copy-done.29), channel_id=1, source_target_pairs={{0,4},{4,0},{1,5},{5,1},{2,6},{6,2},{3,7},{7,3},{8,12},{12,8},{9,1... | collective-permute-start | bytes 1179656 | tf_op jit(solution)/shard_map/qkv_weight_grad/ppermute | solution.py:1125
  232.0 1.6 copy-start
  232.1 11.2 %collective-permute-start.16 = (bf16[208,576]{1,0:T(8,128)(2,1)S(1)}, bf16[208,576]{1,0:T(8,128)(2,1)S(1)}, u32[]{:S(2)}, u32[]{:S(2)}) collective-permute-start(bf16[208,576]{1,0:T(8,128)(2,1)S(1)} %dynamic-slice_bitcast_fusion.1), channel_id=1, source_target_pairs={{0,2},{2,0},{1,3},{3,1},{4,6},{6,4},{5,7},{7,5},{8,10},{10,8},{9,1... | collective-permute-start | bytes 718856 | tf_op jit(solution)/shard_map/qkv_weight_grad/ppermute | solution.py:764
  233.6 9.7 %copy-start.1 = (bf16[2,208,576]{2,1,0:T(8,128)(2,1)S(1)}, bf16[2,208,576]{2,1,0:T(8,128)(2,1)}, u32[]{:S(2)}) copy-start(bf16[2,208,576]{2,1,0:T(8,128)(2,1)} %copy-done) | copy-start | bytes 1437700
  241.4 8.4 %collective-permute-start.17 = (bf16[2,64,768]{2,1,0:T(8,128)(2,1)S(1)}, bf16[2,64,768]{2,1,0:T(8,128)(2,1)S(1)}, u32[]{:S(2)}, u32[]{:S(2)}) collective-permute-start(bf16[2,64,768]{2,1,0:T(8,128)(2,1)S(1)} %fusion.7), channel_id=1, source_target_pairs={{0,8},{8,0},{1,9},{9,1},{2,10},{10,2},{3,11},{11,3},{4,12},{12,4},... | collective-permute-start | bytes 589832 | tf_op jit(solution)/shard_map/input_grad/ppermute | solution.py:1141
  244.3 17.9 %copy-start.12 = (f32[128,768]{1,0:T(8,128)S(1)}, f32[128,768]{1,0:T(8,128)}, u32[]{:S(2)}) copy-start(f32[128,768]{1,0:T(8,128)} %get-tuple-element.84) | copy-start | bytes 1179652
  244.3 18.7 %all-to-all-start.6 = ((bf16[8,32,576]{2,1,0:T(8,128)(2,1)}), bf16[8,32,576]{2,1,0:T(8,128)(2,1)S(1)}, u32[]{:S(2)}, u32[]{:S(2)}) async-start(bf16[8,32,576]{2,1,0:T(8,128)(2,1)} %maximum_maximum_fusion.refs_1_), calls=%async_computation.6 | async-start | bytes 655360 | tf_op jit(solution)/shard_map/qkv_weight_grad/all_to_all | solution.py:1149
  250.8 11.4 %collective-permute-start.18 = (bf16[64,768]{1,0:T(8,128)(2,1)S(1)}, bf16[64,768]{1,0:T(8,128)(2,1)S(1)}, u32[]{:S(2)}, u32[]{:S(2)}) collective-permute-start(bf16[64,768]{1,0:T(8,128)(2,1)S(1)} %fusion.8), channel_id=1, source_target_pairs={{0,16},{16,0},{1,17},{17,1},{2,18},{18,2},{3,19},{19,3},{4,20},{20... | collective-permute-start | bytes 294920 | tf_op jit(solution)/shard_map/input_grad/ppermute | solution.py:1145
  263.0 1.6 copy-start.4
  266.5 12.1 %all-to-all-start.7 = ((bf16[8,24,1280]{2,1,0:T(8,128)(2,1)}), bf16[8,24,1280]{2,1,0:T(8,128)(2,1)S(1)}, u32[]{:S(2)}, u32[]{:S(2)}) async-start(bf16[8,24,1280]{2,1,0:T(8,128)(2,1)} %bitcast.65), calls=%async_computation.8 | async-start | bytes 983040 | tf_op jit(solution)/shard_map/ff_weight_grads/all_to_all | solution.py:1153
  271.7 1.5 collective-permute-start.19
  278.6 0.8 copy-start.6
Sparse Core Ops, SparseCore 0:
  40.5 54.2 all-gather.2
  197.5 51.8 reduce-scatter.1
where the time goes:
time: 291 us; the launch traced here: 290 us
  Pallas kernels  68.1 us (23%)
  blocking collectives  67.7 us (23%)
  waiting for transfers between devices  51.1 us (18%)
  starting transfers between devices  40.5 us (14%)
  local copies, waits for them, and re-layouts  27.6 us (9%)
  other arithmetic  16.6 us (6%)
  between operations  15.5 us (5%)
    all_gather x2, blocking collectives, gather_plane(): return lax.all_gather(block, PLANE, axis=0, tiled=True)  25.7 us
    all_to_all x1, blocking collectives, body(): lax.all_to_all(attended_low.reshape(8, row_count, GROUP_WIDTH), SEQ_GROUP...  16.9 us
    all_to_all x1, blocking collectives, spread_plane(): lax.all_to_all(parts.reshape(4, -1, parts.shape[1]), PLANE, 0, 0, tiled=T...  15.1 us
    pallas_call x2, Pallas kernels, attend_back(): pl.pallas_call(functools.partial(attend_back_kernel, len(earlier), count,...  14.4 us
    pallas_call x3, Pallas kernels, attend(): pl.pallas_call(functools.partial(attend_kernel, len(earlier), count, firs...  13.2 us
    all_gather x1, blocking collectives, body(): parcels = lax.all_gather(hold(parcel, chunk), CHUNKS, axis=0, tiled=False)  10 us
    ppermute x1, waiting for transfers between devices, body(): lax.ppermute(pick(parts, 1 - s_at).astype(BF16), 's', SWAP).astype(F32)  8.36 us
    unnamed x68, local copies, waits for them, and re-layouts  8.34 us
  transfers between devices with their start and end apart: 28, of which 15 were waited for; matrix products, arithmetic and copies ran while one was open for 11% of the time, Pallas kernels for 15%

commit v1 on v0

--- a/solution.py
+++ b/solution.py
@@ -723,7 +723,66 @@
     )(place, chunk, grads, shifts)
 
 
-def unpack_kernel(half, ring, parts_ref, in_ref, attn_ref, vec_ref):
+def share_kernel(shard, shifts, first_ref, parts_ref, weight_ref, sums_ref, shift_ref):
+    totals = [
+        parts_ref[group].astype(F32) + parts_ref[GROUPS + group].astype(F32)
+        for group in range(GROUPS)
+    ]
+
+    def part(number, rows):
+        cols = slice(number * GROUP_WIDTH, (number + 1) * GROUP_WIDTH)
+        return jnp.concatenate([total[rows, cols] for total in totals], axis=1)
+
+    width = GROUPS * GROUP_WIDTH
+    for number in range(3):
+        weight_ref[:, number * width : (number + 1) * width] = part(number, slice(0, shard))
+    sums = jnp.concatenate(
+        [
+            part(0, slice(shard, shard + 1)),
+            part(2, slice(shard, shard + 1)),
+            jnp.zeros((6, width), F32),
+        ]
+    )
+    sums_ref[...] = pltpu.roll(sums, width - first_ref[0], 1)[:2, :shard]
+    shift_ref[...] = sum(total[shard + 1 : shard + 2, :shifts] for total in totals)
+
+
+def share(first, parts, shard, shifts):
+    width = GROUPS * GROUP_WIDTH
+    vmem = pl.BlockSpec(memory_space=pltpu.VMEM)
+    return pl.pallas_call(
+        functools.partial(share_kernel, shard, shifts),
+        out_shape=(
+            jax.ShapeDtypeStruct((shard, 3 * width), F32),
+            jax.ShapeDtypeStruct((2, shard), F32),
+            jax.ShapeDtypeStruct((1, shifts), F32),
+        ),
+        in_specs=[pl.BlockSpec(memory_space=pltpu.SMEM), vmem],
+        out_specs=(vmem,) * 3,
+        compiler_params=pltpu.CompilerParams(vmem_limit_bytes=VMEM_BYTES),
+        cost_estimate=pl.CostEstimate(flops=10**10, bytes_accessed=10**6, transcendentals=0),
+        name="share",
+    )(first, parts)
+
+
+def unpack_kernel(
+    half,
+    ring,
+    core_ref,
+    parts_ref,
+    keep_ref,
+    come_ref,
+    _,
+    __,
+    in_ref,
+    attn_ref,
+    vec_ref,
+    out_ref,
+):
+    keep, come = keep_ref[...].astype(F32), come_ref[...].astype(F32)
+    own_first = core_ref[0] == 0
+    out_ref[:, :half] = jnp.where(own_first, keep, come)
+    out_ref[:, half:] = jnp.where(own_first, come, keep)
     start = half + 128
     units = parts_ref.shape[3] - start
     piece = units // ring
@@ -742,7 +801,7 @@
     vec_ref[...] = vectors.T[:8]
 
 
-def unpack(parts, half, ring):
+def unpack(core, parts, keep, come, half, ring, *earlier):
     shard, cols = parts.shape[2:]
     units = cols - half - 128
     vmem = pl.BlockSpec(memory_space=pltpu.VMEM)
@@ -752,12 +811,15 @@
             jax.ShapeDtypeStruct((shard, 8 * units), F32),
             jax.ShapeDtypeStruct((shard, 2 * half), F32),
             jax.ShapeDtypeStruct((8, shard), F32),
-        ),
-        in_specs=[vmem],
-        out_specs=(vmem,) * 3,
+            jax.ShapeDtypeStruct((keep.shape[0], 2 * half), F32),
+        ),
+        in_specs=[pl.BlockSpec(memory_space=pltpu.SMEM)]
+        + [vmem] * 3
+        + [pl.BlockSpec(memory_space=pl.ANY)] * 2,
+        out_specs=(vmem,) * 4,
         compiler_params=pltpu.CompilerParams(vmem_limit_bytes=VMEM_BYTES),
         name="unpack",
-    )(parts)
+    )(core, parts, keep, come, *earlier)
 
 
 def swap_sum(keep, give, axis):
@@ -1138,34 +1200,56 @@
             axis=1,
         )
     with jax.named_scope("input_grad"):
-        from_r = lax.ppermute(pick_at(parts, 1 - r_at, 1).astype(BF16), "r", SWAP)
+        from_r = lax.ppermute(
+            hold(pick_at(parts, 1 - r_at, 1).astype(BF16), row_sums), "r", SWAP
+        )
         parts = hold(pick_at(parts, r_at, 1), shares) + from_r.astype(F32)
-        input_grad = first_grad.reshape(2, row_count, width) + two(
-            pick(parts, s_at),
-            lax.ppermute(pick(parts, 1 - s_at).astype(BF16), "s", SWAP).astype(F32),
-            s_at,
-        )
     with jax.named_scope("qkv_weight_grad"):
         shares = lax.all_to_all(shares, SEQ_AXIS, 0, 0, tiled=True)
+        from_s = lax.ppermute(
+            hold(pick(parts, 1 - s_at).astype(BF16), shares), "s", SWAP
+        )
     with jax.named_scope("ff_weight_grads"):
         own_cols = half + 128 + units
         row_sums = hold(row_sums, shares)
+        plane_rows = row_sums[:, :own_cols].reshape(8, shard, own_cols)
+    with jax.named_scope("qkv_weight_grad"):
+        first_col = lax.axis_index(EVERY) * shard
+        if outer == 1:
+            grad_w_qkv, grad_qv, grad_in_bias = share(
+                first_col.reshape(1).astype(jnp.int32), hold(shares, plane_rows), shard, 2 * ff_shard
+            )
+            grad_in_bias = grad_in_bias[0]
+        else:
+            totals = jnp.sum(
+                shares.astype(F32).reshape(2 * outer, GROUPS, shard + 8, qkv_cols), axis=0
+            )
+            grad_w_qkv = (
+                totals[:, :shard]
+                .reshape(GROUPS, shard, 3, GROUP_WIDTH)
+                .transpose(1, 2, 0, 3)
+                .reshape(shard, 3 * width)
+            )
+            sums = (
+                totals[:, shard].reshape(GROUPS, 3, GROUP_WIDTH).transpose(1, 0, 2).reshape(3, width)
+            )
+            grad_qv = lax.dynamic_slice_in_dim(sums[0::2], first_col, shard, 1)
+            grad_in_bias = jnp.sum(totals[:, shard + 1, : 2 * ff_shard], axis=0)
+    with jax.named_scope("input_grad"):
+        input_grad = first_grad.reshape(2, row_count, width) + two(
+            pick(parts, s_at), from_s.astype(F32), s_at
+        )
+    with jax.named_scope("ff_weight_grads"):
         exchanged = lax.all_to_all(
-            row_sums[:, :own_cols].reshape(8, shard, own_cols), ("x", "y", "c"), 0, 0, tiled=True
+            plane_rows, ("x", "y", "c"), 0, 0, tiled=True
         ).reshape(4, 2, shard, own_cols)
         out_sums = row_sums[:, own_cols:].reshape(2, ff_shard, half)
-        grad_w_out = (
-            two(
-                pick(out_sums, c_at),
-                lax.ppermute(pick(out_sums, 1 - c_at), "c", SWAP),
-                c_at,
-            )
-            .transpose(1, 0, 2)
-            .reshape(ff_shard, width)
-            .astype(F32)
-        )
+        out_come = lax.ppermute(pick(out_sums, 1 - c_at), "c", SWAP)
+        out_keep = pick(out_sums, c_at)
         if outer == 1:
-            grad_w_in, grad_w_attn, vector_grads = unpack(exchanged, half, ring)
+            grad_w_in, grad_w_attn, vector_grads, grad_w_out = unpack(
+                core, exchanged, out_keep, out_come, half, ring, grad_w_qkv, input_grad
+            )
         else:
             grad_w_in = (
                 exchanged[..., half + 128 :]
@@ -1180,19 +1264,12 @@
                 .reshape(shard, width)
             )
             vector_grads = jnp.sum(exchanged[:, 0, :, half : half + 8].astype(F32), axis=0).T
-    with jax.named_scope("qkv_weight_grad"):
-        shares = shares.astype(F32)
-        totals = jnp.sum(shares.reshape(2 * outer, GROUPS, shard + 8, qkv_cols), axis=0)
-        grad_w_qkv = (
-            totals[:, :shard]
-            .reshape(GROUPS, shard, 3, GROUP_WIDTH)
-            .transpose(1, 2, 0, 3)
-            .reshape(shard, 3 * width)
-        )
-        sums = totals[:, shard].reshape(GROUPS, 3, GROUP_WIDTH).transpose(1, 0, 2).reshape(3, width)
-        grad_qv = lax.dynamic_slice_in_dim(sums[0::2], lax.axis_index(EVERY) * shard, shard, 1)
-        grad_in_bias = jnp.sum(totals[:, shard + 1, : 2 * ff_shard], axis=0)
-
+            grad_w_out = (
+                two(out_keep, out_come, c_at)
+                .transpose(1, 0, 2)
+                .reshape(ff_shard, width)
+                .astype(F32)
+            )
     return (
         result.reshape(2, row_count, width).astype(BF16),
         input_grad,

time: 291 us -> 287 us (0.986)
    ppermute x5, waiting for transfers between devices: 0.74 us -> 7.76 us  [swap_sum(): lax.ppermute(give.astype(BF16), axis, SWAP).astype(F32)]
    ppermute x1, waiting for transfers between devices: 6.62 us -> 0.01 us  [body(): from_x = lax.ppermute(input_give, 'x', SWAP)]
    all_to_all x1, waiting for transfers between devices: 0.01 us -> 6.31 us  [body(): shares = lax.all_to_all(shares, SEQ_AXIS, 0, 0, tiled=True)]
    all_to_all x1, waiting for transfers between devices: 4.7 us -> 0.01 us  [body(): lax.all_to_all(plane_rows, ('x', 'y', 'c'), 0, 0, tiled=True)]
    ppermute x3, waiting for transfers between devices: 10.5 us -> 6.15 us  [the longest x1 6.15 us: body(): lax.ppermute(hold(pick(parts, 1 - s_at).astype(BF16), shares), 's', SWAP)]
    unnamed x68 -> x70, local copies, waits for them, and re-layouts: 8.34 us -> 9.05 us
  transfers between devices with their start and end apart: 28 -> 28, of which waited for: 15 -> 13; matrix products, arithmetic and copies ran while one was open for 11% -> 11% of each run, Pallas kernels for 15% -> 16%
where the time goes in v1:
time: 287 us; the launch traced here: 285 us
  Pallas kernels  69.9 us (24%)
  blocking collectives  68 us (24%)
  waiting for transfers between devices  48.7 us (17%)
  starting transfers between devices  38.2 us (13%)
  local copies, waits for them, and re-layouts  27.3 us (10%)
  between operations  15.5 us (5%)
  other arithmetic  14.9 us (5%)
    all_gather x2, blocking collectives, gather_plane(): return lax.all_gather(block, PLANE, axis=0, tiled=True)  26 us
    all_to_all x1, blocking collectives, body(): lax.all_to_all(attended_low.reshape(8, row_count, GROUP_WIDTH), SEQ_GROUP...  17 us
    all_to_all x1, blocking collectives, spread_plane(): lax.all_to_all(parts.reshape(4, -1, parts.shape[1]), PLANE, 0, 0, tiled=T...  15.1 us
    pallas_call x2, Pallas kernels, attend_back(): pl.pallas_call(functools.partial(attend_back_kernel, len(earlier), count,...  14.3 us
    pallas_call x3, Pallas kernels, attend(): pl.pallas_call(functools.partial(attend_kernel, len(earlier), count, firs...  13.1 us
    all_gather x1, blocking collectives, body(): parcels = lax.all_gather(hold(parcel, chunk), CHUNKS, axis=0, tiled=False)  10 us
    unnamed x70, local copies, waits for them, and re-layouts  9.05 us
    ppermute x5, waiting for transfers between devices, swap_sum(): lax.ppermute(give.astype(BF16), axis, SWAP).astype(F32)  7.76 us
  transfers between devices with their start and end apart: 28, of which 13 were waited for; matrix products, arithmetic and copies ran while one was open for 11% of the time, Pallas kernels for 16%

profile of v1, /device:TPU:0, one launch (start us, length us, event | category | flops | bytes accessed | tf_op | source)
XLA Modules:
  0.0 285.1 jit_solution(16231530956282725991)
XLA Ops:
  7.2 1.0 constant_dynamic-slice_fusion.9
  8.2 4.1 %collective-permute-start = (bf16[64,768]{1,0:T(8,128)(2,1)S(1)}, bf16[64,768]{1,0:T(8,128)(2,1)S(1)}, u32[]{:S(2)}, u32[]{:S(2)}) collective-permute-start(bf16[64,768]{1,0:T(8,128)(2,1)S(1)} %get-tuple-element.115), channel_id=1, source_target_pairs={{0,16},{16,0},{1,17},{17,1},{2,18},{18,2},{3,19},{19,3},{4,20},{20... | collective-permute-start | bytes 294920 | tf_op jit(solution)/shard_map/gather_tokens/ppermute | solution.py:973
  12.3 0.9 reshape.247
  13.6 1.4 reshape.244
  16.6 3.8 %all-to-all-start = ((bf16[8,24,1152]{2,1,0:T(8,128)(2,1)}), bf16[8,24,1152]{2,1,0:T(8,128)(2,1)S(1)}, u32[]{:S(2)}, u32[]{:S(2)}) async-start(bf16[8,24,1152]{2,1,0:T(8,128)(2,1)} %pad_maximum_fusion.2), calls=%async_computation | async-start | bytes 884736 | tf_op jit(solution)/shard_map/gather_ff_weights/all_to_all | solution.py:913
  21.4 1.6 collective-permute-start.1
  23.1 5.7 %collective-permute-done.1 = bf16[2,64,768]{2,1,0:T(8,128)(2,1)S(1)} collective-permute-done((bf16[2,64,768]{2,1,0:T(8,128)(2,1)S(1)}, bf16[2,64,768]{2,1,0:T(8,128)(2,1)S(1)}, u32[]{:S(2)}, u32[]{:S(2)}) %collective-permute-start.1) | collective-permute-done | bytes 196640 | tf_op jit(solution)/shard_map/gather_tokens/ppermute | solution.py:975
  29.6 0.9 pad_maximum_fusion.1.refs_1_
  30.9 1.7 collective-permute-start.3
  34.1 3.4 %all-to-all-start.1 = ((bf16[8,24,640]{2,1,0:T(8,128)(2,1)}), bf16[8,24,640]{2,1,0:T(8,128)(2,1)S(1)}, u32[]{:S(2)}, u32[]{:S(2)}) async-start(bf16[8,24,640]{2,1,0:T(8,128)(2,1)} %bitcast.26), calls=%async_computation.1 | async-start | bytes 491520 | tf_op jit(solution)/shard_map/gather_qkv_weights/all_to_all | solution.py:968
  38.3 4.7 %collective-permute-done.3 = bf16[2,2,64,768]{3,2,1,0:T(8,128)(2,1)S(1)} collective-permute-done((bf16[2,2,64,768]{3,2,1,0:T(8,128)(2,1)}, bf16[2,2,64,768]{3,2,1,0:T(8,128)(2,1)S(1)}, u32[]{:S(2)}, u32[]{:S(2)}) %collective-permute-start.3) | collective-permute-done | bytes 393248 | tf_op jit(solution)/shard_map/gather_tokens/ppermute | solution.py:977
  43.1 1.0 copy.74
  44.1 1.6 all-to-all-done.1.refs_0_
  46.4 10.0 %all-gather = bf16[32,24,640]{2,1,0:T(8,128)(2,1)S(1)} all-gather(bf16[8,24,640]{2,1,0:T(8,128)(2,1)} %hold.13), channel_id=2, replica_groups=mesh['s'=2,'e'=1,'r'=2,'x'=2,'y'=2,'c'=2] {'e','y','c'}, dimensions={0}, use_global_device_ids=true | all-gather | bytes 1228800 | tf_op jit(solution)/shard_map/gather_qkv_weights/all_gather | solution.py:981
  57.6 1.4 fusion.refs_0_.refs_1_
  62.4 1.1 fusion.1.q_ref
  63.5 5.4 %attend.3 = (f32[192,512]{1,0:T(8,128)}, f32[6,512]{1,0:T(8,128)}) custom-call(f32[3]{0:T(128)} %power_multiply_fusion.slopes_ref, bf16[512,192]{1,0:T(8,128)(2,1)} %fusion.1.q_ref, f32[1,512]{1,0:T(1,128)} %get-tuple-element.126.pq_ref.pk_ref, f32[2,512]{1,0:T(2,128)} %maximum_bitcast_fusion.1.pk_ref, bf16[512,384]{1,0:T(8,128)(2,1)} %fusion.refs_0_.refs_1_, ...), custom_call_target="tpu_custom_call" | custom-call | flops 6442450944 | bytes 524288 | tf_op jit(solution)/shard_map/attention/attend/pallas_call | solution.py:147
  68.9 1.9 collective-permute-done.4.refs_0_
  72.2 3.7 %attend.4 = (f32[192,512]{1,0:T(8,128)}, f32[6,512]{1,0:T(8,128)}) custom-call(f32[3]{0:T(128)} %power_multiply_fusion.slopes_ref, bf16[512,192]{1,0:T(8,128)(2,1)} %fusion.1.q_ref, f32[1,512]{1,0:T(1,128)} %get-tuple-element.126.pq_ref.pk_ref, f32[1,512]{1,0:T(1,128)} %get-tuple-element.123.pk_ref, f32[8,768]{1,0:T(8,128)} %convert_element_type.113.refs_0_.vec_ref, ...), custom_call_target="tpu_custom_call" | custom-call | flops 3221225472 | bytes 262144 | tf_op jit(solution)/shard_map/attention/attend/pallas_call | solution.py:147
  76.7 4.0 %attend.5 = (f32[192,512]{1,0:T(8,128)}, f32[3,512]{1,0:T(4,128)}, bf16[512,192]{1,0:T(8,128)(2,1)}) custom-call(f32[3]{0:T(128)} %power_multiply_fusion.slopes_ref, bf16[512,192]{1,0:T(8,128)(2,1)} %fusion.1.q_ref, f32[1,512]{1,0:T(1,128)} %get-tuple-element.126.pq_ref.pk_ref, f32[1,512]{1,0:T(1,128)} %get-tuple-element.125.pk_ref, ...), custom_call_target="tpu_custom_call" | custom-call | flops 3221225472 | bytes 262144 | tf_op jit(solution)/shard_map/attention/attend/pallas_call | solution.py:147
  80.7 17.0 %all_to_all.40.refs_1_.mixed_ref = bf16[8,64,192]{2,1,0:T(8,128)(2,1)} all-to-all(bf16[8,64,192]{2,1,0:T(8,128)(2,1)} %bitcast.155), channel_id=1, replica_groups=mesh['s'=2,'e'=1,'r'=2,'x'=2,'y'=2,'c'=2] {'s','r','x'}, dimensions={0} | all-to-all | bytes 393216 | tf_op jit(solution)/shard_map/return_attended/all_to_all | solution.py:1065
  97.7 1.1 slice.144.own_ref
  98.9 2.0 collective-permute-done.7.swap_ref
  101.7 4.3 %first_norm.1 = (bf16[128,768]{1,0:T(8,128)(2,1)}, f32[128,768]{1,0:T(8,128)}, f32[128,768]{1,0:T(8,128)}, f32[128,1]{1,0:T(8,128)}, bf16[2,768,384]{2,1,0:T(8,128)(2,1)}) custom-call(s32[1]{0:T(128)} %bitcast.core_ref, bf16[8,64,192]{2,1,0:T(8,128)(2,1)} %all_to_all.40.refs_1_.mixed_ref, bf16[128,768]{1,0:T(8,128)(2,1)} %bitcast.156, ...), custom_call_target="tpu_custom_call" | custom-call | flops 4831838208 | bytes 2359296 | tf_op jit(solution)/shard_map/first_norm/first_norm/pallas_call | solution.py:344
  106.9 13.3 %all_gather.18.hidden_ref = bf16[512,768]{1,0:T(8,128)(2,1)} all-gather(bf16[128,768]{1,0:T(8,128)(2,1)S(1)} %copy-done.9), channel_id=1, replica_groups=mesh['s'=2,'e'=1,'r'=2,'x'=2,'y'=2,'c'=2] {'x','y'}, dimensions={0}, use_global_device_ids=true | all-gather | bytes 983040 | tf_op jit(solution)/shard_map/gather_hidden/all_gather | solution.py:830
  120.2 1.4 copy-done.27
  121.6 7.7 %ff_forward.1 = (bf16[512,768]{1,0:T(8,128)(2,1)}, bf16[512,768]{1,0:T(8,128)(2,1)}, bf16[512,768]{1,0:T(8,128)(2,1)}, bf16[512,768]{1,0:T(8,128)(2,1)}, bf16[2,...) custom-call(s32[1]{0:T(128)} %bitcast.core_ref, bf16[512,768]{1,0:T(8,128)(2,1)} %all_gather.18.hidden_ref, ...), custom_call_target="tpu_custom_call" | custom-call | flops 9663676416 | bytes 3538944 | tf_op jit(solution)/shard_map/ff_forward/ff_forward/pallas_call | solution.py:420
  129.4 15.1 %all_to_all.41.parts_ref = bf16[4,128,768]{2,1,0:T(8,128)(2,1)} all-to-all(bf16[4,128,768]{2,1,0:T(8,128)(2,1)} %bitcast.145), channel_id=1, replica_groups=mesh['s'=2,'e'=1,'r'=2,'x'=2,'y'=2,'c'=2] {'x','y'}, dimensions={0} | all-to-all | bytes 1572864 | tf_op jit(solution)/shard_map/sum_ff/all_to_all | solution.py:834
  144.5 2.5 second_norm.1
  147.0 12.6 %all_gather.19.grad_ref = bf16[512,768]{1,0:T(8,128)(2,1)} all-gather(bf16[128,768]{1,0:T(8,128)(2,1)} %get-tuple-element.73), channel_id=1, replica_groups=mesh['s'=2,'e'=1,'r'=2,'x'=2,'y'=2,'c'=2] {'x','y'}, dimensions={0}, use_global_device_ids=true | all-gather | bytes 983040 | tf_op jit(solution)/shard_map/gather_ff_grad/all_gather | solution.py:830
  159.6 6.8 %ff_backward.1 = (bf16[2,512,768]{2,1,0:T(8,128)(2,1)}, bf16[512,768]{1,0:T(8,128)(2,1)}, f32[2,768]{1,0:T(2,128)}, bf16[2,512,384]{2,1,0:T(8,128)(2,1)}) custom-call(bf16[512,768]{1,0:T(8,128)(2,1)} %all_gather.19.grad_ref, bf16[512,768]{1,0:T(8,128)(2,1)} %get-tuple-element.74.slope_ref, bf16[512,768]{1,0:T(8,128)(2,1)} %get-tuple-element.75.gelu_ref, ...), custom_call_target="tpu_custom_call" | custom-call | flops 9663676416 | bytes 3538944 | tf_op jit(solution)/shard_map/ff_backward/ff_backward/pallas_call | solution.py:517
  166.4 3.5 %all-to-all-start.4 = ((bf16[4,128,768]{2,1,0:T(8,128)(2,1)}), bf16[4,128,768]{2,1,0:T(8,128)(2,1)S(1)}, u32[]{:S(2)}, u32[]{:S(2)}) async-start(bf16[4,128,768]{2,1,0:T(8,128)(2,1)} %bitcast.144), calls=%async_computation.4 | async-start | bytes 1572864 | tf_op jit(solution)/shard_map/sum_hidden_grad/all_to_all | solution.py:834
  169.9 6.3 %ff_grads.1 = (bf16[768,1152]{1,0:T(8,128)(2,1)}, bf16[768,1152]{1,0:T(8,128)(2,1)}) custom-call(s32[1]{0:T(128)} %bitcast.core_ref, bf16[512,768]{1,0:T(8,128)(2,1)} %get-tuple-element.84.act_ref, bf16[2,512,384]{2,1,0:T(8,128)(2,1)} %get-tuple-element.85.half_ref, bf16[512,768]{1,0:T(8,128)(2,1)} %all_gather.18.hidden_ref, ...), custom_call_target="tpu_custom_call" | custom-call | flops 6000000000 | bytes 10000 | tf_op jit(solution)/shard_map/ff_weight_grads/ff_grads/pallas_call | solution.py:558
  176.2 1.7 all-to-all-done.4.parts_ref
  177.9 0.9 copy-done.10
  178.8 4.1 %first_back.1 = (f32[128,768]{1,0:T(8,128)}, bf16[8,64,192]{2,1,0:T(8,128)(2,1)}, bf16[768,512]{1,0:T(8,128)(2,1)}, bf16[768,512]{1,0:T(8,128)(2,1)}) custom-call(s32[1]{0:T(128)} %bitcast.core_ref, bf16[4,128,768]{2,1,0:T(8,128)(2,1)} %copy-done.10, f32[128,768]{1,0:T(8,128)} %get-tuple-element.79.second_ref, f32[128,768]{1,0:T(8,128)} %get-tuple-element.80.normal_ref, ...), custom_call_target="tpu_custom_call" | custom-call | flops 4831838208 | bytes 2359296 | tf_op jit(solution)/shard_map/first_norm_back/first_back/pallas_call | solution.py:621
  182.9 4.2 %all-to-all-start.5 = ((bf16[8,64,192]{2,1,0:T(8,128)(2,1)}), bf16[8,64,192]{2,1,0:T(8,128)(2,1)}, u32[]{:S(2)}, u32[]{:S(2)}) async-start(bf16[8,64,192]{2,1,0:T(8,128)(2,1)} %get-tuple-element.89), calls=%async_computation.5 | async-start | bytes 524288 | tf_op jit(solution)/shard_map/send_out_grad/all_to_all | solution.py:1126
  187.2 1.6 add_convert_fusion.1
  189.2 1.7 pad_maximum_fusion.refs_0_
  190.9 6.0 %all-to-all-done.5 = bf16[8,64,192]{2,1,0:T(8,128)(2,1)} async-done(((bf16[8,64,192]{2,1,0:T(8,128)(2,1)}), bf16[8,64,192]{2,1,0:T(8,128)(2,1)}, u32[]{:S(2)}, u32[]{:S(2)}) %all-to-all-start.5) | async-done | bytes 196640 | tf_op jit(solution)/shard_map/send_out_grad/all_to_all | solution.py:1126
  197.5 9.4 %attend_back.2 = (f32[192,512]{1,0:T(8,128)}, bf16[512,384]{1,0:T(8,128)(2,1)}, bf16[512,384]{1,0:T(8,128)(2,1)}, bf16[512,384]{1,0:T(8,128)(2,1)}) custom-call(f32[3]{0:T(128)} %power_multiply_fusion.slopes_ref, bf16[512,192]{1,0:T(8,128)(2,1)} %fusion.1.q_ref, f32[1,512]{1,0:T(1,128)} %get-tuple-element.126.pq_ref.pk_ref, ...), custom_call_target="tpu_custom_call" | custom-call | flops 12683575296 | bytes 786432 | tf_op jit(solution)/shard_map/attention_back/attend_back/pallas_call | solution.py:240
  208.9 1.1 add_convert_fusion.3.refs_0_
  210.0 1.5 collective-permute-start.13
  211.6 4.9 %attend_back.3 = (bf16[512,192]{1,0:T(8,128)(2,1)}, bf16[512,384]{1,0:T(8,128)(2,1)}) custom-call(f32[3]{0:T(128)} %power_multiply_fusion.slopes_ref, bf16[512,192]{1,0:T(8,128)(2,1)} %fusion.1.q_ref, f32[1,512]{1,0:T(1,128)} %get-tuple-element.126.pq_ref.pk_ref, f32[1,512]{1,0:T(1,128)} %get-tuple-element.126.pq_ref.pk_ref, ...), custom_call_target="tpu_custom_call" | custom-call | flops 4227858432 | bytes 262144 | tf_op jit(solution)/shard_map/attention_back/attend_back/pallas_call | solution.py:240
  216.5 4.8 %collective-permute-done.13.y_ref = bf16[512,384]{1,0:T(8,128)(2,1)S(1)} collective-permute-done((bf16[512,384]{1,0:T(8,128)(2,1)S(1)}, bf16[512,384]{1,0:T(8,128)(2,1)S(1)}, u32[]{:S(2)}, u32[]{:S(2)}) %collective-permute-start.13) | collective-permute-done | bytes 393248 | tf_op jit(solution)/shard_map/sum_kv_grads/ppermute | solution.py:1166
  222.0 3.7 %input_back.1 = (bf16[4,64,768]{2,1,0:T(8,128)(2,1)}, bf16[4,64,768]{2,1,0:T(8,128)(2,1)}, bf16[512,576]{1,0:T(8,128)(2,1)}) custom-call(s32[3]{0:T(128)} %pad_add_fusion.place_ref, bf16[512,192]{1,0:T(8,128)(2,1)} %get-tuple-element.98.dq_ref, bf16[512,384]{1,0:T(8,128)(2,1)} %get-tuple-element.99.own_ref, bf16[512,384]{1,0:T(8,128)(2,1)} %copy-done.31, ...), custom_call_target="tpu_custom_call" | custom-call | flops 2264924160 | bytes 1572864 | tf_op jit(solution)/shard_map/input_back/input_back/pallas_call | solution.py:661
  225.6 3.1 %qkv_weight.1 = (bf16[2,208,576]{2,1,0:T(8,128)(2,1)}, bf16[2,208,576]{2,1,0:T(8,128)(2,1)}) custom-call(s32[3]{0:T(128)} %pad_add_fusion.place_ref, bf16[512,768]{1,0:T(8,128)(2,1)} %bitcast.130, bf16[512,576]{1,0:T(8,128)(2,1)} %get-tuple-element.102.grad_ref, f32[8,192]{1,0:T(8,128)} %reshape.261.shift_ref), custom_call_target="tpu_custom_call" | custom-call | flops 3170893824 | bytes 1572864 | tf_op jit(solution)/shard_map/qkv_weight_grad/qkv_weight/pallas_call | solution.py:713
  228.8 2.1 collective-permute-done.14
  230.9 1.2 add_convert_fusion.2.refs_1_
  232.1 1.5 collective-permute-start.16
  233.7 1.4 collective-permute-start.15
  235.2 5.5 %collective-permute-done.16 = bf16[208,576]{1,0:T(8,128)(2,1)S(1)} collective-permute-done((bf16[208,576]{1,0:T(8,128)(2,1)S(1)}, bf16[208,576]{1,0:T(8,128)(2,1)S(1)}, u32[]{:S(2)}, u32[]{:S(2)}) %collective-permute-start.16) | collective-permute-done | bytes 239648 | tf_op jit(solution)/shard_map/qkv_weight_grad/ppermute | solution.py:826
  240.8 0.8 maximum_maximum_fusion.refs_1_
  241.7 3.6 %all-to-all-start.6 = ((bf16[8,32,576]{2,1,0:T(8,128)(2,1)}), bf16[8,32,576]{2,1,0:T(8,128)(2,1)S(1)}, u32[]{:S(2)}, u32[]{:S(2)}) async-start(bf16[8,32,576]{2,1,0:T(8,128)(2,1)} %maximum_maximum_fusion.refs_1_), calls=%async_computation.7 | async-start | bytes 655360 | tf_op jit(solution)/shard_map/qkv_weight_grad/all_to_all | solution.py:1208
  245.3 1.1 convert_add_fusion
  247.1 2.0 collective-permute-start.17
  249.9 6.3 %all-to-all-done.6.refs_1_.refs_0_ = bf16[8,32,576]{2,1,0:T(8,128)(2,1)S(1)} async-done(((bf16[8,32,576]{2,1,0:T(8,128)(2,1)}), bf16[8,32,576]{2,1,0:T(8,128)(2,1)S(1)}, u32[]{:S(2)}, u32[]{:S(2)}) %all-to-all-start.6) | async-done | bytes 294944 | tf_op jit(solution)/shard_map/qkv_weight_grad/all_to_all | solution.py:1208
  256.9 1.8 slice.148
  258.8 0.9 slice.149
  259.7 3.5 %all-to-all-start.7 = ((bf16[8,24,1280]{2,1,0:T(8,128)(2,1)}), bf16[8,24,1280]{2,1,0:T(8,128)(2,1)S(1)}, u32[]{:S(2)}, u32[]{:S(2)}) async-start(bf16[8,24,1280]{2,1,0:T(8,128)(2,1)} %bitcast.63.refs_1_), calls=%async_computation.8 | async-start | bytes 983040 | tf_op jit(solution)/shard_map/ff_weight_grads/all_to_all | solution.py:1243
  265.0 1.9 share.1
  266.9 6.1 %collective-permute-done.18 = bf16[64,768]{1,0:T(8,128)(2,1)S(1)} collective-permute-done((bf16[64,768]{1,0:T(8,128)(2,1)}, bf16[64,768]{1,0:T(8,128)(2,1)S(1)}, u32[]{:S(2)}, u32[]{:S(2)}) %collective-permute-start.18) | collective-permute-done | bytes 98336 | tf_op jit(solution)/shard_map/qkv_weight_grad/ppermute | solution.py:1209
  274.7 2.1 unpack.1
  276.8 1.4 slice_bitcast_fusion.2
  (182 shorter events, 24.6 us)
Async XLA Ops:
  7.2 8.4 %copy-start.17 = (bf16[24,768]{1,0:T(8,128)(2,1)S(1)}, bf16[24,768]{1,0:T(8,128)(2,1)}, u32[]{:S(2)}) copy-start(bf16[24,768]{1,0:T(8,128)(2,1)} %param.19) | copy-start | bytes 110596
  8.2 13.2 %collective-permute-start = (bf16[64,768]{1,0:T(8,128)(2,1)S(1)}, bf16[64,768]{1,0:T(8,128)(2,1)S(1)}, u32[]{:S(2)}, u32[]{:S(2)}) collective-permute-start(bf16[64,768]{1,0:T(8,128)(2,1)S(1)} %get-tuple-element.115), channel_id=1, source_target_pairs={{0,16},{16,0},{1,17},{17,1},{2,18},{18,2},{3,19},{19,3},{4,20},{20... | collective-permute-start | bytes 294920 | tf_op jit(solution)/shard_map/gather_tokens/ppermute | solution.py:973
  13.6 9.5 %collective-permute-start.2 = (bf16[96,384]{1,0:T(8,128)(2,1)S(1)}, bf16[96,384]{1,0:T(8,128)(2,1)S(1)}, u32[]{:S(2)}, u32[]{:S(2)}) collective-permute-start(bf16[96,384]{1,0:T(8,128)(2,1)S(1)} %bitcast.159), channel_id=1, source_target_pairs={{0,1},{1,0},{2,3},{3,2},{4,5},{5,4},{6,7},{7,6},{8,9},{9,8},{10,11... | collective-permute-start | bytes 221192 | tf_op jit(solution)/shard_map/gather_ff_weights/ppermute | solution.py:918
  15.1 5.3 %copy-start.19 = (s32[2,256]{1,0:T(2,128)S(1)}, s32[2,256]{1,0:T(2,128)}, u32[]{:S(2)}) copy-start(s32[2,256]{1,0:T(2,128)} %param.16) | copy-start | bytes 6148
  15.1 5.4 %copy-start.33 = (bf16[192]{0:T(256)(128)(2,1)S(1)}, bf16[192]{0:T(256)(128)(2,1)}, u32[]{:S(2)}) copy-start(bf16[192]{0:T(256)(128)(2,1)} %param.24) | copy-start | bytes 1156
  15.1 5.5 %copy-start.15 = (bf16[24,2304]{1,0:T(8,128)(2,1)S(1)}, bf16[24,2304]{1,0:T(8,128)(2,1)}, u32[]{:S(2)}) copy-start(bf16[24,2304]{1,0:T(8,128)(2,1)} %param.17) | copy-start | bytes 331780
  15.6 5.4 %copy-start.20 = (bf16[2,24]{1,0:T(2,128)(2,1)S(1)}, bf16[2,24]{1,0:T(2,128)(2,1)}, u32[]{:S(2)}) copy-start(bf16[2,24]{1,0:T(2,128)(2,1)} %param.18) | copy-start | bytes 292
  15.6 5.4 %copy-start.21 = (bf16[24]{0:T(256)(128)(2,1)S(1)}, bf16[24]{0:T(256)(128)(2,1)}, u32[]{:S(2)}) copy-start(bf16[24]{0:T(256)(128)(2,1)} %param.20) | copy-start | bytes 148
  15.7 5.4 %copy-start.22 = (bf16[24]{0:T(256)(128)(2,1)S(1)}, bf16[24]{0:T(256)(128)(2,1)}, u32[]{:S(2)}) copy-start(bf16[24]{0:T(256)(128)(2,1)} %param.21) | copy-start | bytes 148
  15.7 5.4 %copy-start.23 = (bf16[24]{0:T(256)(128)(2,1)S(1)}, bf16[24]{0:T(256)(128)(2,1)}, u32[]{:S(2)}) copy-start(bf16[24]{0:T(256)(128)(2,1)} %param.22) | copy-start | bytes 148
  15.7 5.4 %copy-start.24 = (bf16[24]{0:T(256)(128)(2,1)S(1)}, bf16[24]{0:T(256)(128)(2,1)}, u32[]{:S(2)}) copy-start(bf16[24]{0:T(256)(128)(2,1)} %param.26) | copy-start | bytes 148
  15.7 5.4 %copy-start.25 = (bf16[24]{0:T(256)(128)(2,1)S(1)}, bf16[24]{0:T(256)(128)(2,1)}, u32[]{:S(2)}) copy-start(bf16[24]{0:T(256)(128)(2,1)} %param.27) | copy-start | bytes 148
  15.7 5.4 %copy-start.26 = (bf16[24]{0:T(256)(128)(2,1)S(1)}, bf16[24]{0:T(256)(128)(2,1)}, u32[]{:S(2)}) copy-start(bf16[24]{0:T(256)(128)(2,1)} %param.28) | copy-start | bytes 148
  16.6 13.0 %all-to-all-start = ((bf16[8,24,1152]{2,1,0:T(8,128)(2,1)}), bf16[8,24,1152]{2,1,0:T(8,128)(2,1)S(1)}, u32[]{:S(2)}, u32[]{:S(2)}) async-start(bf16[8,24,1152]{2,1,0:T(8,128)(2,1)} %pad_maximum_fusion.2), calls=%async_computation | async-start | bytes 884736 | tf_op jit(solution)/shard_map/gather_ff_weights/all_to_all | solution.py:913
  21.4 7.4 %collective-permute-start.1 = (bf16[2,64,768]{2,1,0:T(8,128)(2,1)S(1)}, bf16[2,64,768]{2,1,0:T(8,128)(2,1)S(1)}, u32[]{:S(2)}, u32[]{:S(2)}) collective-permute-start(bf16[2,64,768]{2,1,0:T(8,128)(2,1)S(1)} %maximum_select_fusion.4), channel_id=1, source_target_pairs={{0,8},{8,0},{1,9},{9,1},{2,10},{10,2},{3,11},{11,3},{4,12},{12,4},... | collective-permute-start | bytes 589832 | tf_op jit(solution)/shard_map/gather_tokens/ppermute | solution.py:975
  30.9 12.0 %copy-start.3 = (bf16[2,2,64,768]{3,2,1,0:T(8,128)(2,1)S(1)}, bf16[2,2,64,768]{3,2,1,0:T(8,128)(2,1)}, u32[]{:S(2)}) copy-start(bf16[2,2,64,768]{3,2,1,0:T(8,128)(2,1)} %hold.12) | copy-start | bytes 1179652
  30.9 12.0 %collective-permute-start.3 = (bf16[2,2,64,768]{3,2,1,0:T(8,128)(2,1)}, bf16[2,2,64,768]{3,2,1,0:T(8,128)(2,1)S(1)}, u32[]{:S(2)}, u32[]{:S(2)}) collective-permute-start(bf16[2,2,64,768]{3,2,1,0:T(8,128)(2,1)} %hold.12), channel_id=1, source_target_pairs={{0,4},{4,0},{1,5},{5,1},{2,6},{6,2},{3,7},{7,3},{8,12},{12,8},{9,1... | collective-permute-start | bytes 1179656 | tf_op jit(solution)/shard_map/gather_tokens/ppermute | solution.py:977
  34.1 11.6 %all-to-all-start.1 = ((bf16[8,24,640]{2,1,0:T(8,128)(2,1)}), bf16[8,24,640]{2,1,0:T(8,128)(2,1)S(1)}, u32[]{:S(2)}, u32[]{:S(2)}) async-start(bf16[8,24,640]{2,1,0:T(8,128)(2,1)} %bitcast.26), calls=%async_computation.1 | async-start | bytes 491520 | tf_op jit(solution)/shard_map/gather_qkv_weights/all_to_all | solution.py:968
  37.5 60.2 %all-gather.3.cloned.1.call-start = ((), (), s32[]{:S(2)}) async-start(), calls=%async_computation.9 | async-start | bytes 2949120 | tf_op jit(solution)/shard_map/gather_ff_weights/all_gather | solution.py:1006
  45.7 0.7 copy-start.5
  56.4 1.2 copy-start.4
  56.6 6.9 %copy-start.8 = (bf16[2,1,2,2,2,2,24,576]{7,6,5,4,3,2,0,1:T(8,128)(2,1)}, bf16[2,1,2,2,2,2,24,576]{7,6,5,4,3,2,0,1:T(8,128)(2,1)S(1)}, u32[]{:S(2)}) copy-start(bf16[2,1,2,2,2,2,24,576]{7,6,5,4,3,2,0,1:T(8,128)(2,1)S(1)} %copy.78) | copy-start | bytes 2654212
  59.0 4.5 %collective-permute-start.5 = (bf16[512,384]{1,0:T(8,128)(2,1)}, bf16[512,384]{1,0:T(8,128)(2,1)}, u32[]{:S(2)}, u32[]{:S(2)}) collective-permute-start(bf16[512,384]{1,0:T(8,128)(2,1)} %fusion.refs_0_.refs_1_), channel_id=1, source_target_pairs={{0,1},{1,0},{2,3},{3,2},{4,5},{5,4},{6,7},{7,6},{8,9},{9,8},{10,11... | collective-permute-start | bytes 1179656 | tf_op jit(solution)/shard_map/gather_kv/ppermute | solution.py:1026
  59.4 11.4 %collective-permute-start.4 = (bf16[512,384]{1,0:T(8,128)(2,1)}, bf16[512,384]{1,0:T(8,128)(2,1)S(1)}, u32[]{:S(2)}, u32[]{:S(2)}) collective-permute-start(bf16[512,384]{1,0:T(8,128)(2,1)} %fusion.refs_0_.refs_1_), channel_id=1, source_target_pairs={{0,2},{2,0},{1,3},{3,1},{4,6},{6,4},{5,7},{7,5},{8,10},{10,8},{9,1... | collective-permute-start | bytes 1179656 | tf_op jit(solution)/shard_map/gather_kv/ppermute | solution.py:1025
  70.8 0.7 copy-start.13
  71.5 4.4 %collective-permute-start.6 = (bf16[512,384]{1,0:T(8,128)(2,1)}, bf16[512,384]{1,0:T(8,128)(2,1)S(1)}, u32[]{:S(2)}, u32[]{:S(2)}) collective-permute-start(bf16[512,384]{1,0:T(8,128)(2,1)} %hold.14.refs_2_), channel_id=1, source_target_pairs={{0,1},{1,0},{2,3},{3,2},{4,5},{5,4},{6,7},{7,6},{8,9},{9,8},{10,11... | collective-permute-start | bytes 1179656 | tf_op jit(solution)/shard_map/attention/ppermute | solution.py:1061
  76.0 0.8 copy-start.29
  98.8 2.1 copy-start.11
  98.8 2.1 collective-permute-start.7
  100.9 0.8 copy-start.28
  106.0 0.9 copy-start.9
  106.0 14.2 %collective-permute-start.8 = (bf16[768,1536]{1,0:T(8,128)(2,1)}, bf16[768,1536]{1,0:T(8,128)(2,1)S(1)}, u32[]{:S(2)}, u32[]{:S(2)}) collective-permute-start(bf16[768,1536]{1,0:T(8,128)(2,1)} %hold.16.own_ref), channel_id=1, source_target_pairs={{0,1},{1,0},{2,3},{3,2},{4,5},{5,4},{6,7},{7,6},{8,9},{9,8},{10,11... | collective-permute-start | bytes 7077896 | tf_op jit(solution)/shard_map/first_norm/ppermute | solution.py:1082
  120.2 1.4 copy-start.27
  166.4 11.5 %all-to-all-start.4 = ((bf16[4,128,768]{2,1,0:T(8,128)(2,1)}), bf16[4,128,768]{2,1,0:T(8,128)(2,1)S(1)}, u32[]{:S(2)}, u32[]{:S(2)}) async-start(bf16[4,128,768]{2,1,0:T(8,128)(2,1)} %bitcast.144), calls=%async_computation.4 | async-start | bytes 1572864 | tf_op jit(solution)/shard_map/sum_hidden_grad/all_to_all | solution.py:834
  176.2 12.6 %collective-permute-start.10 = (bf16[768,1152]{1,0:T(8,128)(2,1)}, bf16[768,1152]{1,0:T(8,128)(2,1)S(1)}, u32[]{:S(2)}, u32[]{:S(2)}) collective-permute-start(bf16[768,1152]{1,0:T(8,128)(2,1)} %get-tuple-element.94), channel_id=1, source_target_pairs={{0,1},{1,0},{2,3},{3,2},{4,5},{5,4},{6,7},{7,6},{8,9},{9,8},{10,11... | collective-permute-start | bytes 5308424 | tf_op jit(solution)/shard_map/attn_weight_grad/ppermute | solution.py:826
  177.9 0.9 copy-start.10
  182.9 5.9 %copy-start.7 = (bf16[768,1152]{1,0:T(8,128)(2,1)S(1)}, bf16[768,1152]{1,0:T(8,128)(2,1)}, u32[]{:S(2)}) copy-start(bf16[768,1152]{1,0:T(8,128)(2,1)} %get-tuple-element.87._) | copy-start | bytes 5308420
  182.9 4.3 %collective-permute-start.9 = (bf16[768,512]{1,0:T(8,128)(2,1)}, bf16[768,512]{1,0:T(8,128)(2,1)}, u32[]{:S(2)}, u32[]{:S(2)}) collective-permute-start(bf16[768,512]{1,0:T(8,128)(2,1)} %get-tuple-element.93), channel_id=1, source_target_pairs={{0,1},{1,0},{2,3},{3,2},{4,5},{5,4},{6,7},{7,6},{8,9},{9,8},{10,11... | collective-permute-start | bytes 2359304 | tf_op jit(solution)/shard_map/attn_weight_grad/ppermute | solution.py:826
  182.9 13.9 %all-to-all-start.5 = ((bf16[8,64,192]{2,1,0:T(8,128)(2,1)}), bf16[8,64,192]{2,1,0:T(8,128)(2,1)}, u32[]{:S(2)}, u32[]{:S(2)}) async-start(bf16[8,64,192]{2,1,0:T(8,128)(2,1)} %get-tuple-element.89), calls=%async_computation.5 | async-start | bytes 524288 | tf_op jit(solution)/shard_map/send_out_grad/all_to_all | solution.py:1126
  187.2 60.0 %reduce-scatter.2.cloned.1.call-start = ((), (), s32[]{:S(2)}) async-start(), calls=%async_computation.10 | async-start | bytes 3194880 | tf_op jit(solution)/shard_map/attn_weight_grad/reduce_scatter | solution.py:1134
  197.5 10.0 %copy-start.18 = (f32[2,768]{1,0:T(2,128)S(1)}, f32[2,768]{1,0:T(2,128)}, u32[]{:S(2)}) copy-start(f32[2,768]{1,0:T(2,128)} %get-tuple-element.103) | copy-start | bytes 18436
  207.0 1.9 collective-permute-start.11
  208.2 8.2 %collective-permute-start.12 = (bf16[512,384]{1,0:T(8,128)(2,1)}, bf16[512,384]{1,0:T(8,128)(2,1)S(1)}, u32[]{:S(2)}, u32[]{:S(2)}) collective-permute-start(bf16[512,384]{1,0:T(8,128)(2,1)} %get-tuple-element.100), channel_id=1, source_target_pairs={{0,1},{1,0},{2,3},{3,2},{4,5},{5,4},{6,7},{7,6},{8,9},{9,8},{10,11... | collective-permute-start | bytes 1179656 | tf_op jit(solution)/shard_map/sum_kv_grads/ppermute | solution.py:1165
  210.0 1.6 copy-start.14
  210.0 11.2 %collective-permute-start.13 = (bf16[512,384]{1,0:T(8,128)(2,1)S(1)}, bf16[512,384]{1,0:T(8,128)(2,1)S(1)}, u32[]{:S(2)}, u32[]{:S(2)}) collective-permute-start(bf16[512,384]{1,0:T(8,128)(2,1)S(1)} %add_convert_fusion.3.refs_0_), channel_id=1, source_target_pairs={{0,2},{2,0},{1,3},{3,1},{4,6},{6,4},{5,7},{7,5},{8,10},{10,8},{9,1... | collective-permute-start | bytes 1179656 | tf_op jit(solution)/shard_map/sum_kv_grads/ppermute | solution.py:1166
  216.5 4.8 %copy-start.31 = (bf16[512,384]{1,0:T(8,128)(2,1)}, bf16[512,384]{1,0:T(8,128)(2,1)S(1)}, u32[]{:S(2)}) copy-start(bf16[512,384]{1,0:T(8,128)(2,1)S(1)} %collective-permute-done.12.c_ref) | copy-start | bytes 1179652
  221.2 0.7 copy-start.32
  228.8 5.0 %copy-start.30 = (bf16[4,64,768]{2,1,0:T(8,128)(2,1)S(1)}, bf16[4,64,768]{2,1,0:T(8,128)(2,1)}, u32[]{:S(2)}) copy-start(bf16[4,64,768]{2,1,0:T(8,128)(2,1)} %get-tuple-element.106) | copy-start | bytes 1179652
  228.8 2.1 collective-permute-start.14
  232.1 13.2 %copy-start.1 = (bf16[2,208,576]{2,1,0:T(8,128)(2,1)}, bf16[2,208,576]{2,1,0:T(8,128)(2,1)S(1)}, u32[]{:S(2)}) copy-start(bf16[2,208,576]{2,1,0:T(8,128)(2,1)S(1)} %add_convert_fusion.2.refs_1_) | copy-start | bytes 1437700
  232.1 8.5 %collective-permute-start.16 = (bf16[208,576]{1,0:T(8,128)(2,1)S(1)}, bf16[208,576]{1,0:T(8,128)(2,1)S(1)}, u32[]{:S(2)}, u32[]{:S(2)}) collective-permute-start(bf16[208,576]{1,0:T(8,128)(2,1)S(1)} %dynamic-slice_bitcast_fusion.1), channel_id=1, source_target_pairs={{0,2},{2,0},{1,3},{3,1},{4,6},{6,4},{5,7},{7,5},{8,10},{10,8},{9,1... | collective-permute-start | bytes 718856 | tf_op jit(solution)/shard_map/qkv_weight_grad/ppermute | solution.py:826
  233.7 11.5 %collective-permute-start.15 = (bf16[4,64,768]{2,1,0:T(8,128)(2,1)S(1)}, bf16[4,64,768]{2,1,0:T(8,128)(2,1)S(1)}, u32[]{:S(2)}, u32[]{:S(2)}) collective-permute-start(bf16[4,64,768]{2,1,0:T(8,128)(2,1)S(1)} %copy-done.30), channel_id=1, source_target_pairs={{0,4},{4,0},{1,5},{5,1},{2,6},{6,2},{3,7},{7,3},{8,12},{12,8},{9,1... | collective-permute-start | bytes 1179656 | tf_op jit(solution)/shard_map/qkv_weight_grad/ppermute | solution.py:1187
  241.7 14.5 %all-to-all-start.6 = ((bf16[8,32,576]{2,1,0:T(8,128)(2,1)}), bf16[8,32,576]{2,1,0:T(8,128)(2,1)S(1)}, u32[]{:S(2)}, u32[]{:S(2)}) async-start(bf16[8,32,576]{2,1,0:T(8,128)(2,1)} %maximum_maximum_fusion.refs_1_), calls=%async_computation.7 | async-start | bytes 655360 | tf_op jit(solution)/shard_map/qkv_weight_grad/all_to_all | solution.py:1208
  247.1 16.8 %collective-permute-start.17 = (bf16[2,64,768]{2,1,0:T(8,128)(2,1)}, bf16[2,64,768]{2,1,0:T(8,128)(2,1)S(1)}, u32[]{:S(2)}, u32[]{:S(2)}) collective-permute-start(bf16[2,64,768]{2,1,0:T(8,128)(2,1)} %hold.20), channel_id=1, source_target_pairs={{0,8},{8,0},{1,9},{9,1},{2,10},{10,2},{3,11},{11,3},{4,12},{12,4},... | collective-permute-start | bytes 589832 | tf_op jit(solution)/shard_map/input_grad/ppermute | solution.py:1203
  249.9 14.0 %copy-start.2 = (f32[2,64,768]{2,1,0:T(8,128)S(1)}, f32[2,64,768]{2,1,0:T(8,128)}, u32[]{:S(2)}) copy-start(f32[2,64,768]{2,1,0:T(8,128)} %hold.19) | copy-start | bytes 1179652
  256.2 0.7 copy-start
  259.7 14.2 %all-to-all-start.7 = ((bf16[8,24,1280]{2,1,0:T(8,128)(2,1)}), bf16[8,24,1280]{2,1,0:T(8,128)(2,1)S(1)}, u32[]{:S(2)}, u32[]{:S(2)}) async-start(bf16[8,24,1280]{2,1,0:T(8,128)(2,1)} %bitcast.63.refs_1_), calls=%async_computation.8 | async-start | bytes 983040 | tf_op jit(solution)/shard_map/ff_weight_grads/all_to_all | solution.py:1243
  264.6 9.3 %collective-permute-start.19 = (bf16[96,384]{1,0:T(8,128)(2,1)S(1)}, bf16[96,384]{1,0:T(8,128)(2,1)S(1)}, u32[]{:S(2)}, u32[]{:S(2)}) collective-permute-start(bf16[96,384]{1,0:T(8,128)(2,1)S(1)} %get-tuple-element.116), channel_id=1, source_target_pairs={{0,1},{1,0},{2,3},{3,2},{4,5},{5,4},{6,7},{7,6},{8,9},{9,8},{10,11... | collective-permute-start | bytes 221192 | tf_op jit(solution)/shard_map/ff_weight_grads/ppermute | solution.py:1247
  265.0 8.0 %collective-permute-start.18 = (bf16[64,768]{1,0:T(8,128)(2,1)}, bf16[64,768]{1,0:T(8,128)(2,1)S(1)}, u32[]{:S(2)}, u32[]{:S(2)}) collective-permute-start(bf16[64,768]{1,0:T(8,128)(2,1)} %hold.21), channel_id=1, source_target_pairs={{0,16},{16,0},{1,17},{17,1},{2,18},{18,2},{3,19},{19,3},{4,20},{20... | collective-permute-start | bytes 294920 | tf_op jit(solution)/shard_map/qkv_weight_grad/ppermute | solution.py:1209
  265.0 8.1 %copy-start.12 = (f32[128,768]{1,0:T(8,128)S(1)}, f32[128,768]{1,0:T(8,128)}, u32[]{:S(2)}) copy-start(f32[128,768]{1,0:T(8,128)} %get-tuple-element.88) | copy-start | bytes 1179652
  273.9 0.6 copy-start.16
  273.9 0.8 copy-start.6
Sparse Core Ops, SparseCore 0:
  40.5 54.3 all-gather.2
  197.0 50.0 reduce-scatter.1

commit v2 on v1

--- a/solution.py
+++ b/solution.py
@@ -268,16 +268,6 @@
     )
 
 
-def assemble(core_ref, own_ref, swap_ref, columns, target, sems):
-    core = core_ref[0]
-    copies = []
-    for which, (piece, half) in enumerate(((own_ref, core), (swap_ref, 1 - core))):
-        copy = pltpu.make_async_copy(piece.at[:, columns], target.at[half], sems.at[which])
-        copy.start()
-        copies.append(copy)
-    return copies
-
-
 def merged(parts_ref):
     return jnp.concatenate(
         [
@@ -290,7 +280,6 @@
 
 
 def first_norm_kernel(
-    columns,
     core_ref,
     mixed_ref,
     rows_ref,
@@ -301,13 +290,11 @@
     hidden_ref,
     normal_ref,
     scale_ref,
-    weight_ref,
-    sems,
 ):
-    for copy in assemble(core_ref, own_ref, swap_ref, columns, weight_ref, sems):
-        copy.wait()
     mixed = merged(mixed_ref)
-    lin = jnp.concatenate([nn(mixed, weight_ref[0]), nn(mixed, weight_ref[1])], axis=1)
+    first = core_ref[0] == 0
+    own, swap = nn(mixed, own_ref[...]), nn(mixed, swap_ref[...])
+    lin = jnp.concatenate([jnp.where(first, own, swap), jnp.where(first, swap, own)], axis=1)
     total = rows_ref[...].astype(F32) + (lin + vec_ref[2:3, :])
     normal, scale = normalised(total)
     hidden = normal * vec_ref[3:4, :] + vec_ref[4:5, :]
@@ -337,24 +324,19 @@
     return jnp.sum(values, axis=0, keepdims=True)
 
 
-def first_norm(core, mixed, rows, vectors, own, swap, columns):
+def first_norm(core, mixed, rows, vectors, own, swap):
     tokens, width = rows.shape
     vmem = pl.BlockSpec(memory_space=pltpu.VMEM)
-    half = columns.stop - columns.start
     return pl.pallas_call(
-        functools.partial(first_norm_kernel, columns),
+        first_norm_kernel,
         out_shape=(
             jax.ShapeDtypeStruct((tokens, width), BF16),
             jax.ShapeDtypeStruct((tokens, width), F32),
             jax.ShapeDtypeStruct((tokens, width), F32),
             jax.ShapeDtypeStruct((tokens, 1), F32),
-            jax.ShapeDtypeStruct((2, width, half), BF16),
-        ),
-        in_specs=[pl.BlockSpec(memory_space=pltpu.SMEM)]
-        + [vmem] * 3
-        + [pl.BlockSpec(memory_space=pl.ANY)] * 2,
-        out_specs=(vmem,) * 5,
-        scratch_shapes=[pltpu.SemaphoreType.DMA((2,))],
+        ),
+        in_specs=[pl.BlockSpec(memory_space=pltpu.SMEM)] + [vmem] * 5,
+        out_specs=(vmem,) * 4,
         compiler_params=pltpu.CompilerParams(vmem_limit_bytes=VMEM_BYTES),
         cost_estimate=pl.CostEstimate(
             flops=64 * tokens * width * width, bytes_accessed=4 * width * width, transcendentals=0
@@ -364,74 +346,49 @@
 
 
 def ff_forward_kernel(
-    in_columns,
-    out_columns,
-    core_ref,
-    hidden_ref,
-    bias_ref,
-    own_ref,
-    swap_ref,
-    act_ref,
-    slope_ref,
-    gelu_ref,
-    parts_ref,
-    w_in_ref,
-    w_out_ref,
-    sems,
+    units, out_columns, core_ref, hidden_ref, bias_ref, own_ref, swap_ref, act_ref, slope_ref, gelu_ref, parts_ref
 ):
-    in_copies = assemble(core_ref, own_ref, swap_ref, in_columns, w_in_ref, sems.at[0])
-    out_copies = assemble(core_ref, own_ref, swap_ref, out_columns, w_out_ref, sems.at[1])
-    for copy in in_copies:
-        copy.wait()
     tokens = hidden_ref.shape[0]
-
-    def expand(tile, carry):
+    first = core_ref[0] == 0
+
+    def visit(tile, carry):
         at = pl.ds(pl.multiple_of(tile * FF_TILE, FF_TILE), FF_TILE)
         rows = hidden_ref[at, :]
-        gate = nn(rows, w_in_ref[0]) + bias_ref[0:1, :]
-        up = nn(rows, w_in_ref[1]) + bias_ref[1:2, :]
+        own = nn(rows, own_ref[:, :units])
+        swap = nn(rows, swap_ref[:, :units])
+        gate = jnp.where(first, own, swap) + bias_ref[0:1, :]
+        up = jnp.where(first, swap, own) + bias_ref[1:2, :]
         cdf = 0.5 * (1.0 + lax.erf(gate * (0.5**0.5)))
         density = jnp.exp(-0.5 * gate * gate) * 0.3989422804014327
         gelu = gate * cdf
-        act_ref[at, :] = (gelu * up).astype(BF16)
+        act = (gelu * up).astype(BF16)
+        act_ref[at, :] = act
         gelu_ref[at, :] = gelu.astype(BF16)
         slope_ref[at, :] = (up * (cdf + gate * density)).astype(BF16)
+        own = nn(act, own_ref[:, out_columns]).astype(BF16)
+        swap = nn(act, swap_ref[:, out_columns]).astype(BF16)
+        parts_ref[at, :] = jnp.concatenate(
+            [jnp.where(first, own, swap), jnp.where(first, swap, own)], axis=1
+        )
         return carry
 
-    lax.fori_loop(0, tokens // FF_TILE, expand, 0)
-    for copy in out_copies:
-        copy.wait()
-
-    def contract(tile, carry):
-        at = pl.ds(pl.multiple_of(tile * FF_TILE, FF_TILE), FF_TILE)
-        rows = act_ref[at, :]
-        parts_ref[at, :] = jnp.concatenate(
-            [nn(rows, w_out_ref[0]), nn(rows, w_out_ref[1])], axis=1
-        ).astype(BF16)
-        return carry
-
-    lax.fori_loop(0, tokens // FF_TILE, contract, 0)
-
-
-def ff_forward(core, hidden, bias, own, swap, in_columns, out_columns):
+    lax.fori_loop(0, tokens // FF_TILE, visit, 0)
+
+
+def ff_forward(core, hidden, bias, own, swap, out_columns):
     tokens, width = hidden.shape
     units = bias.shape[1]
     vmem = pl.BlockSpec(memory_space=pltpu.VMEM)
     return pl.pallas_call(
-        functools.partial(ff_forward_kernel, in_columns, out_columns),
+        functools.partial(ff_forward_kernel, units, out_columns),
         out_shape=(
             jax.ShapeDtypeStruct((tokens, units), BF16),
             jax.ShapeDtypeStruct((tokens, units), BF16),
             jax.ShapeDtypeStruct((tokens, units), BF16),
             jax.ShapeDtypeStruct((tokens, width), BF16),
-            jax.ShapeDtypeStruct((2, width, units), BF16),
-            jax.ShapeDtypeStruct((2, units, width // 2), BF16),
-        ),
-        in_specs=[pl.BlockSpec(memory_space=pltpu.SMEM)]
-        + [vmem] * 2
-        + [pl.BlockSpec(memory_space=pl.ANY)] * 2,
-        out_specs=(vmem,) * 6,
-        scratch_shapes=[pltpu.SemaphoreType.DMA((2, 2))],
+        ),
+        in_specs=[pl.BlockSpec(memory_space=pltpu.SMEM)] + [vmem] * 4,
+        out_specs=(vmem,) * 4,
         compiler_params=pltpu.CompilerParams(vmem_limit_bytes=VMEM_BYTES),
         cost_estimate=pl.CostEstimate(
             flops=32 * tokens * width * units,
@@ -486,10 +443,22 @@
 
 
 def ff_backward_kernel(
-    grad_ref, slope_ref, gelu_ref, w_in_ref, w_out_ref, joined_ref, parts_ref, bias_ref, half_ref
+    units,
+    out_columns,
+    core_ref,
+    grad_ref,
+    slope_ref,
+    gelu_ref,
+    own_ref,
+    swap_ref,
+    joined_ref,
+    parts_ref,
+    bias_ref,
+    half_ref,
 ):
     tokens, width = grad_ref.shape
     half = width // 2
+    first = core_ref[0] == 0
     bias_ref[...] = jnp.zeros_like(bias_ref)
 
     def visit(tile, carry):
@@ -497,32 +466,37 @@
         left, right = grad_ref[at, :half], grad_ref[at, half:]
         half_ref[0, at, :] = left
         half_ref[1, at, :] = right
-        act_grad = nt(left, w_out_ref[0]) + nt(right, w_out_ref[1])
+        act_grad = nt(jnp.where(first, left, right), own_ref[:, out_columns]) + nt(
+            jnp.where(first, right, left), swap_ref[:, out_columns]
+        )
+        joined = []
         for which, factor in ((0, slope_ref), (1, gelu_ref)):
-            joined = (act_grad * factor[at, :].astype(F32)).astype(BF16)
-            joined_ref[which, at, :] = joined
-            bias_ref[which : which + 1, :] += column_sum(joined.astype(F32))
+            side = (act_grad * factor[at, :].astype(F32)).astype(BF16)
+            joined_ref[which, at, :] = side
+            bias_ref[which : which + 1, :] += column_sum(side.astype(F32))
+            joined.append(side)
         parts_ref[at, :] = (
-            nt(joined_ref[0, at, :], w_in_ref[0]) + nt(joined_ref[1, at, :], w_in_ref[1])
+            nt(jnp.where(first, joined[0], joined[1]), own_ref[:, :units])
+            + nt(jnp.where(first, joined[1], joined[0]), swap_ref[:, :units])
         ).astype(BF16)
         return carry
 
     lax.fori_loop(0, tokens // FF_TILE, visit, 0)
 
 
-def ff_backward(grads, slope, gelu, w_in, w_out):
+def ff_backward(core, grads, slope, gelu, own, swap, out_columns):
     tokens, width = grads.shape
     units = slope.shape[1]
     vmem = pl.BlockSpec(memory_space=pltpu.VMEM)
     return pl.pallas_call(
-        ff_backward_kernel,
+        functools.partial(ff_backward_kernel, units, out_columns),
         out_shape=(
             jax.ShapeDtypeStruct((2, tokens, units), BF16),
             jax.ShapeDtypeStruct((tokens, width), BF16),
             jax.ShapeDtypeStruct((2, units), F32),
             jax.ShapeDtypeStruct((2, tokens, width // 2), BF16),
         ),
-        in_specs=[vmem] * 5,
+        in_specs=[pl.BlockSpec(memory_space=pltpu.SMEM)] + [vmem] * 5,
         out_specs=(vmem,) * 4,
         compiler_params=pltpu.CompilerParams(vmem_limit_bytes=VMEM_BYTES),
         cost_estimate=pl.CostEstimate(
@@ -531,7 +505,7 @@
             transcendentals=0,
         ),
         name="ff_backward",
-    )(grads, slope, gelu, w_in, w_out)
+    )(core, grads, slope, gelu, own, swap)
 
 
 def ff_grads_kernel(core_ref, act_ref, half_ref, hidden_ref, joined_ref, keep_ref, give_ref):
@@ -573,7 +547,8 @@
     normal_ref,
     scale_ref,
     vec_ref,
-    weight_ref,
+    own_ref,
+    swap_ref,
     sums_ref,
     mixed_ref,
     _,
@@ -589,7 +564,11 @@
     back = norm_back(grads, normal, scale_ref[...], vec_ref[3:4, :])
     low = back.astype(BF16)
     grad_ref[...] = back
-    out_grad = nt(low[:, :half], weight_ref[0]) + nt(low[:, half:], weight_ref[1])
+    own_left = core_ref[0] == 0
+    left, right = low[:, :half], low[:, half:]
+    out_grad = nt(jnp.where(own_left, left, right), own_ref[...]) + nt(
+        jnp.where(own_left, right, left), swap_ref[...]
+    )
     for seq in range(2):
         for group in range(GROUPS):
             out_ref[seq * GROUPS + group] = out_grad[
@@ -610,12 +589,13 @@
     mixed = merged(mixed_ref)
     left = tn(mixed, low[:, :half]).astype(BF16)
     right = tn(mixed, low[:, half:]).astype(BF16)
-    own_left = core_ref[0] == 0
     keep_ref[:, :half] = jnp.where(own_left, left, right)
     give_ref[:, :half] = jnp.where(own_left, right, left)
 
 
-def first_back(core, parts, second_grad, normal, scale, vectors, weight, sums, mixed, earlier):
+def first_back(
+    core, parts, second_grad, normal, scale, vectors, own, swap, sums, mixed, earlier
+):
     tokens, width = second_grad.shape
     vmem = pl.BlockSpec(memory_space=pltpu.VMEM)
     return pl.pallas_call(
@@ -627,7 +607,7 @@
             jax.ShapeDtypeStruct((width, width // 2 + 128), BF16),
         ),
         in_specs=[pl.BlockSpec(memory_space=pltpu.SMEM)]
-        + [vmem] * 8
+        + [vmem] * 9
         + [pl.BlockSpec(memory_space=pl.ANY)],
         out_specs=(vmem,) * 4,
         compiler_params=pltpu.CompilerParams(vmem_limit_bytes=VMEM_BYTES),
@@ -635,7 +615,7 @@
             flops=64 * tokens * width * width, bytes_accessed=4 * width * width, transcendentals=0
         ),
         name="first_back",
-    )(core, parts, second_grad, normal, scale, vectors, weight, sums, mixed, earlier)
+    )(core, parts, second_grad, normal, scale, vectors, own, swap, sums, mixed, earlier)
 
 
 def input_back_kernel(
@@ -723,6 +703,37 @@
     )(place, chunk, grads, shifts)
 
 
+def spread_kernel(ring, in_ref, attn_ref, out_ref):
+    units = in_ref.shape[1] // 8
+    piece = units // ring
+    half = attn_ref.shape[1] // 2
+    for side in range(2):
+        for plane in range(4):
+            out_ref[2 * plane + side, :, :units] = jnp.concatenate(
+                [
+                    in_ref[:, at : at + piece]
+                    for at in (
+                        (side * ring + place) * 4 * piece + plane * piece for place in range(ring)
+                    )
+                ],
+                axis=1,
+            )
+            out_ref[2 * plane + side, :, units:] = attn_ref[:, side * half : (side + 1) * half]
+
+
+def spread_weights(w_in, w_attn_out, ring):
+    shard, cols = w_in.shape
+    vmem = pl.BlockSpec(memory_space=pltpu.VMEM)
+    return pl.pallas_call(
+        functools.partial(spread_kernel, ring),
+        out_shape=jax.ShapeDtypeStruct((8, shard, cols // 8 + w_attn_out.shape[1] // 2), BF16),
+        in_specs=[vmem] * 2,
+        out_specs=vmem,
+        compiler_params=pltpu.CompilerParams(vmem_limit_bytes=VMEM_BYTES),
+        name="spread",
+    )(w_in, w_attn_out)
+
+
 def share_kernel(shard, shifts, first_ref, parts_ref, weight_ref, sums_ref, shift_ref):
     totals = [
         parts_ref[group].astype(F32) + parts_ref[GROUPS + group].astype(F32)
@@ -776,8 +787,8 @@
     __,
     in_ref,
     attn_ref,
-    vec_ref,
     out_ref,
+    *vec_refs,
 ):
     keep, come = keep_ref[...].astype(F32), come_ref[...].astype(F32)
     own_first = core_ref[0] == 0
@@ -798,7 +809,9 @@
             parts_ref[plane, side, :, :half].astype(F32) for plane in range(4)
         )
     vectors = sum(parts_ref[plane, 0, :, half:start].astype(F32) for plane in range(4))
-    vec_ref[...] = vectors.T[:8]
+    rows = vectors.T
+    for number, vec_ref in enumerate(vec_refs):
+        vec_ref[...] = rows[number : number + 1]
 
 
 def unpack(core, parts, keep, come, half, ring, *earlier):
@@ -810,13 +823,13 @@
         out_shape=(
             jax.ShapeDtypeStruct((shard, 8 * units), F32),
             jax.ShapeDtypeStruct((shard, 2 * half), F32),
-            jax.ShapeDtypeStruct((8, shard), F32),
             jax.ShapeDtypeStruct((keep.shape[0], 2 * half), F32),
-        ),
+        )
+        + (jax.ShapeDtypeStruct((1, shard), F32),) * 6,
         in_specs=[pl.BlockSpec(memory_space=pltpu.SMEM)]
         + [vmem] * 3
         + [pl.BlockSpec(memory_space=pl.ANY)] * 2,
-        out_specs=(vmem,) * 4,
+        out_specs=(vmem,) * 9,
         compiler_params=pltpu.CompilerParams(vmem_limit_bytes=VMEM_BYTES),
         name="unpack",
     )(core, parts, keep, come, *earlier)
@@ -901,15 +914,18 @@
     half = width // 2
 
     with jax.named_scope("gather_ff_weights"):
-        in_cols = (
-            w_in.reshape(shard, 2, ring, 4, 2 * ff_shard)
-            .transpose(3, 1, 0, 2, 4)
-            .reshape(4, 2, shard, units)
-        )
-        attn_cols = w_attn_out.reshape(shard, 2, half).transpose(1, 0, 2)
-        in_parts = jnp.concatenate(
-            [in_cols, jnp.broadcast_to(attn_cols, (4, 2, shard, half))], axis=3
-        ).reshape(8, shard, units + half)
+        if outer == 1:
+            in_parts = spread_weights(w_in, w_attn_out, ring)
+        else:
+            in_cols = (
+                w_in.reshape(shard, 2, ring, 4, 2 * ff_shard)
+                .transpose(3, 1, 0, 2, 4)
+                .reshape(4, 2, shard, units)
+            )
+            attn_cols = w_attn_out.reshape(shard, 2, half).transpose(1, 0, 2)
+            in_parts = jnp.concatenate(
+                [in_cols, jnp.broadcast_to(attn_cols, (4, 2, shard, half))], axis=3
+            ).reshape(8, shard, units + half)
         in_parts = lax.all_to_all(
             in_parts, ("x", "y", "c"), 0, 0, tiled=True
         ).reshape(8 * shard, units + half)
@@ -1069,27 +1085,25 @@
         packed = hold(packed, returned)
         attn_own = packed[:, units : units + half]
         attn_swap = lax.ppermute(attn_own, "c", SWAP)
-        hidden_low, hidden, normal, scale, attn_full = first_norm(
+        hidden_low, hidden, normal, scale = first_norm(
             core,
             returned,
             tokens.reshape(2 * row_count, width),
             vectors,
             attn_own,
             attn_swap,
-            slice(0, half),
         )
         packed = hold(packed, hidden_low)
         swapped = lax.ppermute(packed, "c", SWAP)
     with jax.named_scope("gather_hidden"):
         hidden_group = gather_plane(hidden_low)
     with jax.named_scope("ff_forward"):
-        activated_low, slope, gelu, ff_parts, in_slice, out_slice = ff_forward(
+        activated_low, slope, gelu, ff_parts = ff_forward(
             core,
             hidden_group,
             in_shift,
             packed,
             swapped,
-            slice(0, units),
             slice(units + half, units + width),
         )
     with jax.named_scope("sum_ff"):
@@ -1102,7 +1116,7 @@
         ff_grads = gather_plane(ff_grad)
     with jax.named_scope("ff_backward"):
         joined_grad, hidden_parts, grad_in_shift, grad_halves = ff_backward(
-            ff_grads, slope, gelu, in_slice, out_slice
+            core, ff_grads, slope, gelu, packed, swapped, slice(units + half, units + width)
         )
     with jax.named_scope("sum_hidden_grad"):
         hidden_parts = spread_plane(hidden_parts)
@@ -1117,7 +1131,8 @@
             normal,
             scale,
             vectors,
-            attn_full,
+            attn_own,
+            attn_swap,
             sums,
             returned,
             ff_keep,
@@ -1247,9 +1262,10 @@
         out_come = lax.ppermute(pick(out_sums, 1 - c_at), "c", SWAP)
         out_keep = pick(out_sums, c_at)
         if outer == 1:
-            grad_w_in, grad_w_attn, vector_grads, grad_w_out = unpack(
+            grad_w_in, grad_w_attn, grad_w_out, *vector_grads = unpack(
                 core, exchanged, out_keep, out_come, half, ring, grad_w_qkv, input_grad
             )
+            vector_grads = [row.reshape(shard) for row in vector_grads]
         else:
             grad_w_in = (
                 exchanged[..., half + 128 :]

time: 287 us -> 283 us (0.986)
  local copies, waits for them, and re-layouts: 27.3 us -> 24 us
    pallas_call x3 -> x4, Pallas kernels: 18.8 us -> 19.1 us  [the longest x1 7.26 us: ff_backward(): pl.pallas_call(functools.partial(ff_backward_kernel, units, out_columns),...]
    unnamed x70 -> x68, local copies, waits for them, and re-layouts: 9.05 us -> 9.06 us
  transfers between devices with their start and end apart: 28 -> 28, of which waited for: 13 -> 13; matrix products, arithmetic and copies ran while one was open for 11% -> 10% of each run, Pallas kernels for 16% -> 17%
where the time goes in v2:
time: 283 us; the launch traced here: 281 us
  Pallas kernels  70.5 us (25%)
  blocking collectives  67.7 us (24%)
  waiting for transfers between devices  48.7 us (17%)
  starting transfers between devices  38.1 us (13%)
  local copies, waits for them, and re-layouts  24 us (8%)
  between operations  15.4 us (5%)
  other arithmetic  14.1 us (5%)
    all_gather x2, blocking collectives, gather_plane(): return lax.all_gather(block, PLANE, axis=0, tiled=True)  25.6 us
    all_to_all x1, blocking collectives, body(): lax.all_to_all(attended_low.reshape(8, row_count, GROUP_WIDTH), SEQ_GROUP...  17.2 us
    all_to_all x1, blocking collectives, spread_plane(): lax.all_to_all(parts.reshape(4, -1, parts.shape[1]), PLANE, 0, 0, tiled=T...  15.1 us
    pallas_call x2, Pallas kernels, attend_back(): pl.pallas_call(functools.partial(attend_back_kernel, len(earlier), count,...  14.6 us
    pallas_call x3, Pallas kernels, attend(): pl.pallas_call(functools.partial(attend_kernel, len(earlier), count, firs...  13.1 us
    all_gather x1, blocking collectives, body(): parcels = lax.all_gather(hold(parcel, chunk), CHUNKS, axis=0, tiled=False)  9.83 us
    unnamed x68, local copies, waits for them, and re-layouts  9.06 us
    ppermute x5, waiting for transfers between devices, swap_sum(): lax.ppermute(give.astype(BF16), axis, SWAP).astype(F32)  7.8 us
  transfers between devices with their start and end apart: 28, of which 13 were waited for; matrix products, arithmetic and copies ran while one was open for 10% of the time, Pallas kernels for 17%

profile of v2, /device:TPU:0, one launch (start us, length us, event | category | flops | bytes accessed | tf_op | source)
XLA Modules:
  0.0 281.0 jit_solution(16090943635758360799)
XLA Ops:
  7.2 1.0 constant_dynamic-slice_fusion.9
  8.2 4.1 %collective-permute-start = (bf16[64,768]{1,0:T(8,128)(2,1)S(1)}, bf16[64,768]{1,0:T(8,128)(2,1)S(1)}, u32[]{:S(2)}, u32[]{:S(2)}) collective-permute-start(bf16[64,768]{1,0:T(8,128)(2,1)S(1)} %get-tuple-element.119), channel_id=1, source_target_pairs={{0,16},{16,0},{1,17},{17,1},{2,18},{18,2},{3,19},{19,3},{4,20},{20... | collective-permute-start | bytes 294920 | tf_op jit(solution)/shard_map/gather_tokens/ppermute | solution.py:989
  12.3 0.9 reshape.252
  13.8 1.9 spread.1
  15.6 3.8 %all-to-all-start = ((bf16[8,24,1152]{2,1,0:T(8,128)(2,1)}), bf16[8,24,1152]{2,1,0:T(8,128)(2,1)S(1)}, u32[]{:S(2)}, u32[]{:S(2)}) async-start(bf16[8,24,1152]{2,1,0:T(8,128)(2,1)} %spread.1), calls=%async_computation | async-start | bytes 884736 | tf_op jit(solution)/shard_map/gather_ff_weights/all_to_all | solution.py:929
  20.5 1.6 collective-permute-start.1
  22.2 5.7 %collective-permute-done.1 = bf16[2,64,768]{2,1,0:T(8,128)(2,1)S(1)} collective-permute-done((bf16[2,64,768]{2,1,0:T(8,128)(2,1)S(1)}, bf16[2,64,768]{2,1,0:T(8,128)(2,1)S(1)}, u32[]{:S(2)}, u32[]{:S(2)}) %collective-permute-start.1) | collective-permute-done | bytes 196640 | tf_op jit(solution)/shard_map/gather_tokens/ppermute | solution.py:991
  28.6 0.9 pad_maximum_fusion.1.refs_1_
  30.0 1.7 collective-permute-start.3
  33.2 3.4 %all-to-all-start.1 = ((bf16[8,24,640]{2,1,0:T(8,128)(2,1)}), bf16[8,24,640]{2,1,0:T(8,128)(2,1)S(1)}, u32[]{:S(2)}, u32[]{:S(2)}) async-start(bf16[8,24,640]{2,1,0:T(8,128)(2,1)} %bitcast.23), calls=%async_computation.1 | async-start | bytes 491520 | tf_op jit(solution)/shard_map/gather_qkv_weights/all_to_all | solution.py:984
  37.3 4.7 %collective-permute-done.3 = bf16[2,2,64,768]{3,2,1,0:T(8,128)(2,1)S(1)} collective-permute-done((bf16[2,2,64,768]{3,2,1,0:T(8,128)(2,1)}, bf16[2,2,64,768]{3,2,1,0:T(8,128)(2,1)S(1)}, u32[]{:S(2)}, u32[]{:S(2)}) %collective-permute-start.3) | collective-permute-done | bytes 393248 | tf_op jit(solution)/shard_map/gather_tokens/ppermute | solution.py:993
  42.2 1.0 copy.66
  43.2 1.5 all-to-all-done.1.refs_0_
  45.5 9.8 %all-gather = bf16[32,24,640]{2,1,0:T(8,128)(2,1)S(1)} all-gather(bf16[8,24,640]{2,1,0:T(8,128)(2,1)} %hold.13), channel_id=2, replica_groups=mesh['s'=2,'e'=1,'r'=2,'x'=2,'y'=2,'c'=2] {'e','y','c'}, dimensions={0}, use_global_device_ids=true | all-gather | bytes 1228800 | tf_op jit(solution)/shard_map/gather_qkv_weights/all_gather | solution.py:997
  56.5 1.4 fusion.refs_0_.refs_1_
  61.3 1.1 fusion.1.q_ref
  62.4 5.4 %attend.3 = (f32[192,512]{1,0:T(8,128)}, f32[6,512]{1,0:T(8,128)}) custom-call(f32[3]{0:T(128)} %power_multiply_fusion.slopes_ref, bf16[512,192]{1,0:T(8,128)(2,1)} %fusion.1.q_ref, f32[1,512]{1,0:T(1,128)} %get-tuple-element.130.pq_ref.pk_ref, f32[2,512]{1,0:T(2,128)} %maximum_bitcast_fusion.1.pk_ref, bf16[512,384]{1,0:T(8,128)(2,1)} %fusion.refs_0_.refs_1_, ...), custom_call_target="tpu_custom_call" | custom-call | flops 6442450944 | bytes 524288 | tf_op jit(solution)/shard_map/attention/attend/pallas_call | solution.py:147
  67.8 1.9 collective-permute-done.4.refs_0_
  71.1 3.7 %attend.4 = (f32[192,512]{1,0:T(8,128)}, f32[6,512]{1,0:T(8,128)}) custom-call(f32[3]{0:T(128)} %power_multiply_fusion.slopes_ref, bf16[512,192]{1,0:T(8,128)(2,1)} %fusion.1.q_ref, f32[1,512]{1,0:T(1,128)} %get-tuple-element.130.pq_ref.pk_ref, f32[1,512]{1,0:T(1,128)} %get-tuple-element.127.pk_ref, f32[8,768]{1,0:T(8,128)} %convert_element_type.113.refs_0_.vec_ref, ...), custom_call_target="tpu_custom_call" | custom-call | flops 3221225472 | bytes 262144 | tf_op jit(solution)/shard_map/attention/attend/pallas_call | solution.py:147
  75.6 4.0 %attend.5 = (f32[192,512]{1,0:T(8,128)}, f32[3,512]{1,0:T(4,128)}, bf16[512,192]{1,0:T(8,128)(2,1)}) custom-call(f32[3]{0:T(128)} %power_multiply_fusion.slopes_ref, bf16[512,192]{1,0:T(8,128)(2,1)} %fusion.1.q_ref, f32[1,512]{1,0:T(1,128)} %get-tuple-element.130.pq_ref.pk_ref, f32[1,512]{1,0:T(1,128)} %get-tuple-element.129.pk_ref, ...), custom_call_target="tpu_custom_call" | custom-call | flops 3221225472 | bytes 262144 | tf_op jit(solution)/shard_map/attention/attend/pallas_call | solution.py:147
  79.6 17.2 %all_to_all.40.refs_1_.mixed_ref = bf16[8,64,192]{2,1,0:T(8,128)(2,1)} all-to-all(bf16[8,64,192]{2,1,0:T(8,128)(2,1)} %bitcast.144), channel_id=1, replica_groups=mesh['s'=2,'e'=1,'r'=2,'x'=2,'y'=2,'c'=2] {'s','r','x'}, dimensions={0} | all-to-all | bytes 393216 | tf_op jit(solution)/shard_map/return_attended/all_to_all | solution.py:1081
  96.7 1.1 slice.120.own_ref
  98.0 2.0 collective-permute-done.7.swap_ref
  100.0 0.8 copy-done.27
  100.8 3.0 %first_norm.1 = (bf16[128,768]{1,0:T(8,128)(2,1)}, f32[128,768]{1,0:T(8,128)}, f32[128,768]{1,0:T(8,128)}, f32[128,1]{1,0:T(8,128)}) custom-call(s32[1]{0:T(128)} %bitcast.core_ref, bf16[8,64,192]{2,1,0:T(8,128)(2,1)} %all_to_all.40.refs_1_.mixed_ref, bf16[128,768]{1,0:T(8,128)(2,1)} %bitcast.145, f32[8,768]{1,0:T(8,128)} %convert_element_type.113.refs_0_.vec_ref, ...), custom_call_target="tpu_custom_call" | custom-call | flops 4831838208 | bytes 2359296 | tf_op jit(solution)/shard_map/first_norm/first_norm/pallas_call | solution.py:330
  104.7 13.4 %all_gather.18.hidden_ref = bf16[512,768]{1,0:T(8,128)(2,1)} all-gather(bf16[128,768]{1,0:T(8,128)(2,1)S(1)} %copy-done.9), channel_id=1, replica_groups=mesh['s'=2,'e'=1,'r'=2,'x'=2,'y'=2,'c'=2] {'x','y'}, dimensions={0}, use_global_device_ids=true | all-gather | bytes 983040 | tf_op jit(solution)/shard_map/gather_hidden/all_gather | solution.py:843
  118.2 1.4 copy-done.26
  119.6 6.9 %ff_forward.1 = (bf16[512,768]{1,0:T(8,128)(2,1)}, bf16[512,768]{1,0:T(8,128)(2,1)}, bf16[512,768]{1,0:T(8,128)(2,1)}, bf16[512,768]{1,0:T(8,128)(2,1)}) custom-call(s32[1]{0:T(128)} %bitcast.core_ref, bf16[512,768]{1,0:T(8,128)(2,1)} %all_gather.18.hidden_ref, f32[2,768]{1,0:T(2,128)} %reshape.279.refs_1_.bias_ref, bf16[768,1536]{1,0:T(8,128)(2,1)} %hold.16.own_ref, ...), custom_call_target="tpu_custom_call" | custom-call | flops 9663676416 | bytes 3538944 | tf_op jit(solution)/shard_map/ff_forward/ff_forward/pallas_call | solution.py:382
  126.5 15.1 %all_to_all.41.parts_ref = bf16[4,128,768]{2,1,0:T(8,128)(2,1)} all-to-all(bf16[4,128,768]{2,1,0:T(8,128)(2,1)} %bitcast.135), channel_id=1, replica_groups=mesh['s'=2,'e'=1,'r'=2,'x'=2,'y'=2,'c'=2] {'x','y'}, dimensions={0} | all-to-all | bytes 1572864 | tf_op jit(solution)/shard_map/sum_ff/all_to_all | solution.py:847
  141.7 2.5 second_norm.1
  144.2 12.2 %all_gather.19.grad_ref = bf16[512,768]{1,0:T(8,128)(2,1)} all-gather(bf16[128,768]{1,0:T(8,128)(2,1)} %get-tuple-element.75), channel_id=1, replica_groups=mesh['s'=2,'e'=1,'r'=2,'x'=2,'y'=2,'c'=2] {'x','y'}, dimensions={0}, use_global_device_ids=true | all-gather | bytes 983040 | tf_op jit(solution)/shard_map/gather_ff_grad/all_gather | solution.py:843
  156.3 7.3 %ff_backward.1 = (bf16[2,512,768]{2,1,0:T(8,128)(2,1)}, bf16[512,768]{1,0:T(8,128)(2,1)}, f32[2,768]{1,0:T(2,128)}, bf16[2,512,384]{2,1,0:T(8,128)(2,1)}) custom-call(s32[1]{0:T(128)} %bitcast.core_ref, bf16[512,768]{1,0:T(8,128)(2,1)} %all_gather.19.grad_ref, bf16[512,768]{1,0:T(8,128)(2,1)} %get-tuple-element.76.slope_ref, ...), custom_call_target="tpu_custom_call" | custom-call | flops 9663676416 | bytes 3538944 | tf_op jit(solution)/shard_map/ff_backward/ff_backward/pallas_call | solution.py:491
  163.6 3.5 %all-to-all-start.4 = ((bf16[4,128,768]{2,1,0:T(8,128)(2,1)}), bf16[4,128,768]{2,1,0:T(8,128)(2,1)S(1)}, u32[]{:S(2)}, u32[]{:S(2)}) async-start(bf16[4,128,768]{2,1,0:T(8,128)(2,1)} %bitcast.134), calls=%async_computation.4 | async-start | bytes 1572864 | tf_op jit(solution)/shard_map/sum_hidden_grad/all_to_all | solution.py:847
  167.1 6.3 %ff_grads.1 = (bf16[768,1152]{1,0:T(8,128)(2,1)}, bf16[768,1152]{1,0:T(8,128)(2,1)}) custom-call(s32[1]{0:T(128)} %bitcast.core_ref, bf16[512,768]{1,0:T(8,128)(2,1)} %get-tuple-element.83.act_ref, bf16[2,512,384]{2,1,0:T(8,128)(2,1)} %get-tuple-element.84.half_ref, bf16[512,768]{1,0:T(8,128)(2,1)} %all_gather.18.hidden_ref, ...), custom_call_target="tpu_custom_call" | custom-call | flops 6000000000 | bytes 10000 | tf_op jit(solution)/shard_map/ff_weight_grads/ff_grads/pallas_call | solution.py:532
  173.4 1.7 all-to-all-done.4.parts_ref
  175.1 0.9 copy-done.10
  176.0 4.1 %first_back.1 = (f32[128,768]{1,0:T(8,128)}, bf16[8,64,192]{2,1,0:T(8,128)(2,1)}, bf16[768,512]{1,0:T(8,128)(2,1)}, bf16[768,512]{1,0:T(8,128)(2,1)}) custom-call(s32[1]{0:T(128)} %bitcast.core_ref, bf16[4,128,768]{2,1,0:T(8,128)(2,1)} %copy-done.10, f32[128,768]{1,0:T(8,128)} %get-tuple-element.79.second_ref, f32[128,768]{1,0:T(8,128)} %get-tuple-element.80.normal_ref, ...), custom_call_target="tpu_custom_call" | custom-call | flops 4831838208 | bytes 2359296 | tf_op jit(solution)/shard_map/first_norm_back/first_back/pallas_call | solution.py:601
  180.1 4.2 %all-to-all-start.5 = ((bf16[8,64,192]{2,1,0:T(8,128)(2,1)}), bf16[8,64,192]{2,1,0:T(8,128)(2,1)}, u32[]{:S(2)}, u32[]{:S(2)}) async-start(bf16[8,64,192]{2,1,0:T(8,128)(2,1)} %get-tuple-element.88), calls=%async_computation.5 | async-start | bytes 524288 | tf_op jit(solution)/shard_map/send_out_grad/all_to_all | solution.py:1141
  184.4 1.6 add_convert_fusion.1
  186.4 1.6 pad_maximum_fusion.refs_0_
  188.0 6.0 %all-to-all-done.5 = bf16[8,64,192]{2,1,0:T(8,128)(2,1)} async-done(((bf16[8,64,192]{2,1,0:T(8,128)(2,1)}), bf16[8,64,192]{2,1,0:T(8,128)(2,1)}, u32[]{:S(2)}, u32[]{:S(2)}) %all-to-all-start.5) | async-done | bytes 196640 | tf_op jit(solution)/shard_map/send_out_grad/all_to_all | solution.py:1141
  194.7 9.7 %attend_back.2 = (f32[192,512]{1,0:T(8,128)}, bf16[512,384]{1,0:T(8,128)(2,1)}, bf16[512,384]{1,0:T(8,128)(2,1)}, bf16[512,384]{1,0:T(8,128)(2,1)}) custom-call(f32[3]{0:T(128)} %power_multiply_fusion.slopes_ref, bf16[512,192]{1,0:T(8,128)(2,1)} %fusion.1.q_ref, f32[1,512]{1,0:T(1,128)} %get-tuple-element.130.pq_ref.pk_ref, ...), custom_call_target="tpu_custom_call" | custom-call | flops 12683575296 | bytes 786432 | tf_op jit(solution)/shard_map/attention_back/attend_back/pallas_call | solution.py:240
  206.3 1.1 add_convert_fusion.3.refs_0_
  207.4 1.5 collective-permute-start.13
  208.9 4.9 %attend_back.3 = (bf16[512,192]{1,0:T(8,128)(2,1)}, bf16[512,384]{1,0:T(8,128)(2,1)}) custom-call(f32[3]{0:T(128)} %power_multiply_fusion.slopes_ref, bf16[512,192]{1,0:T(8,128)(2,1)} %fusion.1.q_ref, f32[1,512]{1,0:T(1,128)} %get-tuple-element.130.pq_ref.pk_ref, f32[1,512]{1,0:T(1,128)} %get-tuple-element.130.pq_ref.pk_ref, ...), custom_call_target="tpu_custom_call" | custom-call | flops 4227858432 | bytes 262144 | tf_op jit(solution)/shard_map/attention_back/attend_back/pallas_call | solution.py:240
  213.9 4.8 %collective-permute-done.13.y_ref = bf16[512,384]{1,0:T(8,128)(2,1)S(1)} collective-permute-done((bf16[512,384]{1,0:T(8,128)(2,1)S(1)}, bf16[512,384]{1,0:T(8,128)(2,1)S(1)}, u32[]{:S(2)}, u32[]{:S(2)}) %collective-permute-start.13) | collective-permute-done | bytes 393248 | tf_op jit(solution)/shard_map/sum_kv_grads/ppermute | solution.py:1181
  219.4 3.6 %input_back.1 = (bf16[4,64,768]{2,1,0:T(8,128)(2,1)}, bf16[4,64,768]{2,1,0:T(8,128)(2,1)}, bf16[512,576]{1,0:T(8,128)(2,1)}) custom-call(s32[3]{0:T(128)} %pad_add_fusion.place_ref, bf16[512,192]{1,0:T(8,128)(2,1)} %get-tuple-element.97.dq_ref, bf16[512,384]{1,0:T(8,128)(2,1)} %get-tuple-element.98.own_ref, bf16[512,384]{1,0:T(8,128)(2,1)} %copy-done.30, ...), custom_call_target="tpu_custom_call" | custom-call | flops 2264924160 | bytes 1572864 | tf_op jit(solution)/shard_map/input_back/input_back/pallas_call | solution.py:641
  223.0 3.2 %qkv_weight.1 = (bf16[2,208,576]{2,1,0:T(8,128)(2,1)}, bf16[2,208,576]{2,1,0:T(8,128)(2,1)}) custom-call(s32[3]{0:T(128)} %pad_add_fusion.place_ref, bf16[512,768]{1,0:T(8,128)(2,1)} %bitcast.121, bf16[512,576]{1,0:T(8,128)(2,1)} %get-tuple-element.101.grad_ref, f32[8,192]{1,0:T(8,128)} %reshape.266.shift_ref), custom_call_target="tpu_custom_call" | custom-call | flops 3170893824 | bytes 1572864 | tf_op jit(solution)/shard_map/qkv_weight_grad/qkv_weight/pallas_call | solution.py:693
  226.2 2.1 collective-permute-done.14
  228.3 1.2 add_convert_fusion.2.refs_1_
  229.5 1.5 collective-permute-start.16
  231.1 1.4 collective-permute-start.15
  232.5 5.5 %collective-permute-done.16 = bf16[208,576]{1,0:T(8,128)(2,1)S(1)} collective-permute-done((bf16[208,576]{1,0:T(8,128)(2,1)S(1)}, bf16[208,576]{1,0:T(8,128)(2,1)S(1)}, u32[]{:S(2)}, u32[]{:S(2)}) %collective-permute-start.16) | collective-permute-done | bytes 239648 | tf_op jit(solution)/shard_map/qkv_weight_grad/ppermute | solution.py:839
  238.2 0.9 maximum_maximum_fusion.refs_1_
  239.1 3.6 %all-to-all-start.6 = ((bf16[8,32,576]{2,1,0:T(8,128)(2,1)}), bf16[8,32,576]{2,1,0:T(8,128)(2,1)S(1)}, u32[]{:S(2)}, u32[]{:S(2)}) async-start(bf16[8,32,576]{2,1,0:T(8,128)(2,1)} %maximum_maximum_fusion.refs_1_), calls=%async_computation.7 | async-start | bytes 655360 | tf_op jit(solution)/shard_map/qkv_weight_grad/all_to_all | solution.py:1223
  242.6 1.1 convert_add_fusion
  244.4 2.0 collective-permute-start.17
  247.2 6.3 %all-to-all-done.6.refs_1_.refs_0_ = bf16[8,32,576]{2,1,0:T(8,128)(2,1)S(1)} async-done(((bf16[8,32,576]{2,1,0:T(8,128)(2,1)}), bf16[8,32,576]{2,1,0:T(8,128)(2,1)S(1)}, u32[]{:S(2)}, u32[]{:S(2)}) %all-to-all-start.6) | async-done | bytes 294944 | tf_op jit(solution)/shard_map/qkv_weight_grad/all_to_all | solution.py:1223
  254.3 1.8 slice.124
  256.1 0.9 slice.125
  257.0 3.5 %all-to-all-start.7 = ((bf16[8,24,1280]{2,1,0:T(8,128)(2,1)}), bf16[8,24,1280]{2,1,0:T(8,128)(2,1)S(1)}, u32[]{:S(2)}, u32[]{:S(2)}) async-start(bf16[8,24,1280]{2,1,0:T(8,128)(2,1)} %bitcast.60.refs_1_), calls=%async_computation.8 | async-start | bytes 983040 | tf_op jit(solution)/shard_map/ff_weight_grads/all_to_all | solution.py:1258
  262.4 1.9 share.1
  264.2 6.1 %collective-permute-done.18 = bf16[64,768]{1,0:T(8,128)(2,1)S(1)} collective-permute-done((bf16[64,768]{1,0:T(8,128)(2,1)}, bf16[64,768]{1,0:T(8,128)(2,1)S(1)}, u32[]{:S(2)}, u32[]{:S(2)}) %collective-permute-start.18) | collective-permute-done | bytes 98336 | tf_op jit(solution)/shard_map/qkv_weight_grad/ppermute | solution.py:1224
  272.0 2.1 unpack.1
  (173 shorter events, 22.4 us)
Async XLA Ops:
  7.2 12.3 %copy-start.18 = (s32[2,256]{1,0:T(2,128)S(1)}, s32[2,256]{1,0:T(2,128)}, u32[]{:S(2)}) copy-start(s32[2,256]{1,0:T(2,128)} %param.16) | copy-start | bytes 6148
  7.2 12.4 %copy-start.32 = (bf16[192]{0:T(256)(128)(2,1)S(1)}, bf16[192]{0:T(256)(128)(2,1)}, u32[]{:S(2)}) copy-start(bf16[192]{0:T(256)(128)(2,1)} %param.24) | copy-start | bytes 1156
  7.2 12.5 %copy-start.15 = (bf16[24,2304]{1,0:T(8,128)(2,1)S(1)}, bf16[24,2304]{1,0:T(8,128)(2,1)}, u32[]{:S(2)}) copy-start(bf16[24,2304]{1,0:T(8,128)(2,1)} %param.17) | copy-start | bytes 331780
  8.2 12.2 %collective-permute-start = (bf16[64,768]{1,0:T(8,128)(2,1)S(1)}, bf16[64,768]{1,0:T(8,128)(2,1)S(1)}, u32[]{:S(2)}, u32[]{:S(2)}) collective-permute-start(bf16[64,768]{1,0:T(8,128)(2,1)S(1)} %get-tuple-element.119), channel_id=1, source_target_pairs={{0,16},{16,0},{1,17},{17,1},{2,18},{18,2},{3,19},{19,3},{4,20},{20... | collective-permute-start | bytes 294920 | tf_op jit(solution)/shard_map/gather_tokens/ppermute | solution.py:989
  13.3 6.8 %copy-start.19 = (bf16[2,24]{1,0:T(2,128)(2,1)S(1)}, bf16[2,24]{1,0:T(2,128)(2,1)}, u32[]{:S(2)}) copy-start(bf16[2,24]{1,0:T(2,128)(2,1)} %param.18) | copy-start | bytes 292
  13.3 6.8 %copy-start.20 = (bf16[24]{0:T(256)(128)(2,1)S(1)}, bf16[24]{0:T(256)(128)(2,1)}, u32[]{:S(2)}) copy-start(bf16[24]{0:T(256)(128)(2,1)} %param.20) | copy-start | bytes 148
  13.3 6.8 %copy-start.21 = (bf16[24]{0:T(256)(128)(2,1)S(1)}, bf16[24]{0:T(256)(128)(2,1)}, u32[]{:S(2)}) copy-start(bf16[24]{0:T(256)(128)(2,1)} %param.21) | copy-start | bytes 148
  13.3 6.8 %copy-start.22 = (bf16[24]{0:T(256)(128)(2,1)S(1)}, bf16[24]{0:T(256)(128)(2,1)}, u32[]{:S(2)}) copy-start(bf16[24]{0:T(256)(128)(2,1)} %param.22) | copy-start | bytes 148
  13.3 6.8 %copy-start.23 = (bf16[24]{0:T(256)(128)(2,1)S(1)}, bf16[24]{0:T(256)(128)(2,1)}, u32[]{:S(2)}) copy-start(bf16[24]{0:T(256)(128)(2,1)} %param.26) | copy-start | bytes 148
  13.3 6.8 %copy-start.24 = (bf16[24]{0:T(256)(128)(2,1)S(1)}, bf16[24]{0:T(256)(128)(2,1)}, u32[]{:S(2)}) copy-start(bf16[24]{0:T(256)(128)(2,1)} %param.27) | copy-start | bytes 148
  13.3 6.8 %copy-start.25 = (bf16[24]{0:T(256)(128)(2,1)S(1)}, bf16[24]{0:T(256)(128)(2,1)}, u32[]{:S(2)}) copy-start(bf16[24]{0:T(256)(128)(2,1)} %param.28) | copy-start | bytes 148
  13.7 8.4 %collective-permute-start.2 = (bf16[96,384]{1,0:T(8,128)(2,1)S(1)}, bf16[96,384]{1,0:T(8,128)(2,1)S(1)}, u32[]{:S(2)}, u32[]{:S(2)}) collective-permute-start(bf16[96,384]{1,0:T(8,128)(2,1)S(1)} %bitcast.147), channel_id=1, source_target_pairs={{0,1},{1,0},{2,3},{3,2},{4,5},{5,4},{6,7},{7,6},{8,9},{9,8},{10,11... | collective-permute-start | bytes 221192 | tf_op jit(solution)/shard_map/gather_ff_weights/ppermute | solution.py:934
  15.6 13.0 %all-to-all-start = ((bf16[8,24,1152]{2,1,0:T(8,128)(2,1)}), bf16[8,24,1152]{2,1,0:T(8,128)(2,1)S(1)}, u32[]{:S(2)}, u32[]{:S(2)}) async-start(bf16[8,24,1152]{2,1,0:T(8,128)(2,1)} %spread.1), calls=%async_computation | async-start | bytes 884736 | tf_op jit(solution)/shard_map/gather_ff_weights/all_to_all | solution.py:929
  20.5 7.4 %collective-permute-start.1 = (bf16[2,64,768]{2,1,0:T(8,128)(2,1)S(1)}, bf16[2,64,768]{2,1,0:T(8,128)(2,1)S(1)}, u32[]{:S(2)}, u32[]{:S(2)}) collective-permute-start(bf16[2,64,768]{2,1,0:T(8,128)(2,1)S(1)} %maximum_select_fusion.4), channel_id=1, source_target_pairs={{0,8},{8,0},{1,9},{9,1},{2,10},{10,2},{3,11},{11,3},{4,12},{12,4},... | collective-permute-start | bytes 589832 | tf_op jit(solution)/shard_map/gather_tokens/ppermute | solution.py:991
  30.0 12.0 %copy-start.3 = (bf16[2,2,64,768]{3,2,1,0:T(8,128)(2,1)S(1)}, bf16[2,2,64,768]{3,2,1,0:T(8,128)(2,1)}, u32[]{:S(2)}) copy-start(bf16[2,2,64,768]{3,2,1,0:T(8,128)(2,1)} %hold.12) | copy-start | bytes 1179652
  30.0 12.0 %collective-permute-start.3 = (bf16[2,2,64,768]{3,2,1,0:T(8,128)(2,1)}, bf16[2,2,64,768]{3,2,1,0:T(8,128)(2,1)S(1)}, u32[]{:S(2)}, u32[]{:S(2)}) collective-permute-start(bf16[2,2,64,768]{3,2,1,0:T(8,128)(2,1)} %hold.12), channel_id=1, source_target_pairs={{0,4},{4,0},{1,5},{5,1},{2,6},{6,2},{3,7},{7,3},{8,12},{12,8},{9,1... | collective-permute-start | bytes 1179656 | tf_op jit(solution)/shard_map/gather_tokens/ppermute | solution.py:993
  33.2 11.6 %all-to-all-start.1 = ((bf16[8,24,640]{2,1,0:T(8,128)(2,1)}), bf16[8,24,640]{2,1,0:T(8,128)(2,1)S(1)}, u32[]{:S(2)}, u32[]{:S(2)}) async-start(bf16[8,24,640]{2,1,0:T(8,128)(2,1)} %bitcast.23), calls=%async_computation.1 | async-start | bytes 491520 | tf_op jit(solution)/shard_map/gather_qkv_weights/all_to_all | solution.py:984
  36.6 60.2 %all-gather.3.cloned.1.call-start = ((), (), s32[]{:S(2)}) async-start(), calls=%async_computation.9 | async-start | bytes 2949120 | tf_op jit(solution)/shard_map/gather_ff_weights/all_gather | solution.py:1022
  44.8 0.7 copy-start.5
  55.3 1.2 copy-start.4
  55.5 6.9 %copy-start.8 = (bf16[2,1,2,2,2,2,24,576]{7,6,5,4,3,2,0,1:T(8,128)(2,1)}, bf16[2,1,2,2,2,2,24,576]{7,6,5,4,3,2,0,1:T(8,128)(2,1)S(1)}, u32[]{:S(2)}) copy-start(bf16[2,1,2,2,2,2,24,576]{7,6,5,4,3,2,0,1:T(8,128)(2,1)S(1)} %copy.70) | copy-start | bytes 2654212
  57.9 4.5 %collective-permute-start.5 = (bf16[512,384]{1,0:T(8,128)(2,1)}, bf16[512,384]{1,0:T(8,128)(2,1)}, u32[]{:S(2)}, u32[]{:S(2)}) collective-permute-start(bf16[512,384]{1,0:T(8,128)(2,1)} %fusion.refs_0_.refs_1_), channel_id=1, source_target_pairs={{0,1},{1,0},{2,3},{3,2},{4,5},{5,4},{6,7},{7,6},{8,9},{9,8},{10,11... | collective-permute-start | bytes 1179656 | tf_op jit(solution)/shard_map/gather_kv/ppermute | solution.py:1042
  58.3 11.4 %collective-permute-start.4 = (bf16[512,384]{1,0:T(8,128)(2,1)}, bf16[512,384]{1,0:T(8,128)(2,1)S(1)}, u32[]{:S(2)}, u32[]{:S(2)}) collective-permute-start(bf16[512,384]{1,0:T(8,128)(2,1)} %fusion.refs_0_.refs_1_), channel_id=1, source_target_pairs={{0,2},{2,0},{1,3},{3,1},{4,6},{6,4},{5,7},{7,5},{8,10},{10,8},{9,1... | collective-permute-start | bytes 1179656 | tf_op jit(solution)/shard_map/gather_kv/ppermute | solution.py:1041
  69.7 0.7 copy-start.13
  70.4 4.4 %collective-permute-start.6 = (bf16[512,384]{1,0:T(8,128)(2,1)}, bf16[512,384]{1,0:T(8,128)(2,1)S(1)}, u32[]{:S(2)}, u32[]{:S(2)}) collective-permute-start(bf16[512,384]{1,0:T(8,128)(2,1)} %hold.14.refs_2_), channel_id=1, source_target_pairs={{0,1},{1,0},{2,3},{3,2},{4,5},{5,4},{6,7},{7,6},{8,9},{9,8},{10,11... | collective-permute-start | bytes 1179656 | tf_op jit(solution)/shard_map/attention/ppermute | solution.py:1077
  74.8 0.7 copy-start.28
  97.9 2.1 copy-start.11
  97.9 2.1 collective-permute-start.7
  99.9 0.8 copy-start.27
  103.8 0.9 copy-start.9
  103.8 14.4 %collective-permute-start.8 = (bf16[768,1536]{1,0:T(8,128)(2,1)}, bf16[768,1536]{1,0:T(8,128)(2,1)S(1)}, u32[]{:S(2)}, u32[]{:S(2)}) collective-permute-start(bf16[768,1536]{1,0:T(8,128)(2,1)} %hold.16.own_ref), channel_id=1, source_target_pairs={{0,1},{1,0},{2,3},{3,2},{4,5},{5,4},{6,7},{7,6},{8,9},{9,8},{10,11... | collective-permute-start | bytes 7077896 | tf_op jit(solution)/shard_map/first_norm/ppermute | solution.py:1097
  118.2 1.4 copy-start.26
  163.6 11.5 %all-to-all-start.4 = ((bf16[4,128,768]{2,1,0:T(8,128)(2,1)}), bf16[4,128,768]{2,1,0:T(8,128)(2,1)S(1)}, u32[]{:S(2)}, u32[]{:S(2)}) async-start(bf16[4,128,768]{2,1,0:T(8,128)(2,1)} %bitcast.134), calls=%async_computation.4 | async-start | bytes 1572864 | tf_op jit(solution)/shard_map/sum_hidden_grad/all_to_all | solution.py:847
  173.4 12.5 %collective-permute-start.10 = (bf16[768,1152]{1,0:T(8,128)(2,1)}, bf16[768,1152]{1,0:T(8,128)(2,1)S(1)}, u32[]{:S(2)}, u32[]{:S(2)}) collective-permute-start(bf16[768,1152]{1,0:T(8,128)(2,1)} %get-tuple-element.93), channel_id=1, source_target_pairs={{0,1},{1,0},{2,3},{3,2},{4,5},{5,4},{6,7},{7,6},{8,9},{9,8},{10,11... | collective-permute-start | bytes 5308424 | tf_op jit(solution)/shard_map/attn_weight_grad/ppermute | solution.py:839
  175.1 0.9 copy-start.10
  180.1 5.9 %copy-start.7 = (bf16[768,1152]{1,0:T(8,128)(2,1)S(1)}, bf16[768,1152]{1,0:T(8,128)(2,1)}, u32[]{:S(2)}) copy-start(bf16[768,1152]{1,0:T(8,128)(2,1)} %get-tuple-element.86._) | copy-start | bytes 5308420
  180.1 4.2 %collective-permute-start.9 = (bf16[768,512]{1,0:T(8,128)(2,1)}, bf16[768,512]{1,0:T(8,128)(2,1)}, u32[]{:S(2)}, u32[]{:S(2)}) collective-permute-start(bf16[768,512]{1,0:T(8,128)(2,1)} %get-tuple-element.92), channel_id=1, source_target_pairs={{0,1},{1,0},{2,3},{3,2},{4,5},{5,4},{6,7},{7,6},{8,9},{9,8},{10,11... | collective-permute-start | bytes 2359304 | tf_op jit(solution)/shard_map/attn_weight_grad/ppermute | solution.py:839
  180.1 13.9 %all-to-all-start.5 = ((bf16[8,64,192]{2,1,0:T(8,128)(2,1)}), bf16[8,64,192]{2,1,0:T(8,128)(2,1)}, u32[]{:S(2)}, u32[]{:S(2)}) async-start(bf16[8,64,192]{2,1,0:T(8,128)(2,1)} %get-tuple-element.88), calls=%async_computation.5 | async-start | bytes 524288 | tf_op jit(solution)/shard_map/send_out_grad/all_to_all | solution.py:1141
  184.3 60.1 %reduce-scatter.2.cloned.1.call-start = ((), (), s32[]{:S(2)}) async-start(), calls=%async_computation.10 | async-start | bytes 3194880 | tf_op jit(solution)/shard_map/attn_weight_grad/reduce_scatter | solution.py:1149
  194.7 10.3 %copy-start.17 = (f32[2,768]{1,0:T(2,128)S(1)}, f32[2,768]{1,0:T(2,128)}, u32[]{:S(2)}) copy-start(f32[2,768]{1,0:T(2,128)} %get-tuple-element.102) | copy-start | bytes 18436
  204.4 1.9 collective-permute-start.11
  205.6 8.2 %collective-permute-start.12 = (bf16[512,384]{1,0:T(8,128)(2,1)}, bf16[512,384]{1,0:T(8,128)(2,1)S(1)}, u32[]{:S(2)}, u32[]{:S(2)}) collective-permute-start(bf16[512,384]{1,0:T(8,128)(2,1)} %get-tuple-element.99), channel_id=1, source_target_pairs={{0,1},{1,0},{2,3},{3,2},{4,5},{5,4},{6,7},{7,6},{8,9},{9,8},{10,11... | collective-permute-start | bytes 1179656 | tf_op jit(solution)/shard_map/sum_kv_grads/ppermute | solution.py:1180
  207.4 1.5 copy-start.14
  207.4 11.2 %collective-permute-start.13 = (bf16[512,384]{1,0:T(8,128)(2,1)S(1)}, bf16[512,384]{1,0:T(8,128)(2,1)S(1)}, u32[]{:S(2)}, u32[]{:S(2)}) collective-permute-start(bf16[512,384]{1,0:T(8,128)(2,1)S(1)} %add_convert_fusion.3.refs_0_), channel_id=1, source_target_pairs={{0,2},{2,0},{1,3},{3,1},{4,6},{6,4},{5,7},{7,5},{8,10},{10,8},{9,1... | collective-permute-start | bytes 1179656 | tf_op jit(solution)/shard_map/sum_kv_grads/ppermute | solution.py:1181
  213.8 4.8 %copy-start.30 = (bf16[512,384]{1,0:T(8,128)(2,1)}, bf16[512,384]{1,0:T(8,128)(2,1)S(1)}, u32[]{:S(2)}) copy-start(bf16[512,384]{1,0:T(8,128)(2,1)S(1)} %collective-permute-done.12.c_ref) | copy-start | bytes 1179652
  218.6 0.7 copy-start.31
  226.2 4.9 %copy-start.29 = (bf16[4,64,768]{2,1,0:T(8,128)(2,1)S(1)}, bf16[4,64,768]{2,1,0:T(8,128)(2,1)}, u32[]{:S(2)}) copy-start(bf16[4,64,768]{2,1,0:T(8,128)(2,1)} %get-tuple-element.105) | copy-start | bytes 1179652
  226.2 2.1 collective-permute-start.14
  229.5 13.2 %copy-start.1 = (bf16[2,208,576]{2,1,0:T(8,128)(2,1)}, bf16[2,208,576]{2,1,0:T(8,128)(2,1)S(1)}, u32[]{:S(2)}) copy-start(bf16[2,208,576]{2,1,0:T(8,128)(2,1)S(1)} %add_convert_fusion.2.refs_1_) | copy-start | bytes 1437700
  229.5 8.5 %collective-permute-start.16 = (bf16[208,576]{1,0:T(8,128)(2,1)S(1)}, bf16[208,576]{1,0:T(8,128)(2,1)S(1)}, u32[]{:S(2)}, u32[]{:S(2)}) collective-permute-start(bf16[208,576]{1,0:T(8,128)(2,1)S(1)} %dynamic-slice_bitcast_fusion.1), channel_id=1, source_target_pairs={{0,2},{2,0},{1,3},{3,1},{4,6},{6,4},{5,7},{7,5},{8,10},{10,8},{9,1... | collective-permute-start | bytes 718856 | tf_op jit(solution)/shard_map/qkv_weight_grad/ppermute | solution.py:839
  231.1 11.5 %collective-permute-start.15 = (bf16[4,64,768]{2,1,0:T(8,128)(2,1)S(1)}, bf16[4,64,768]{2,1,0:T(8,128)(2,1)S(1)}, u32[]{:S(2)}, u32[]{:S(2)}) collective-permute-start(bf16[4,64,768]{2,1,0:T(8,128)(2,1)S(1)} %copy-done.29), channel_id=1, source_target_pairs={{0,4},{4,0},{1,5},{5,1},{2,6},{6,2},{3,7},{7,3},{8,12},{12,8},{9,1... | collective-permute-start | bytes 1179656 | tf_op jit(solution)/shard_map/qkv_weight_grad/ppermute | solution.py:1202
  239.1 14.5 %all-to-all-start.6 = ((bf16[8,32,576]{2,1,0:T(8,128)(2,1)}), bf16[8,32,576]{2,1,0:T(8,128)(2,1)S(1)}, u32[]{:S(2)}, u32[]{:S(2)}) async-start(bf16[8,32,576]{2,1,0:T(8,128)(2,1)} %maximum_maximum_fusion.refs_1_), calls=%async_computation.7 | async-start | bytes 655360 | tf_op jit(solution)/shard_map/qkv_weight_grad/all_to_all | solution.py:1223
  244.4 16.8 %collective-permute-start.17 = (bf16[2,64,768]{2,1,0:T(8,128)(2,1)}, bf16[2,64,768]{2,1,0:T(8,128)(2,1)S(1)}, u32[]{:S(2)}, u32[]{:S(2)}) collective-permute-start(bf16[2,64,768]{2,1,0:T(8,128)(2,1)} %hold.20), channel_id=1, source_target_pairs={{0,8},{8,0},{1,9},{9,1},{2,10},{10,2},{3,11},{11,3},{4,12},{12,4},... | collective-permute-start | bytes 589832 | tf_op jit(solution)/shard_map/input_grad/ppermute | solution.py:1218
  247.2 14.0 %copy-start.2 = (f32[2,64,768]{2,1,0:T(8,128)S(1)}, f32[2,64,768]{2,1,0:T(8,128)}, u32[]{:S(2)}) copy-start(f32[2,64,768]{2,1,0:T(8,128)} %hold.19) | copy-start | bytes 1179652
  253.5 0.7 copy-start
  257.0 14.2 %all-to-all-start.7 = ((bf16[8,24,1280]{2,1,0:T(8,128)(2,1)}), bf16[8,24,1280]{2,1,0:T(8,128)(2,1)S(1)}, u32[]{:S(2)}, u32[]{:S(2)}) async-start(bf16[8,24,1280]{2,1,0:T(8,128)(2,1)} %bitcast.60.refs_1_), calls=%async_computation.8 | async-start | bytes 983040 | tf_op jit(solution)/shard_map/ff_weight_grads/all_to_all | solution.py:1258
  261.9 9.3 %collective-permute-start.19 = (bf16[96,384]{1,0:T(8,128)(2,1)S(1)}, bf16[96,384]{1,0:T(8,128)(2,1)S(1)}, u32[]{:S(2)}, u32[]{:S(2)}) collective-permute-start(bf16[96,384]{1,0:T(8,128)(2,1)S(1)} %get-tuple-element.120), channel_id=1, source_target_pairs={{0,1},{1,0},{2,3},{3,2},{4,5},{5,4},{6,7},{7,6},{8,9},{9,8},{10,11... | collective-permute-start | bytes 221192 | tf_op jit(solution)/shard_map/ff_weight_grads/ppermute | solution.py:1262
  262.3 8.0 %collective-permute-start.18 = (bf16[64,768]{1,0:T(8,128)(2,1)}, bf16[64,768]{1,0:T(8,128)(2,1)S(1)}, u32[]{:S(2)}, u32[]{:S(2)}) collective-permute-start(bf16[64,768]{1,0:T(8,128)(2,1)} %hold.21), channel_id=1, source_target_pairs={{0,16},{16,0},{1,17},{17,1},{2,18},{18,2},{3,19},{19,3},{4,20},{20... | collective-permute-start | bytes 294920 | tf_op jit(solution)/shard_map/qkv_weight_grad/ppermute | solution.py:1224
  262.3 8.1 %copy-start.12 = (f32[128,768]{1,0:T(8,128)S(1)}, f32[128,768]{1,0:T(8,128)}, u32[]{:S(2)}) copy-start(f32[128,768]{1,0:T(8,128)} %get-tuple-element.87) | copy-start | bytes 1179652
  271.2 0.6 copy-start.16
  271.2 0.8 copy-start.6
Sparse Core Ops, SparseCore 0:
  39.6 54.9 all-gather.2
  194.2 50.0 reduce-scatter.1

commit v3 on v2

--- a/solution.py
+++ b/solution.py
@@ -618,13 +618,8 @@
     )(core, parts, second_grad, normal, scale, vectors, own, swap, sums, mixed, earlier)
 
 
-def input_back_kernel(
-    place_ref, dq_ref, own_ref, c_ref, y_ref, weight_ref, keep_ref, give_ref, grad_ref
-):
-    kv_grad = own_ref[...].astype(F32) + c_ref[...].astype(F32) + y_ref[...].astype(F32)
-    grads = jnp.concatenate([dq_ref[...], kv_grad.astype(BF16)], axis=1)
-    grad_ref[...] = grads
-    inputs = nt(grads, weight_ref[...]).astype(BF16)
+def input_back_kernel(place_ref, grad_ref, weight_ref, keep_ref, give_ref):
+    inputs = nt(grad_ref[...], weight_ref[...]).astype(BF16)
     pairs, count = keep_ref.shape[0], keep_ref.shape[1]
     own_first = place_ref[2] == 0
     for pair in range(pairs):
@@ -634,8 +629,8 @@
         give_ref[pair] = jnp.where(own_first, second, first)
 
 
-def input_back(place, query_grads, own, from_c, from_y, weight):
-    tokens = query_grads.shape[0]
+def input_back(place, grads, weight):
+    tokens = grads.shape[0]
     width, cols = weight.shape
     vmem = pl.BlockSpec(memory_space=pltpu.VMEM)
     return pl.pallas_call(
@@ -643,20 +638,32 @@
         out_shape=(
             jax.ShapeDtypeStruct((4, tokens // 8, width), BF16),
             jax.ShapeDtypeStruct((4, tokens // 8, width), BF16),
-            jax.ShapeDtypeStruct((tokens, cols), BF16),
-        ),
-        in_specs=[pl.BlockSpec(memory_space=pltpu.SMEM)] + [vmem] * 5,
-        out_specs=(vmem,) * 3,
+        ),
+        in_specs=[pl.BlockSpec(memory_space=pltpu.SMEM)] + [vmem] * 2,
+        out_specs=(vmem,) * 2,
         compiler_params=pltpu.CompilerParams(vmem_limit_bytes=VMEM_BYTES),
         cost_estimate=pl.CostEstimate(
             flops=10 * tokens * width * cols, bytes_accessed=4 * tokens * width, transcendentals=0
         ),
         name="input_back",
-    )(place, query_grads, own, from_c, from_y, weight)
-
-
-def qkv_weight_kernel(place_ref, chunk_ref, grad_ref, shift_ref, keep_ref, give_ref):
-    grads = grad_ref[...]
+    )(place, grads, weight)
+
+
+def qkv_weight_kernel(
+    place_ref,
+    dq_ref,
+    own_ref,
+    c_ref,
+    y_ref,
+    chunk_ref,
+    shift_ref,
+    keep_ref,
+    give_ref,
+    grad_ref,
+):
+    kv_grad = own_ref[...].astype(F32) + c_ref[...].astype(F32) + y_ref[...].astype(F32)
+    grads = jnp.concatenate([dq_ref[...], kv_grad.astype(BF16)], axis=1)
+    grad_ref[...] = grads
     weights = tn(chunk_ref[...], grads)
     cols = weights.shape[1]
     owners, shifts = shift_ref.shape
@@ -685,22 +692,23 @@
         give_ref[y_side] = jnp.where(own_first, blocks[1], blocks[0])
 
 
-def qkv_weight(place, chunk, grads, shifts):
+def qkv_weight(place, query_grads, own, from_c, from_y, chunk, shifts):
     tokens, width = chunk.shape
-    cols = grads.shape[1]
+    cols = query_grads.shape[1] + own.shape[1]
     rows = width // 4 + shifts.shape[0] + 8
     vmem = pl.BlockSpec(memory_space=pltpu.VMEM)
     return pl.pallas_call(
         qkv_weight_kernel,
-        out_shape=(jax.ShapeDtypeStruct((2, rows, cols), BF16),) * 2,
-        in_specs=[pl.BlockSpec(memory_space=pltpu.SMEM)] + [vmem] * 3,
-        out_specs=(vmem,) * 2,
+        out_shape=(jax.ShapeDtypeStruct((2, rows, cols), BF16),) * 2
+        + (jax.ShapeDtypeStruct((tokens, cols), BF16),),
+        in_specs=[pl.BlockSpec(memory_space=pltpu.SMEM)] + [vmem] * 6,
+        out_specs=(vmem,) * 3,
         compiler_params=pltpu.CompilerParams(vmem_limit_bytes=VMEM_BYTES),
         cost_estimate=pl.CostEstimate(
             flops=14 * tokens * width * cols, bytes_accessed=4 * tokens * width, transcendentals=0
         ),
         name="qkv_weight",
-    )(place, chunk, grads, shifts)
+    )(place, query_grads, own, from_c, from_y, chunk, shifts)
 
 
 def spread_kernel(ring, in_ref, attn_ref, out_ref):
@@ -754,7 +762,8 @@
             jnp.zeros((6, width), F32),
         ]
     )
-    sums_ref[...] = pltpu.roll(sums, width - first_ref[0], 1)[:2, :shard]
+    turn = jnp.where(first_ref[0] == 0, 0, width - first_ref[0])
+    sums_ref[...] = pltpu.roll(sums, turn, 1)[:2, :shard]
     shift_ref[...] = sum(total[shard + 1 : shard + 2, :shifts] for total in totals)
 
 
@@ -1186,18 +1195,18 @@
             ).astype(BF16)
             from_c = from_y = jnp.zeros_like(own_part)
 
-    with jax.named_scope("input_back"):
-        spot = jnp.stack([c_at, y_at, x_at]).astype(jnp.int32)
-        input_keep, input_give, qkv_grad = input_back(
-            spot, query_grads, own_part, from_c, from_y, qkv_slice
-        )
+    spot = jnp.stack([c_at, y_at, x_at]).astype(jnp.int32)
     with jax.named_scope("qkv_weight_grad"):
-        keep, give = qkv_weight(
+        keep, give, qkv_grad = qkv_weight(
             spot,
+            query_grads,
+            own_part,
+            from_c,
+            from_y,
             chunk,
-            qkv_grad,
             grad_in_shift.reshape(seq_size, 2 * ff_shard),
         )
+        input_keep, input_give = input_back(spot, qkv_grad, qkv_slice)
         bundle = swap_sum(keep, give, "c").astype(BF16)
         from_x = lax.ppermute(input_give, "x", SWAP)
         parts = (hold(input_keep, bundle).astype(F32) + from_x.astype(F32)).reshape(

time: 283 us -> 280 us (0.989)
    ppermute x1, waiting for transfers between devices: 0.01 us -> 3.11 us  [body(): from_x = lax.ppermute(input_give, 'x', SWAP)]
    ppermute x5, waiting for transfers between devices: 7.8 us -> 4.7 us  [swap_sum(): lax.ppermute(give.astype(BF16), axis, SWAP).astype(F32)]
    unnamed x68 -> x66, local copies, waits for them, and re-layouts: 9.06 us -> 9.13 us
  transfers between devices with their start and end apart: 28 -> 28, of which waited for: 13 -> 14; matrix products, arithmetic and copies ran while one was open for 10% -> 10% of each run, Pallas kernels for 17% -> 18%
where the time goes in v3:
time: 280 us; the launch traced here: 278 us
  Pallas kernels  70.6 us (25%)
  blocking collectives  67.6 us (24%)
  waiting for transfers between devices  46.1 us (16%)
  starting transfers between devices  37.6 us (13%)
  local copies, waits for them, and re-layouts  24.1 us (9%)
  between operations  15.4 us (6%)
  other arithmetic  14.1 us (5%)
    all_gather x2, blocking collectives, gather_plane(): return lax.all_gather(block, PLANE, axis=0, tiled=True)  25.5 us
    all_to_all x1, blocking collectives, body(): lax.all_to_all(attended_low.reshape(8, row_count, GROUP_WIDTH), SEQ_GROUP...  17.1 us
    all_to_all x1, blocking collectives, spread_plane(): lax.all_to_all(parts.reshape(4, -1, parts.shape[1]), PLANE, 0, 0, tiled=T...  15.1 us
    pallas_call x2, Pallas kernels, attend_back(): pl.pallas_call(functools.partial(attend_back_kernel, len(earlier), count,...  14.6 us
    pallas_call x3, Pallas kernels, attend(): pl.pallas_call(functools.partial(attend_kernel, len(earlier), count, firs...  13.1 us
    all_gather x1, blocking collectives, body(): parcels = lax.all_gather(hold(parcel, chunk), CHUNKS, axis=0, tiled=False)  9.83 us
    unnamed x66, local copies, waits for them, and re-layouts  9.13 us
    pallas_call x1, Pallas kernels, ff_backward(): pl.pallas_call(functools.partial(ff_backward_kernel, units, out_columns),...  7.26 us
  transfers between devices with their start and end apart: 28, of which 14 were waited for; matrix products, arithmetic and copies ran while one was open for 10% of the time, Pallas kernels for 18%

profile of v3, /device:TPU:0, one launch (start us, length us, event | category | flops | bytes accessed | tf_op | source)
XLA Modules:
  0.0 278.0 jit_solution(10011922960304480040)
XLA Ops:
  7.2 1.0 constant_dynamic-slice_fusion.9
  8.2 4.1 %collective-permute-start = (bf16[64,768]{1,0:T(8,128)(2,1)S(1)}, bf16[64,768]{1,0:T(8,128)(2,1)S(1)}, u32[]{:S(2)}, u32[]{:S(2)}) collective-permute-start(bf16[64,768]{1,0:T(8,128)(2,1)S(1)} %get-tuple-element.119), channel_id=1, source_target_pairs={{0,16},{16,0},{1,17},{17,1},{2,18},{18,2},{3,19},{19,3},{4,20},{20... | collective-permute-start | bytes 294920 | tf_op jit(solution)/shard_map/gather_tokens/ppermute | solution.py:998
  12.3 0.9 reshape.252
  13.8 1.9 spread.1
  15.6 3.8 %all-to-all-start = ((bf16[8,24,1152]{2,1,0:T(8,128)(2,1)}), bf16[8,24,1152]{2,1,0:T(8,128)(2,1)S(1)}, u32[]{:S(2)}, u32[]{:S(2)}) async-start(bf16[8,24,1152]{2,1,0:T(8,128)(2,1)} %spread.1), calls=%async_computation | async-start | bytes 884736 | tf_op jit(solution)/shard_map/gather_ff_weights/all_to_all | solution.py:938
  20.5 1.6 collective-permute-start.1
  22.2 5.7 %collective-permute-done.1 = bf16[2,64,768]{2,1,0:T(8,128)(2,1)S(1)} collective-permute-done((bf16[2,64,768]{2,1,0:T(8,128)(2,1)S(1)}, bf16[2,64,768]{2,1,0:T(8,128)(2,1)S(1)}, u32[]{:S(2)}, u32[]{:S(2)}) %collective-permute-start.1) | collective-permute-done | bytes 196640 | tf_op jit(solution)/shard_map/gather_tokens/ppermute | solution.py:1000
  28.6 0.9 pad_maximum_fusion.1.refs_1_
  30.0 1.7 collective-permute-start.3
  33.2 3.4 %all-to-all-start.1 = ((bf16[8,24,640]{2,1,0:T(8,128)(2,1)}), bf16[8,24,640]{2,1,0:T(8,128)(2,1)S(1)}, u32[]{:S(2)}, u32[]{:S(2)}) async-start(bf16[8,24,640]{2,1,0:T(8,128)(2,1)} %bitcast.23), calls=%async_computation.1 | async-start | bytes 491520 | tf_op jit(solution)/shard_map/gather_qkv_weights/all_to_all | solution.py:993
  37.3 4.7 %collective-permute-done.3 = bf16[2,2,64,768]{3,2,1,0:T(8,128)(2,1)S(1)} collective-permute-done((bf16[2,2,64,768]{3,2,1,0:T(8,128)(2,1)}, bf16[2,2,64,768]{3,2,1,0:T(8,128)(2,1)S(1)}, u32[]{:S(2)}, u32[]{:S(2)}) %collective-permute-start.3) | collective-permute-done | bytes 393248 | tf_op jit(solution)/shard_map/gather_tokens/ppermute | solution.py:1002
  42.2 1.0 copy.66
  43.2 1.5 all-to-all-done.1.refs_0_
  45.5 9.8 %all-gather = bf16[32,24,640]{2,1,0:T(8,128)(2,1)S(1)} all-gather(bf16[8,24,640]{2,1,0:T(8,128)(2,1)} %hold.13), channel_id=2, replica_groups=mesh['s'=2,'e'=1,'r'=2,'x'=2,'y'=2,'c'=2] {'e','y','c'}, dimensions={0}, use_global_device_ids=true | all-gather | bytes 1228800 | tf_op jit(solution)/shard_map/gather_qkv_weights/all_gather | solution.py:1006
  56.5 1.4 fusion.refs_0_.refs_1_
  61.3 1.1 fusion.1.q_ref
  62.4 5.4 %attend.3 = (f32[192,512]{1,0:T(8,128)}, f32[6,512]{1,0:T(8,128)}) custom-call(f32[3]{0:T(128)} %power_multiply_fusion.slopes_ref, bf16[512,192]{1,0:T(8,128)(2,1)} %fusion.1.q_ref, f32[1,512]{1,0:T(1,128)} %get-tuple-element.130.pq_ref.pk_ref, f32[2,512]{1,0:T(2,128)} %maximum_bitcast_fusion.1.pk_ref, bf16[512,384]{1,0:T(8,128)(2,1)} %fusion.refs_0_.refs_1_, ...), custom_call_target="tpu_custom_call" | custom-call | flops 6442450944 | bytes 524288 | tf_op jit(solution)/shard_map/attention/attend/pallas_call | solution.py:147
  67.8 1.9 collective-permute-done.4.refs_0_
  71.1 3.8 %attend.4 = (f32[192,512]{1,0:T(8,128)}, f32[6,512]{1,0:T(8,128)}) custom-call(f32[3]{0:T(128)} %power_multiply_fusion.slopes_ref, bf16[512,192]{1,0:T(8,128)(2,1)} %fusion.1.q_ref, f32[1,512]{1,0:T(1,128)} %get-tuple-element.130.pq_ref.pk_ref, f32[1,512]{1,0:T(1,128)} %get-tuple-element.127.pk_ref, f32[8,768]{1,0:T(8,128)} %convert_element_type.113.refs_0_.vec_ref, ...), custom_call_target="tpu_custom_call" | custom-call | flops 3221225472 | bytes 262144 | tf_op jit(solution)/shard_map/attention/attend/pallas_call | solution.py:147
  75.6 4.0 %attend.5 = (f32[192,512]{1,0:T(8,128)}, f32[3,512]{1,0:T(4,128)}, bf16[512,192]{1,0:T(8,128)(2,1)}) custom-call(f32[3]{0:T(128)} %power_multiply_fusion.slopes_ref, bf16[512,192]{1,0:T(8,128)(2,1)} %fusion.1.q_ref, f32[1,512]{1,0:T(1,128)} %get-tuple-element.130.pq_ref.pk_ref, f32[1,512]{1,0:T(1,128)} %get-tuple-element.129.pk_ref, ...), custom_call_target="tpu_custom_call" | custom-call | flops 3221225472 | bytes 262144 | tf_op jit(solution)/shard_map/attention/attend/pallas_call | solution.py:147
  79.6 17.1 %all_to_all.40.refs_1_.mixed_ref = bf16[8,64,192]{2,1,0:T(8,128)(2,1)} all-to-all(bf16[8,64,192]{2,1,0:T(8,128)(2,1)} %bitcast.144), channel_id=1, replica_groups=mesh['s'=2,'e'=1,'r'=2,'x'=2,'y'=2,'c'=2] {'s','r','x'}, dimensions={0} | all-to-all | bytes 393216 | tf_op jit(solution)/shard_map/return_attended/all_to_all | solution.py:1090
  96.7 1.1 slice.120.own_ref
  98.0 2.0 collective-permute-done.7.swap_ref
  100.8 3.0 %first_norm.1 = (bf16[128,768]{1,0:T(8,128)(2,1)}, f32[128,768]{1,0:T(8,128)}, f32[128,768]{1,0:T(8,128)}, f32[128,1]{1,0:T(8,128)}) custom-call(s32[1]{0:T(128)} %bitcast.core_ref, bf16[8,64,192]{2,1,0:T(8,128)(2,1)} %all_to_all.40.refs_1_.mixed_ref, bf16[128,768]{1,0:T(8,128)(2,1)} %bitcast.145, f32[8,768]{1,0:T(8,128)} %convert_element_type.113.refs_0_.vec_ref, ...), custom_call_target="tpu_custom_call" | custom-call | flops 4831838208 | bytes 2359296 | tf_op jit(solution)/shard_map/first_norm/first_norm/pallas_call | solution.py:330
  104.7 13.3 %all_gather.18.hidden_ref = bf16[512,768]{1,0:T(8,128)(2,1)} all-gather(bf16[128,768]{1,0:T(8,128)(2,1)S(1)} %copy-done.9), channel_id=1, replica_groups=mesh['s'=2,'e'=1,'r'=2,'x'=2,'y'=2,'c'=2] {'x','y'}, dimensions={0}, use_global_device_ids=true | all-gather | bytes 983040 | tf_op jit(solution)/shard_map/gather_hidden/all_gather | solution.py:852
  118.1 1.4 copy-done.26
  119.5 6.9 %ff_forward.1 = (bf16[512,768]{1,0:T(8,128)(2,1)}, bf16[512,768]{1,0:T(8,128)(2,1)}, bf16[512,768]{1,0:T(8,128)(2,1)}, bf16[512,768]{1,0:T(8,128)(2,1)}) custom-call(s32[1]{0:T(128)} %bitcast.core_ref, bf16[512,768]{1,0:T(8,128)(2,1)} %all_gather.18.hidden_ref, f32[2,768]{1,0:T(2,128)} %reshape.279.refs_1_.bias_ref, bf16[768,1536]{1,0:T(8,128)(2,1)} %hold.16.own_ref, ...), custom_call_target="tpu_custom_call" | custom-call | flops 9663676416 | bytes 3538944 | tf_op jit(solution)/shard_map/ff_forward/ff_forward/pallas_call | solution.py:382
  126.4 15.1 %all_to_all.41.parts_ref = bf16[4,128,768]{2,1,0:T(8,128)(2,1)} all-to-all(bf16[4,128,768]{2,1,0:T(8,128)(2,1)} %bitcast.135), channel_id=1, replica_groups=mesh['s'=2,'e'=1,'r'=2,'x'=2,'y'=2,'c'=2] {'x','y'}, dimensions={0} | all-to-all | bytes 1572864 | tf_op jit(solution)/shard_map/sum_ff/all_to_all | solution.py:856
  141.5 2.5 second_norm.1
  144.0 12.2 %all_gather.19.grad_ref = bf16[512,768]{1,0:T(8,128)(2,1)} all-gather(bf16[128,768]{1,0:T(8,128)(2,1)} %get-tuple-element.75), channel_id=1, replica_groups=mesh['s'=2,'e'=1,'r'=2,'x'=2,'y'=2,'c'=2] {'x','y'}, dimensions={0}, use_global_device_ids=true | all-gather | bytes 983040 | tf_op jit(solution)/shard_map/gather_ff_grad/all_gather | solution.py:852
  156.2 7.3 %ff_backward.1 = (bf16[2,512,768]{2,1,0:T(8,128)(2,1)}, bf16[512,768]{1,0:T(8,128)(2,1)}, f32[2,768]{1,0:T(2,128)}, bf16[2,512,384]{2,1,0:T(8,128)(2,1)}) custom-call(s32[1]{0:T(128)} %bitcast.core_ref, bf16[512,768]{1,0:T(8,128)(2,1)} %all_gather.19.grad_ref, bf16[512,768]{1,0:T(8,128)(2,1)} %get-tuple-element.76.slope_ref, ...), custom_call_target="tpu_custom_call" | custom-call | flops 9663676416 | bytes 3538944 | tf_op jit(solution)/shard_map/ff_backward/ff_backward/pallas_call | solution.py:491
  163.5 3.5 %all-to-all-start.4 = ((bf16[4,128,768]{2,1,0:T(8,128)(2,1)}), bf16[4,128,768]{2,1,0:T(8,128)(2,1)S(1)}, u32[]{:S(2)}, u32[]{:S(2)}) async-start(bf16[4,128,768]{2,1,0:T(8,128)(2,1)} %bitcast.134), calls=%async_computation.4 | async-start | bytes 1572864 | tf_op jit(solution)/shard_map/sum_hidden_grad/all_to_all | solution.py:856
  167.0 6.3 %ff_grads.1 = (bf16[768,1152]{1,0:T(8,128)(2,1)}, bf16[768,1152]{1,0:T(8,128)(2,1)}) custom-call(s32[1]{0:T(128)} %bitcast.core_ref, bf16[512,768]{1,0:T(8,128)(2,1)} %get-tuple-element.83.act_ref, bf16[2,512,384]{2,1,0:T(8,128)(2,1)} %get-tuple-element.84.half_ref, bf16[512,768]{1,0:T(8,128)(2,1)} %all_gather.18.hidden_ref, ...), custom_call_target="tpu_custom_call" | custom-call | flops 6000000000 | bytes 10000 | tf_op jit(solution)/shard_map/ff_weight_grads/ff_grads/pallas_call | solution.py:532
  173.3 1.7 all-to-all-done.4.parts_ref
  175.0 0.9 copy-done.10
  175.9 4.1 %first_back.1 = (f32[128,768]{1,0:T(8,128)}, bf16[8,64,192]{2,1,0:T(8,128)(2,1)}, bf16[768,512]{1,0:T(8,128)(2,1)}, bf16[768,512]{1,0:T(8,128)(2,1)}) custom-call(s32[1]{0:T(128)} %bitcast.core_ref, bf16[4,128,768]{2,1,0:T(8,128)(2,1)} %copy-done.10, f32[128,768]{1,0:T(8,128)} %get-tuple-element.79.second_ref, f32[128,768]{1,0:T(8,128)} %get-tuple-element.80.normal_ref, ...), custom_call_target="tpu_custom_call" | custom-call | flops 4831838208 | bytes 2359296 | tf_op jit(solution)/shard_map/first_norm_back/first_back/pallas_call | solution.py:601
  180.0 4.2 %all-to-all-start.5 = ((bf16[8,64,192]{2,1,0:T(8,128)(2,1)}), bf16[8,64,192]{2,1,0:T(8,128)(2,1)}, u32[]{:S(2)}, u32[]{:S(2)}) async-start(bf16[8,64,192]{2,1,0:T(8,128)(2,1)} %get-tuple-element.88), calls=%async_computation.5 | async-start | bytes 524288 | tf_op jit(solution)/shard_map/send_out_grad/all_to_all | solution.py:1150
  184.3 1.6 add_convert_fusion.1
  186.3 1.6 pad_maximum_fusion.refs_0_
  187.9 6.0 %all-to-all-done.5 = bf16[8,64,192]{2,1,0:T(8,128)(2,1)} async-done(((bf16[8,64,192]{2,1,0:T(8,128)(2,1)}), bf16[8,64,192]{2,1,0:T(8,128)(2,1)}, u32[]{:S(2)}, u32[]{:S(2)}) %all-to-all-start.5) | async-done | bytes 196640 | tf_op jit(solution)/shard_map/send_out_grad/all_to_all | solution.py:1150
  194.6 9.7 %attend_back.2 = (f32[192,512]{1,0:T(8,128)}, bf16[512,384]{1,0:T(8,128)(2,1)}, bf16[512,384]{1,0:T(8,128)(2,1)}, bf16[512,384]{1,0:T(8,128)(2,1)}) custom-call(f32[3]{0:T(128)} %power_multiply_fusion.slopes_ref, bf16[512,192]{1,0:T(8,128)(2,1)} %fusion.1.q_ref, f32[1,512]{1,0:T(1,128)} %get-tuple-element.130.pq_ref.pk_ref, ...), custom_call_target="tpu_custom_call" | custom-call | flops 12683575296 | bytes 786432 | tf_op jit(solution)/shard_map/attention_back/attend_back/pallas_call | solution.py:240
  206.2 1.1 add_convert_fusion.3.refs_0_
  207.3 1.5 collective-permute-start.13
  208.8 4.9 %attend_back.3 = (bf16[512,192]{1,0:T(8,128)(2,1)}, bf16[512,384]{1,0:T(8,128)(2,1)}) custom-call(f32[3]{0:T(128)} %power_multiply_fusion.slopes_ref, bf16[512,192]{1,0:T(8,128)(2,1)} %fusion.1.q_ref, f32[1,512]{1,0:T(1,128)} %get-tuple-element.130.pq_ref.pk_ref, f32[1,512]{1,0:T(1,128)} %get-tuple-element.130.pq_ref.pk_ref, ...), custom_call_target="tpu_custom_call" | custom-call | flops 4227858432 | bytes 262144 | tf_op jit(solution)/shard_map/attention_back/attend_back/pallas_call | solution.py:240
  213.7 4.8 %collective-permute-done.13.y_ref = bf16[512,384]{1,0:T(8,128)(2,1)S(1)} collective-permute-done((bf16[512,384]{1,0:T(8,128)(2,1)S(1)}, bf16[512,384]{1,0:T(8,128)(2,1)S(1)}, u32[]{:S(2)}, u32[]{:S(2)}) %collective-permute-start.13) | collective-permute-done | bytes 393248 | tf_op jit(solution)/shard_map/sum_kv_grads/ppermute | solution.py:1190
  219.3 3.8 %qkv_weight.1 = (bf16[2,208,576]{2,1,0:T(8,128)(2,1)}, bf16[2,208,576]{2,1,0:T(8,128)(2,1)}, bf16[512,576]{1,0:T(8,128)(2,1)}) custom-call(s32[3]{0:T(128)} %pad_add_fusion.place_ref, bf16[512,192]{1,0:T(8,128)(2,1)} %get-tuple-element.97.dq_ref, bf16[512,384]{1,0:T(8,128)(2,1)} %get-tuple-element.98.own_ref, bf16[512,384]{1,0:T(8,128)(2,1)} %copy-done.29, ...), custom_call_target="tpu_custom_call" | custom-call | flops 3170893824 | bytes 1572864 | tf_op jit(solution)/shard_map/qkv_weight_grad/qkv_weight/pallas_call | solution.py:700
  223.1 2.1 collective-permute-done.14
  225.2 1.2 add_convert_fusion.2.refs_1_
  226.4 1.5 collective-permute-start.16
  228.0 3.1 %input_back.1 = (bf16[4,64,768]{2,1,0:T(8,128)(2,1)}, bf16[4,64,768]{2,1,0:T(8,128)(2,1)}) custom-call(s32[3]{0:T(128)} %pad_add_fusion.place_ref, bf16[512,576]{1,0:T(8,128)(2,1)} %get-tuple-element.101.grad_ref, bf16[768,576]{1,0:T(8,128)(2,1)} %bitcast.131), custom_call_target="tpu_custom_call" | custom-call | flops 2264924160 | bytes 1572864 | tf_op jit(solution)/shard_map/qkv_weight_grad/input_back/pallas_call | solution.py:636
  231.1 1.4 collective-permute-start.15
  232.5 2.4 collective-permute-done.16
  235.1 0.8 maximum_maximum_fusion.refs_1_
  236.0 3.6 %all-to-all-start.6 = ((bf16[8,32,576]{2,1,0:T(8,128)(2,1)}), bf16[8,32,576]{2,1,0:T(8,128)(2,1)S(1)}, u32[]{:S(2)}, u32[]{:S(2)}) async-start(bf16[8,32,576]{2,1,0:T(8,128)(2,1)} %maximum_maximum_fusion.refs_1_), calls=%async_computation.7 | async-start | bytes 655360 | tf_op jit(solution)/shard_map/qkv_weight_grad/all_to_all | solution.py:1232
  239.5 3.1 %collective-permute-done.15 = bf16[4,64,768]{2,1,0:T(8,128)(2,1)S(1)} collective-permute-done((bf16[4,64,768]{2,1,0:T(8,128)(2,1)}, bf16[4,64,768]{2,1,0:T(8,128)(2,1)S(1)}, u32[]{:S(2)}, u32[]{:S(2)}) %collective-permute-start.15) | collective-permute-done | bytes 393248 | tf_op jit(solution)/shard_map/qkv_weight_grad/ppermute | solution.py:1211
  242.6 1.1 convert_add_fusion
  244.4 0.9 collective-permute-start.17
  246.1 4.4 %all-to-all-done.6.refs_1_.refs_0_ = bf16[8,32,576]{2,1,0:T(8,128)(2,1)S(1)} async-done(((bf16[8,32,576]{2,1,0:T(8,128)(2,1)}), bf16[8,32,576]{2,1,0:T(8,128)(2,1)S(1)}, u32[]{:S(2)}, u32[]{:S(2)}) %all-to-all-start.6) | async-done | bytes 294944 | tf_op jit(solution)/shard_map/qkv_weight_grad/all_to_all | solution.py:1232
  251.3 1.8 slice.124
  253.1 0.9 slice.125
  254.0 3.5 %all-to-all-start.7 = ((bf16[8,24,1280]{2,1,0:T(8,128)(2,1)}), bf16[8,24,1280]{2,1,0:T(8,128)(2,1)S(1)}, u32[]{:S(2)}, u32[]{:S(2)}) async-start(bf16[8,24,1280]{2,1,0:T(8,128)(2,1)} %bitcast.60.refs_1_), calls=%async_computation.8 | async-start | bytes 983040 | tf_op jit(solution)/shard_map/ff_weight_grads/all_to_all | solution.py:1267
  260.0 1.9 share.1
  261.9 5.5 %collective-permute-done.18 = bf16[64,768]{1,0:T(8,128)(2,1)S(1)} collective-permute-done((bf16[64,768]{1,0:T(8,128)(2,1)}, bf16[64,768]{1,0:T(8,128)(2,1)S(1)}, u32[]{:S(2)}, u32[]{:S(2)}) %collective-permute-start.18) | collective-permute-done | bytes 98336 | tf_op jit(solution)/shard_map/qkv_weight_grad/ppermute | solution.py:1233
  269.0 2.1 unpack.1
  (171 shorter events, 24.0 us)
Async XLA Ops:
  7.2 12.3 %copy-start.18 = (s32[2,256]{1,0:T(2,128)S(1)}, s32[2,256]{1,0:T(2,128)}, u32[]{:S(2)}) copy-start(s32[2,256]{1,0:T(2,128)} %param.16) | copy-start | bytes 6148
  7.2 12.4 %copy-start.31 = (bf16[192]{0:T(256)(128)(2,1)S(1)}, bf16[192]{0:T(256)(128)(2,1)}, u32[]{:S(2)}) copy-start(bf16[192]{0:T(256)(128)(2,1)} %param.24) | copy-start | bytes 1156
  7.2 12.5 %copy-start.15 = (bf16[24,2304]{1,0:T(8,128)(2,1)S(1)}, bf16[24,2304]{1,0:T(8,128)(2,1)}, u32[]{:S(2)}) copy-start(bf16[24,2304]{1,0:T(8,128)(2,1)} %param.17) | copy-start | bytes 331780
  8.2 12.2 %collective-permute-start = (bf16[64,768]{1,0:T(8,128)(2,1)S(1)}, bf16[64,768]{1,0:T(8,128)(2,1)S(1)}, u32[]{:S(2)}, u32[]{:S(2)}) collective-permute-start(bf16[64,768]{1,0:T(8,128)(2,1)S(1)} %get-tuple-element.119), channel_id=1, source_target_pairs={{0,16},{16,0},{1,17},{17,1},{2,18},{18,2},{3,19},{19,3},{4,20},{20... | collective-permute-start | bytes 294920 | tf_op jit(solution)/shard_map/gather_tokens/ppermute | solution.py:998
  13.3 6.8 %copy-start.19 = (bf16[2,24]{1,0:T(2,128)(2,1)S(1)}, bf16[2,24]{1,0:T(2,128)(2,1)}, u32[]{:S(2)}) copy-start(bf16[2,24]{1,0:T(2,128)(2,1)} %param.18) | copy-start | bytes 292
  13.3 6.8 %copy-start.20 = (bf16[24]{0:T(256)(128)(2,1)S(1)}, bf16[24]{0:T(256)(128)(2,1)}, u32[]{:S(2)}) copy-start(bf16[24]{0:T(256)(128)(2,1)} %param.20) | copy-start | bytes 148
  13.3 6.8 %copy-start.21 = (bf16[24]{0:T(256)(128)(2,1)S(1)}, bf16[24]{0:T(256)(128)(2,1)}, u32[]{:S(2)}) copy-start(bf16[24]{0:T(256)(128)(2,1)} %param.21) | copy-start | bytes 148
  13.3 6.8 %copy-start.22 = (bf16[24]{0:T(256)(128)(2,1)S(1)}, bf16[24]{0:T(256)(128)(2,1)}, u32[]{:S(2)}) copy-start(bf16[24]{0:T(256)(128)(2,1)} %param.22) | copy-start | bytes 148
  13.3 6.8 %copy-start.23 = (bf16[24]{0:T(256)(128)(2,1)S(1)}, bf16[24]{0:T(256)(128)(2,1)}, u32[]{:S(2)}) copy-start(bf16[24]{0:T(256)(128)(2,1)} %param.26) | copy-start | bytes 148
  13.3 6.8 %copy-start.24 = (bf16[24]{0:T(256)(128)(2,1)S(1)}, bf16[24]{0:T(256)(128)(2,1)}, u32[]{:S(2)}) copy-start(bf16[24]{0:T(256)(128)(2,1)} %param.27) | copy-start | bytes 148
  13.3 6.8 %copy-start.25 = (bf16[24]{0:T(256)(128)(2,1)S(1)}, bf16[24]{0:T(256)(128)(2,1)}, u32[]{:S(2)}) copy-start(bf16[24]{0:T(256)(128)(2,1)} %param.28) | copy-start | bytes 148
  13.7 8.4 %collective-permute-start.2 = (bf16[96,384]{1,0:T(8,128)(2,1)S(1)}, bf16[96,384]{1,0:T(8,128)(2,1)S(1)}, u32[]{:S(2)}, u32[]{:S(2)}) collective-permute-start(bf16[96,384]{1,0:T(8,128)(2,1)S(1)} %bitcast.147), channel_id=1, source_target_pairs={{0,1},{1,0},{2,3},{3,2},{4,5},{5,4},{6,7},{7,6},{8,9},{9,8},{10,11... | collective-permute-start | bytes 221192 | tf_op jit(solution)/shard_map/gather_ff_weights/ppermute | solution.py:943
  15.6 13.0 %all-to-all-start = ((bf16[8,24,1152]{2,1,0:T(8,128)(2,1)}), bf16[8,24,1152]{2,1,0:T(8,128)(2,1)S(1)}, u32[]{:S(2)}, u32[]{:S(2)}) async-start(bf16[8,24,1152]{2,1,0:T(8,128)(2,1)} %spread.1), calls=%async_computation | async-start | bytes 884736 | tf_op jit(solution)/shard_map/gather_ff_weights/all_to_all | solution.py:938
  20.5 7.4 %collective-permute-start.1 = (bf16[2,64,768]{2,1,0:T(8,128)(2,1)S(1)}, bf16[2,64,768]{2,1,0:T(8,128)(2,1)S(1)}, u32[]{:S(2)}, u32[]{:S(2)}) collective-permute-start(bf16[2,64,768]{2,1,0:T(8,128)(2,1)S(1)} %maximum_select_fusion.4), channel_id=1, source_target_pairs={{0,8},{8,0},{1,9},{9,1},{2,10},{10,2},{3,11},{11,3},{4,12},{12,4},... | collective-permute-start | bytes 589832 | tf_op jit(solution)/shard_map/gather_tokens/ppermute | solution.py:1000
  30.0 12.0 %copy-start.3 = (bf16[2,2,64,768]{3,2,1,0:T(8,128)(2,1)S(1)}, bf16[2,2,64,768]{3,2,1,0:T(8,128)(2,1)}, u32[]{:S(2)}) copy-start(bf16[2,2,64,768]{3,2,1,0:T(8,128)(2,1)} %hold.12) | copy-start | bytes 1179652
  30.0 12.0 %collective-permute-start.3 = (bf16[2,2,64,768]{3,2,1,0:T(8,128)(2,1)}, bf16[2,2,64,768]{3,2,1,0:T(8,128)(2,1)S(1)}, u32[]{:S(2)}, u32[]{:S(2)}) collective-permute-start(bf16[2,2,64,768]{3,2,1,0:T(8,128)(2,1)} %hold.12), channel_id=1, source_target_pairs={{0,4},{4,0},{1,5},{5,1},{2,6},{6,2},{3,7},{7,3},{8,12},{12,8},{9,1... | collective-permute-start | bytes 1179656 | tf_op jit(solution)/shard_map/gather_tokens/ppermute | solution.py:1002
  33.2 11.6 %all-to-all-start.1 = ((bf16[8,24,640]{2,1,0:T(8,128)(2,1)}), bf16[8,24,640]{2,1,0:T(8,128)(2,1)S(1)}, u32[]{:S(2)}, u32[]{:S(2)}) async-start(bf16[8,24,640]{2,1,0:T(8,128)(2,1)} %bitcast.23), calls=%async_computation.1 | async-start | bytes 491520 | tf_op jit(solution)/shard_map/gather_qkv_weights/all_to_all | solution.py:993
  36.6 60.2 %all-gather.3.cloned.1.call-start = ((), (), s32[]{:S(2)}) async-start(), calls=%async_computation.9 | async-start | bytes 2949120 | tf_op jit(solution)/shard_map/gather_ff_weights/all_gather | solution.py:1031
  44.8 0.7 copy-start.5
  55.3 1.2 copy-start.4
  55.5 6.9 %copy-start.8 = (bf16[2,1,2,2,2,2,24,576]{7,6,5,4,3,2,0,1:T(8,128)(2,1)}, bf16[2,1,2,2,2,2,24,576]{7,6,5,4,3,2,0,1:T(8,128)(2,1)S(1)}, u32[]{:S(2)}) copy-start(bf16[2,1,2,2,2,2,24,576]{7,6,5,4,3,2,0,1:T(8,128)(2,1)S(1)} %copy.70) | copy-start | bytes 2654212
  57.9 4.5 %collective-permute-start.5 = (bf16[512,384]{1,0:T(8,128)(2,1)}, bf16[512,384]{1,0:T(8,128)(2,1)}, u32[]{:S(2)}, u32[]{:S(2)}) collective-permute-start(bf16[512,384]{1,0:T(8,128)(2,1)} %fusion.refs_0_.refs_1_), channel_id=1, source_target_pairs={{0,1},{1,0},{2,3},{3,2},{4,5},{5,4},{6,7},{7,6},{8,9},{9,8},{10,11... | collective-permute-start | bytes 1179656 | tf_op jit(solution)/shard_map/gather_kv/ppermute | solution.py:1051
  58.3 11.4 %collective-permute-start.4 = (bf16[512,384]{1,0:T(8,128)(2,1)}, bf16[512,384]{1,0:T(8,128)(2,1)S(1)}, u32[]{:S(2)}, u32[]{:S(2)}) collective-permute-start(bf16[512,384]{1,0:T(8,128)(2,1)} %fusion.refs_0_.refs_1_), channel_id=1, source_target_pairs={{0,2},{2,0},{1,3},{3,1},{4,6},{6,4},{5,7},{7,5},{8,10},{10,8},{9,1... | collective-permute-start | bytes 1179656 | tf_op jit(solution)/shard_map/gather_kv/ppermute | solution.py:1050
  69.7 0.7 copy-start.13
  70.4 4.5 %collective-permute-start.6 = (bf16[512,384]{1,0:T(8,128)(2,1)}, bf16[512,384]{1,0:T(8,128)(2,1)S(1)}, u32[]{:S(2)}, u32[]{:S(2)}) collective-permute-start(bf16[512,384]{1,0:T(8,128)(2,1)} %hold.14.refs_2_), channel_id=1, source_target_pairs={{0,1},{1,0},{2,3},{3,2},{4,5},{5,4},{6,7},{7,6},{8,9},{9,8},{10,11... | collective-permute-start | bytes 1179656 | tf_op jit(solution)/shard_map/attention/ppermute | solution.py:1086
  74.9 0.8 copy-start.28
  97.9 2.1 copy-start.11
  97.9 2.1 collective-permute-start.7
  99.9 0.8 copy-start.27
  103.8 0.9 copy-start.9
  103.8 14.3 %collective-permute-start.8 = (bf16[768,1536]{1,0:T(8,128)(2,1)}, bf16[768,1536]{1,0:T(8,128)(2,1)S(1)}, u32[]{:S(2)}, u32[]{:S(2)}) collective-permute-start(bf16[768,1536]{1,0:T(8,128)(2,1)} %hold.16.own_ref), channel_id=1, source_target_pairs={{0,1},{1,0},{2,3},{3,2},{4,5},{5,4},{6,7},{7,6},{8,9},{9,8},{10,11... | collective-permute-start | bytes 7077896 | tf_op jit(solution)/shard_map/first_norm/ppermute | solution.py:1106
  118.1 1.4 copy-start.26
  163.5 11.5 %all-to-all-start.4 = ((bf16[4,128,768]{2,1,0:T(8,128)(2,1)}), bf16[4,128,768]{2,1,0:T(8,128)(2,1)S(1)}, u32[]{:S(2)}, u32[]{:S(2)}) async-start(bf16[4,128,768]{2,1,0:T(8,128)(2,1)} %bitcast.134), calls=%async_computation.4 | async-start | bytes 1572864 | tf_op jit(solution)/shard_map/sum_hidden_grad/all_to_all | solution.py:856
  173.3 12.6 %collective-permute-start.10 = (bf16[768,1152]{1,0:T(8,128)(2,1)}, bf16[768,1152]{1,0:T(8,128)(2,1)S(1)}, u32[]{:S(2)}, u32[]{:S(2)}) collective-permute-start(bf16[768,1152]{1,0:T(8,128)(2,1)} %get-tuple-element.93), channel_id=1, source_target_pairs={{0,1},{1,0},{2,3},{3,2},{4,5},{5,4},{6,7},{7,6},{8,9},{9,8},{10,11... | collective-permute-start | bytes 5308424 | tf_op jit(solution)/shard_map/attn_weight_grad/ppermute | solution.py:848
  175.0 0.9 copy-start.10
  180.0 5.9 %copy-start.7 = (bf16[768,1152]{1,0:T(8,128)(2,1)S(1)}, bf16[768,1152]{1,0:T(8,128)(2,1)}, u32[]{:S(2)}) copy-start(bf16[768,1152]{1,0:T(8,128)(2,1)} %get-tuple-element.86._) | copy-start | bytes 5308420
  180.0 4.3 %collective-permute-start.9 = (bf16[768,512]{1,0:T(8,128)(2,1)}, bf16[768,512]{1,0:T(8,128)(2,1)}, u32[]{:S(2)}, u32[]{:S(2)}) collective-permute-start(bf16[768,512]{1,0:T(8,128)(2,1)} %get-tuple-element.92), channel_id=1, source_target_pairs={{0,1},{1,0},{2,3},{3,2},{4,5},{5,4},{6,7},{7,6},{8,9},{9,8},{10,11... | collective-permute-start | bytes 2359304 | tf_op jit(solution)/shard_map/attn_weight_grad/ppermute | solution.py:848
  180.0 13.9 %all-to-all-start.5 = ((bf16[8,64,192]{2,1,0:T(8,128)(2,1)}), bf16[8,64,192]{2,1,0:T(8,128)(2,1)}, u32[]{:S(2)}, u32[]{:S(2)}) async-start(bf16[8,64,192]{2,1,0:T(8,128)(2,1)} %get-tuple-element.88), calls=%async_computation.5 | async-start | bytes 524288 | tf_op jit(solution)/shard_map/send_out_grad/all_to_all | solution.py:1150
  184.2 60.2 %reduce-scatter.2.cloned.1.call-start = ((), (), s32[]{:S(2)}) async-start(), calls=%async_computation.10 | async-start | bytes 3194880 | tf_op jit(solution)/shard_map/attn_weight_grad/reduce_scatter | solution.py:1158
  194.6 10.3 %copy-start.17 = (f32[2,768]{1,0:T(2,128)S(1)}, f32[2,768]{1,0:T(2,128)}, u32[]{:S(2)}) copy-start(f32[2,768]{1,0:T(2,128)} %get-tuple-element.100) | copy-start | bytes 18436
  204.3 1.9 collective-permute-start.11
  205.5 8.2 %collective-permute-start.12 = (bf16[512,384]{1,0:T(8,128)(2,1)}, bf16[512,384]{1,0:T(8,128)(2,1)S(1)}, u32[]{:S(2)}, u32[]{:S(2)}) collective-permute-start(bf16[512,384]{1,0:T(8,128)(2,1)} %get-tuple-element.99), channel_id=1, source_target_pairs={{0,1},{1,0},{2,3},{3,2},{4,5},{5,4},{6,7},{7,6},{8,9},{9,8},{10,11... | collective-permute-start | bytes 1179656 | tf_op jit(solution)/shard_map/sum_kv_grads/ppermute | solution.py:1189
  207.3 1.5 copy-start.14
  207.3 11.2 %collective-permute-start.13 = (bf16[512,384]{1,0:T(8,128)(2,1)S(1)}, bf16[512,384]{1,0:T(8,128)(2,1)S(1)}, u32[]{:S(2)}, u32[]{:S(2)}) collective-permute-start(bf16[512,384]{1,0:T(8,128)(2,1)S(1)} %add_convert_fusion.3.refs_0_), channel_id=1, source_target_pairs={{0,2},{2,0},{1,3},{3,1},{4,6},{6,4},{5,7},{7,5},{8,10},{10,8},{9,1... | collective-permute-start | bytes 1179656 | tf_op jit(solution)/shard_map/sum_kv_grads/ppermute | solution.py:1190
  213.7 4.8 %copy-start.29 = (bf16[512,384]{1,0:T(8,128)(2,1)}, bf16[512,384]{1,0:T(8,128)(2,1)S(1)}, u32[]{:S(2)}) copy-start(bf16[512,384]{1,0:T(8,128)(2,1)S(1)} %collective-permute-done.12.c_ref) | copy-start | bytes 1179652
  218.5 0.8 copy-start.30
  223.1 2.1 collective-permute-start.14
  226.4 8.6 %copy-start.1 = (bf16[2,208,576]{2,1,0:T(8,128)(2,1)}, bf16[2,208,576]{2,1,0:T(8,128)(2,1)S(1)}, u32[]{:S(2)}) copy-start(bf16[2,208,576]{2,1,0:T(8,128)(2,1)S(1)} %add_convert_fusion.2.refs_1_) | copy-start | bytes 1437700
  226.4 8.5 %collective-permute-start.16 = (bf16[208,576]{1,0:T(8,128)(2,1)S(1)}, bf16[208,576]{1,0:T(8,128)(2,1)S(1)}, u32[]{:S(2)}, u32[]{:S(2)}) collective-permute-start(bf16[208,576]{1,0:T(8,128)(2,1)S(1)} %dynamic-slice_bitcast_fusion.1), channel_id=1, source_target_pairs={{0,2},{2,0},{1,3},{3,1},{4,6},{6,4},{5,7},{7,5},{8,10},{10,8},{9,1... | collective-permute-start | bytes 718856 | tf_op jit(solution)/shard_map/qkv_weight_grad/ppermute | solution.py:848
  231.1 11.5 %collective-permute-start.15 = (bf16[4,64,768]{2,1,0:T(8,128)(2,1)}, bf16[4,64,768]{2,1,0:T(8,128)(2,1)S(1)}, u32[]{:S(2)}, u32[]{:S(2)}) collective-permute-start(bf16[4,64,768]{2,1,0:T(8,128)(2,1)} %get-tuple-element.105), channel_id=1, source_target_pairs={{0,4},{4,0},{1,5},{5,1},{2,6},{6,2},{3,7},{7,3},{8,12},{12,8},{9,1... | collective-permute-start | bytes 1179656 | tf_op jit(solution)/shard_map/qkv_weight_grad/ppermute | solution.py:1211
  236.0 14.5 %all-to-all-start.6 = ((bf16[8,32,576]{2,1,0:T(8,128)(2,1)}), bf16[8,32,576]{2,1,0:T(8,128)(2,1)S(1)}, u32[]{:S(2)}, u32[]{:S(2)}) async-start(bf16[8,32,576]{2,1,0:T(8,128)(2,1)} %maximum_maximum_fusion.refs_1_), calls=%async_computation.7 | async-start | bytes 655360 | tf_op jit(solution)/shard_map/qkv_weight_grad/all_to_all | solution.py:1232
  244.4 13.8 %collective-permute-start.17 = (bf16[2,64,768]{2,1,0:T(8,128)(2,1)}, bf16[2,64,768]{2,1,0:T(8,128)(2,1)S(1)}, u32[]{:S(2)}, u32[]{:S(2)}) collective-permute-start(bf16[2,64,768]{2,1,0:T(8,128)(2,1)} %hold.20), channel_id=1, source_target_pairs={{0,8},{8,0},{1,9},{9,1},{2,10},{10,2},{3,11},{11,3},{4,12},{12,4},... | collective-permute-start | bytes 589832 | tf_op jit(solution)/shard_map/input_grad/ppermute | solution.py:1227
  246.1 12.1 %copy-start.2 = (f32[2,64,768]{2,1,0:T(8,128)S(1)}, f32[2,64,768]{2,1,0:T(8,128)}, u32[]{:S(2)}) copy-start(f32[2,64,768]{2,1,0:T(8,128)} %hold.19) | copy-start | bytes 1179652
  250.5 0.7 copy-start
  254.0 14.2 %all-to-all-start.7 = ((bf16[8,24,1280]{2,1,0:T(8,128)(2,1)}), bf16[8,24,1280]{2,1,0:T(8,128)(2,1)S(1)}, u32[]{:S(2)}, u32[]{:S(2)}) async-start(bf16[8,24,1280]{2,1,0:T(8,128)(2,1)} %bitcast.60.refs_1_), calls=%async_computation.8 | async-start | bytes 983040 | tf_op jit(solution)/shard_map/ff_weight_grads/all_to_all | solution.py:1267
  258.9 9.3 %collective-permute-start.19 = (bf16[96,384]{1,0:T(8,128)(2,1)S(1)}, bf16[96,384]{1,0:T(8,128)(2,1)S(1)}, u32[]{:S(2)}, u32[]{:S(2)}) collective-permute-start(bf16[96,384]{1,0:T(8,128)(2,1)S(1)} %get-tuple-element.120), channel_id=1, source_target_pairs={{0,1},{1,0},{2,3},{3,2},{4,5},{5,4},{6,7},{7,6},{8,9},{9,8},{10,11... | collective-permute-start | bytes 221192 | tf_op jit(solution)/shard_map/ff_weight_grads/ppermute | solution.py:1271
  259.3 8.0 %collective-permute-start.18 = (bf16[64,768]{1,0:T(8,128)(2,1)}, bf16[64,768]{1,0:T(8,128)(2,1)S(1)}, u32[]{:S(2)}, u32[]{:S(2)}) collective-permute-start(bf16[64,768]{1,0:T(8,128)(2,1)} %hold.21), channel_id=1, source_target_pairs={{0,16},{16,0},{1,17},{17,1},{2,18},{18,2},{3,19},{19,3},{4,20},{20... | collective-permute-start | bytes 294920 | tf_op jit(solution)/shard_map/qkv_weight_grad/ppermute | solution.py:1233
  260.0 7.4 %copy-start.12 = (f32[128,768]{1,0:T(8,128)S(1)}, f32[128,768]{1,0:T(8,128)}, u32[]{:S(2)}) copy-start(f32[128,768]{1,0:T(8,128)} %get-tuple-element.87) | copy-start | bytes 1179652
  268.2 0.6 copy-start.16
  268.2 0.8 copy-start.6
Sparse Core Ops, SparseCore 0:
  39.6 54.8 all-gather.2
  194.1 50.0 reduce-scatter.1

commit v4 on v3

--- a/solution.py
+++ b/solution.py
@@ -1154,7 +1154,6 @@
         rows = jnp.concatenate(
             [swap_sum(keep, give, "c"), swap_sum(ff_keep, ff_give, "c")], axis=1
         ).astype(BF16)
-        rows = hold(rows, out_grads)
         row_sums = lax.psum_scatter(rows, RING, scatter_dimension=0, tiled=True)
 
     with jax.named_scope("attention_back"):

time: 280 us -> 279 us (level)
  no operation moved by 1% of the time
where the time goes in v4:
time: 279 us; the launch traced here: 277 us
  Pallas kernels  70.7 us (25%)
  blocking collectives  67.6 us (24%)
  waiting for transfers between devices  46.6 us (17%)
  starting transfers between devices  36.3 us (13%)
  local copies, waits for them, and re-layouts  24.1 us (9%)
  between operations  15.4 us (6%)
  other arithmetic  14.1 us (5%)
    all_gather x2, blocking collectives, gather_plane(): return lax.all_gather(block, PLANE, axis=0, tiled=True)  25.5 us
    all_to_all x1, blocking collectives, body(): lax.all_to_all(attended_low.reshape(8, row_count, GROUP_WIDTH), SEQ_GROUP...  17.1 us
    all_to_all x1, blocking collectives, spread_plane(): lax.all_to_all(parts.reshape(4, -1, parts.shape[1]), PLANE, 0, 0, tiled=T...  15.1 us
    pallas_call x2, Pallas kernels, attend_back(): pl.pallas_call(functools.partial(attend_back_kernel, len(earlier), count,...  14.8 us
    pallas_call x3, Pallas kernels, attend(): pl.pallas_call(functools.partial(attend_kernel, len(earlier), count, firs...  13.1 us
    all_gather x1, blocking collectives, body(): parcels = lax.all_gather(hold(parcel, chunk), CHUNKS, axis=0, tiled=False)  9.83 us
    unnamed x66, local copies, waits for them, and re-layouts  9.13 us
    pallas_call x1, Pallas kernels, ff_backward(): pl.pallas_call(functools.partial(ff_backward_kernel, units, out_columns),...  7.26 us
  transfers between devices with their start and end apart: 28, of which 14 were waited for; matrix products, arithmetic and copies ran while one was open for 10% of the time, Pallas kernels for 18%

profile of v4, /device:TPU:0, one launch (start us, length us, event | category | flops | bytes accessed | tf_op | source)
XLA Modules:
  0.0 277.3 jit_solution(8975946117749138767)
XLA Ops:
  7.2 1.0 constant_dynamic-slice_fusion.9
  8.2 4.1 %collective-permute-start = (bf16[64,768]{1,0:T(8,128)(2,1)S(1)}, bf16[64,768]{1,0:T(8,128)(2,1)S(1)}, u32[]{:S(2)}, u32[]{:S(2)}) collective-permute-start(bf16[64,768]{1,0:T(8,128)(2,1)S(1)} %get-tuple-element.119), channel_id=1, source_target_pairs={{0,16},{16,0},{1,17},{17,1},{2,18},{18,2},{3,19},{19,3},{4,20},{20... | collective-permute-start | bytes 294920 | tf_op jit(solution)/shard_map/gather_tokens/ppermute | solution.py:998
  12.3 0.9 reshape.252
  13.8 1.9 spread.1
  15.6 3.8 %all-to-all-start = ((bf16[8,24,1152]{2,1,0:T(8,128)(2,1)}), bf16[8,24,1152]{2,1,0:T(8,128)(2,1)S(1)}, u32[]{:S(2)}, u32[]{:S(2)}) async-start(bf16[8,24,1152]{2,1,0:T(8,128)(2,1)} %spread.1), calls=%async_computation | async-start | bytes 884736 | tf_op jit(solution)/shard_map/gather_ff_weights/all_to_all | solution.py:938
  20.5 1.6 collective-permute-start.1
  22.2 5.7 %collective-permute-done.1 = bf16[2,64,768]{2,1,0:T(8,128)(2,1)S(1)} collective-permute-done((bf16[2,64,768]{2,1,0:T(8,128)(2,1)S(1)}, bf16[2,64,768]{2,1,0:T(8,128)(2,1)S(1)}, u32[]{:S(2)}, u32[]{:S(2)}) %collective-permute-start.1) | collective-permute-done | bytes 196640 | tf_op jit(solution)/shard_map/gather_tokens/ppermute | solution.py:1000
  28.6 0.9 pad_maximum_fusion.1.refs_1_
  30.0 1.7 collective-permute-start.3
  33.2 3.4 %all-to-all-start.1 = ((bf16[8,24,640]{2,1,0:T(8,128)(2,1)}), bf16[8,24,640]{2,1,0:T(8,128)(2,1)S(1)}, u32[]{:S(2)}, u32[]{:S(2)}) async-start(bf16[8,24,640]{2,1,0:T(8,128)(2,1)} %bitcast.23), calls=%async_computation.1 | async-start | bytes 491520 | tf_op jit(solution)/shard_map/gather_qkv_weights/all_to_all | solution.py:993
  37.3 4.7 %collective-permute-done.3 = bf16[2,2,64,768]{3,2,1,0:T(8,128)(2,1)S(1)} collective-permute-done((bf16[2,2,64,768]{3,2,1,0:T(8,128)(2,1)}, bf16[2,2,64,768]{3,2,1,0:T(8,128)(2,1)S(1)}, u32[]{:S(2)}, u32[]{:S(2)}) %collective-permute-start.3) | collective-permute-done | bytes 393248 | tf_op jit(solution)/shard_map/gather_tokens/ppermute | solution.py:1002
  42.2 1.0 copy.65
  43.2 1.5 all-to-all-done.1.refs_0_
  45.5 9.8 %all-gather = bf16[32,24,640]{2,1,0:T(8,128)(2,1)S(1)} all-gather(bf16[8,24,640]{2,1,0:T(8,128)(2,1)} %hold.12), channel_id=2, replica_groups=mesh['s'=2,'e'=1,'r'=2,'x'=2,'y'=2,'c'=2] {'e','y','c'}, dimensions={0}, use_global_device_ids=true | all-gather | bytes 1228800 | tf_op jit(solution)/shard_map/gather_qkv_weights/all_gather | solution.py:1006
  56.5 1.4 fusion.refs_0_.refs_1_
  59.9 0.8 convert_element_type.113.refs_0_.vec_ref
  61.3 1.1 fusion.1.q_ref
  62.4 5.4 %attend.3 = (f32[192,512]{1,0:T(8,128)}, f32[6,512]{1,0:T(8,128)}) custom-call(f32[3]{0:T(128)} %power_multiply_fusion.slopes_ref, bf16[512,192]{1,0:T(8,128)(2,1)} %fusion.1.q_ref, f32[1,512]{1,0:T(1,128)} %get-tuple-element.130.pq_ref.pk_ref, f32[2,512]{1,0:T(2,128)} %maximum_bitcast_fusion.1.pk_ref, bf16[512,384]{1,0:T(8,128)(2,1)} %fusion.refs_0_.refs_1_, ...), custom_call_target="tpu_custom_call" | custom-call | flops 6442450944 | bytes 524288 | tf_op jit(solution)/shard_map/attention/attend/pallas_call | solution.py:147
  67.8 1.9 collective-permute-done.4.refs_0_
  71.1 3.8 %attend.4 = (f32[192,512]{1,0:T(8,128)}, f32[6,512]{1,0:T(8,128)}) custom-call(f32[3]{0:T(128)} %power_multiply_fusion.slopes_ref, bf16[512,192]{1,0:T(8,128)(2,1)} %fusion.1.q_ref, f32[1,512]{1,0:T(1,128)} %get-tuple-element.130.pq_ref.pk_ref, f32[1,512]{1,0:T(1,128)} %get-tuple-element.127.pk_ref, f32[8,768]{1,0:T(8,128)} %convert_element_type.113.refs_0_.vec_ref, ...), custom_call_target="tpu_custom_call" | custom-call | flops 3221225472 | bytes 262144 | tf_op jit(solution)/shard_map/attention/attend/pallas_call | solution.py:147
  75.6 4.0 %attend.5 = (f32[192,512]{1,0:T(8,128)}, f32[3,512]{1,0:T(4,128)}, bf16[512,192]{1,0:T(8,128)(2,1)}) custom-call(f32[3]{0:T(128)} %power_multiply_fusion.slopes_ref, bf16[512,192]{1,0:T(8,128)(2,1)} %fusion.1.q_ref, f32[1,512]{1,0:T(1,128)} %get-tuple-element.130.pq_ref.pk_ref, f32[1,512]{1,0:T(1,128)} %get-tuple-element.129.pk_ref, ...), custom_call_target="tpu_custom_call" | custom-call | flops 3221225472 | bytes 262144 | tf_op jit(solution)/shard_map/attention/attend/pallas_call | solution.py:147
  79.6 17.1 %all_to_all.40.refs_1_.mixed_ref = bf16[8,64,192]{2,1,0:T(8,128)(2,1)} all-to-all(bf16[8,64,192]{2,1,0:T(8,128)(2,1)} %bitcast.144), channel_id=1, replica_groups=mesh['s'=2,'e'=1,'r'=2,'x'=2,'y'=2,'c'=2] {'s','r','x'}, dimensions={0} | all-to-all | bytes 393216 | tf_op jit(solution)/shard_map/return_attended/all_to_all | solution.py:1090
  96.7 1.1 slice.120.own_ref
  98.0 2.0 collective-permute-done.7.swap_ref
  100.8 3.0 %first_norm.1 = (bf16[128,768]{1,0:T(8,128)(2,1)}, f32[128,768]{1,0:T(8,128)}, f32[128,768]{1,0:T(8,128)}, f32[128,1]{1,0:T(8,128)}) custom-call(s32[1]{0:T(128)} %bitcast.core_ref, bf16[8,64,192]{2,1,0:T(8,128)(2,1)} %all_to_all.40.refs_1_.mixed_ref, bf16[128,768]{1,0:T(8,128)(2,1)} %bitcast.145, f32[8,768]{1,0:T(8,128)} %convert_element_type.113.refs_0_.vec_ref, ...), custom_call_target="tpu_custom_call" | custom-call | flops 4831838208 | bytes 2359296 | tf_op jit(solution)/shard_map/first_norm/first_norm/pallas_call | solution.py:330
  104.7 13.3 %all_gather.18.hidden_ref = bf16[512,768]{1,0:T(8,128)(2,1)} all-gather(bf16[128,768]{1,0:T(8,128)(2,1)S(1)} %copy-done.9), channel_id=1, replica_groups=mesh['s'=2,'e'=1,'r'=2,'x'=2,'y'=2,'c'=2] {'x','y'}, dimensions={0}, use_global_device_ids=true | all-gather | bytes 983040 | tf_op jit(solution)/shard_map/gather_hidden/all_gather | solution.py:852
  118.1 1.4 copy-done.26
  119.5 6.9 %ff_forward.1 = (bf16[512,768]{1,0:T(8,128)(2,1)}, bf16[512,768]{1,0:T(8,128)(2,1)}, bf16[512,768]{1,0:T(8,128)(2,1)}, bf16[512,768]{1,0:T(8,128)(2,1)}) custom-call(s32[1]{0:T(128)} %bitcast.core_ref, bf16[512,768]{1,0:T(8,128)(2,1)} %all_gather.18.hidden_ref, f32[2,768]{1,0:T(2,128)} %reshape.279.refs_1_.bias_ref, bf16[768,1536]{1,0:T(8,128)(2,1)} %hold.15.own_ref, ...), custom_call_target="tpu_custom_call" | custom-call | flops 9663676416 | bytes 3538944 | tf_op jit(solution)/shard_map/ff_forward/ff_forward/pallas_call | solution.py:382
  126.4 15.1 %all_to_all.41.parts_ref = bf16[4,128,768]{2,1,0:T(8,128)(2,1)} all-to-all(bf16[4,128,768]{2,1,0:T(8,128)(2,1)} %bitcast.135), channel_id=1, replica_groups=mesh['s'=2,'e'=1,'r'=2,'x'=2,'y'=2,'c'=2] {'x','y'}, dimensions={0} | all-to-all | bytes 1572864 | tf_op jit(solution)/shard_map/sum_ff/all_to_all | solution.py:856
  141.5 2.5 second_norm.1
  144.0 12.2 %all_gather.19.grad_ref = bf16[512,768]{1,0:T(8,128)(2,1)} all-gather(bf16[128,768]{1,0:T(8,128)(2,1)} %get-tuple-element.75), channel_id=1, replica_groups=mesh['s'=2,'e'=1,'r'=2,'x'=2,'y'=2,'c'=2] {'x','y'}, dimensions={0}, use_global_device_ids=true | all-gather | bytes 983040 | tf_op jit(solution)/shard_map/gather_ff_grad/all_gather | solution.py:852
  156.2 7.3 %ff_backward.1 = (bf16[2,512,768]{2,1,0:T(8,128)(2,1)}, bf16[512,768]{1,0:T(8,128)(2,1)}, f32[2,768]{1,0:T(2,128)}, bf16[2,512,384]{2,1,0:T(8,128)(2,1)}) custom-call(s32[1]{0:T(128)} %bitcast.core_ref, bf16[512,768]{1,0:T(8,128)(2,1)} %all_gather.19.grad_ref, bf16[512,768]{1,0:T(8,128)(2,1)} %get-tuple-element.76.slope_ref, ...), custom_call_target="tpu_custom_call" | custom-call | flops 9663676416 | bytes 3538944 | tf_op jit(solution)/shard_map/ff_backward/ff_backward/pallas_call | solution.py:491
  163.5 3.5 %all-to-all-start.4 = ((bf16[4,128,768]{2,1,0:T(8,128)(2,1)}), bf16[4,128,768]{2,1,0:T(8,128)(2,1)S(1)}, u32[]{:S(2)}, u32[]{:S(2)}) async-start(bf16[4,128,768]{2,1,0:T(8,128)(2,1)} %bitcast.134), calls=%async_computation.4 | async-start | bytes 1572864 | tf_op jit(solution)/shard_map/sum_hidden_grad/all_to_all | solution.py:856
  167.0 6.3 %ff_grads.1 = (bf16[768,1152]{1,0:T(8,128)(2,1)}, bf16[768,1152]{1,0:T(8,128)(2,1)}) custom-call(s32[1]{0:T(128)} %bitcast.core_ref, bf16[512,768]{1,0:T(8,128)(2,1)} %get-tuple-element.83.act_ref, bf16[2,512,384]{2,1,0:T(8,128)(2,1)} %get-tuple-element.84.half_ref, bf16[512,768]{1,0:T(8,128)(2,1)} %all_gather.18.hidden_ref, ...), custom_call_target="tpu_custom_call" | custom-call | flops 6000000000 | bytes 10000 | tf_op jit(solution)/shard_map/ff_weight_grads/ff_grads/pallas_call | solution.py:532
  173.3 1.7 all-to-all-done.4.parts_ref
  175.0 0.9 copy-done.10
  175.9 4.1 %first_back.1 = (f32[128,768]{1,0:T(8,128)}, bf16[8,64,192]{2,1,0:T(8,128)(2,1)}, bf16[768,512]{1,0:T(8,128)(2,1)}, bf16[768,512]{1,0:T(8,128)(2,1)}) custom-call(s32[1]{0:T(128)} %bitcast.core_ref, bf16[4,128,768]{2,1,0:T(8,128)(2,1)} %copy-done.10, f32[128,768]{1,0:T(8,128)} %get-tuple-element.79.second_ref, f32[128,768]{1,0:T(8,128)} %get-tuple-element.80.normal_ref, ...), custom_call_target="tpu_custom_call" | custom-call | flops 4831838208 | bytes 2359296 | tf_op jit(solution)/shard_map/first_norm_back/first_back/pallas_call | solution.py:601
  180.0 4.2 %all-to-all-start.5 = ((bf16[8,64,192]{2,1,0:T(8,128)(2,1)}), bf16[8,64,192]{2,1,0:T(8,128)(2,1)}, u32[]{:S(2)}, u32[]{:S(2)}) async-start(bf16[8,64,192]{2,1,0:T(8,128)(2,1)} %get-tuple-element.88), calls=%async_computation.5 | async-start | bytes 524288 | tf_op jit(solution)/shard_map/send_out_grad/all_to_all | solution.py:1150
  184.3 1.6 add_convert_fusion.1
  186.3 1.6 pad_maximum_fusion.refs_0_
  188.6 5.4 %all-to-all-done.5 = bf16[8,64,192]{2,1,0:T(8,128)(2,1)} async-done(((bf16[8,64,192]{2,1,0:T(8,128)(2,1)}), bf16[8,64,192]{2,1,0:T(8,128)(2,1)}, u32[]{:S(2)}, u32[]{:S(2)}) %all-to-all-start.5) | async-done | bytes 196640 | tf_op jit(solution)/shard_map/send_out_grad/all_to_all | solution.py:1150
  193.9 9.9 %attend_back.2 = (f32[192,512]{1,0:T(8,128)}, bf16[512,384]{1,0:T(8,128)(2,1)}, bf16[512,384]{1,0:T(8,128)(2,1)}, bf16[512,384]{1,0:T(8,128)(2,1)}) custom-call(f32[3]{0:T(128)} %power_multiply_fusion.slopes_ref, bf16[512,192]{1,0:T(8,128)(2,1)} %fusion.1.q_ref, f32[1,512]{1,0:T(1,128)} %get-tuple-element.130.pq_ref.pk_ref, ...), custom_call_target="tpu_custom_call" | custom-call | flops 12683575296 | bytes 786432 | tf_op jit(solution)/shard_map/attention_back/attend_back/pallas_call | solution.py:240
  205.7 1.1 add_convert_fusion.3.refs_0_
  206.9 1.4 collective-permute-start.13
  208.2 4.9 %attend_back.3 = (bf16[512,192]{1,0:T(8,128)(2,1)}, bf16[512,384]{1,0:T(8,128)(2,1)}) custom-call(f32[3]{0:T(128)} %power_multiply_fusion.slopes_ref, bf16[512,192]{1,0:T(8,128)(2,1)} %fusion.1.q_ref, f32[1,512]{1,0:T(1,128)} %get-tuple-element.130.pq_ref.pk_ref, f32[1,512]{1,0:T(1,128)} %get-tuple-element.130.pq_ref.pk_ref, ...), custom_call_target="tpu_custom_call" | custom-call | flops 4227858432 | bytes 262144 | tf_op jit(solution)/shard_map/attention_back/attend_back/pallas_call | solution.py:240
  213.1 5.0 %collective-permute-done.13.y_ref = bf16[512,384]{1,0:T(8,128)(2,1)S(1)} collective-permute-done((bf16[512,384]{1,0:T(8,128)(2,1)S(1)}, bf16[512,384]{1,0:T(8,128)(2,1)S(1)}, u32[]{:S(2)}, u32[]{:S(2)}) %collective-permute-start.13) | collective-permute-done | bytes 393248 | tf_op jit(solution)/shard_map/sum_kv_grads/ppermute | solution.py:1189
  218.8 3.8 %qkv_weight.1 = (bf16[2,208,576]{2,1,0:T(8,128)(2,1)}, bf16[2,208,576]{2,1,0:T(8,128)(2,1)}, bf16[512,576]{1,0:T(8,128)(2,1)}) custom-call(s32[3]{0:T(128)} %pad_add_fusion.place_ref, bf16[512,192]{1,0:T(8,128)(2,1)} %get-tuple-element.97.dq_ref, bf16[512,384]{1,0:T(8,128)(2,1)} %get-tuple-element.98.own_ref, bf16[512,384]{1,0:T(8,128)(2,1)} %copy-done.29, ...), custom_call_target="tpu_custom_call" | custom-call | flops 3170893824 | bytes 1572864 | tf_op jit(solution)/shard_map/qkv_weight_grad/qkv_weight/pallas_call | solution.py:700
  222.6 2.1 collective-permute-done.14
  224.7 1.2 add_convert_fusion.2.refs_1_
  226.0 1.3 collective-permute-start.16
  227.4 3.1 %input_back.1 = (bf16[4,64,768]{2,1,0:T(8,128)(2,1)}, bf16[4,64,768]{2,1,0:T(8,128)(2,1)}) custom-call(s32[3]{0:T(128)} %pad_add_fusion.place_ref, bf16[512,576]{1,0:T(8,128)(2,1)} %get-tuple-element.101.grad_ref, bf16[768,576]{1,0:T(8,128)(2,1)} %bitcast.131), custom_call_target="tpu_custom_call" | custom-call | flops 2264924160 | bytes 1572864 | tf_op jit(solution)/shard_map/qkv_weight_grad/input_back/pallas_call | solution.py:636
  230.5 1.4 collective-permute-start.15
  231.9 2.6 collective-permute-done.16
  234.7 0.8 maximum_maximum_fusion.refs_1_
  235.5 3.4 %all-to-all-start.6 = ((bf16[8,32,576]{2,1,0:T(8,128)(2,1)}), bf16[8,32,576]{2,1,0:T(8,128)(2,1)S(1)}, u32[]{:S(2)}, u32[]{:S(2)}) async-start(bf16[8,32,576]{2,1,0:T(8,128)(2,1)} %maximum_maximum_fusion.refs_1_), calls=%async_computation.7 | async-start | bytes 655360 | tf_op jit(solution)/shard_map/qkv_weight_grad/all_to_all | solution.py:1231
  239.0 3.0 %collective-permute-done.15 = bf16[4,64,768]{2,1,0:T(8,128)(2,1)S(1)} collective-permute-done((bf16[4,64,768]{2,1,0:T(8,128)(2,1)}, bf16[4,64,768]{2,1,0:T(8,128)(2,1)S(1)}, u32[]{:S(2)}, u32[]{:S(2)}) %collective-permute-start.15) | collective-permute-done | bytes 393248 | tf_op jit(solution)/shard_map/qkv_weight_grad/ppermute | solution.py:1210
  242.0 1.1 convert_add_fusion
  245.3 4.6 %all-to-all-done.6.refs_1_.refs_0_ = bf16[8,32,576]{2,1,0:T(8,128)(2,1)S(1)} async-done(((bf16[8,32,576]{2,1,0:T(8,128)(2,1)}), bf16[8,32,576]{2,1,0:T(8,128)(2,1)S(1)}, u32[]{:S(2)}, u32[]{:S(2)}) %all-to-all-start.6) | async-done | bytes 294944 | tf_op jit(solution)/shard_map/qkv_weight_grad/all_to_all | solution.py:1231
  250.6 1.8 slice.124
  252.4 0.9 slice.125
  253.4 3.5 %all-to-all-start.7 = ((bf16[8,24,1280]{2,1,0:T(8,128)(2,1)}), bf16[8,24,1280]{2,1,0:T(8,128)(2,1)S(1)}, u32[]{:S(2)}, u32[]{:S(2)}) async-start(bf16[8,24,1280]{2,1,0:T(8,128)(2,1)} %bitcast.60.refs_1_), calls=%async_computation.8 | async-start | bytes 983040 | tf_op jit(solution)/shard_map/ff_weight_grads/all_to_all | solution.py:1266
  258.7 1.9 share.1
  260.5 6.1 %collective-permute-done.18 = bf16[64,768]{1,0:T(8,128)(2,1)S(1)} collective-permute-done((bf16[64,768]{1,0:T(8,128)(2,1)}, bf16[64,768]{1,0:T(8,128)(2,1)S(1)}, u32[]{:S(2)}, u32[]{:S(2)}) %collective-permute-start.18) | collective-permute-done | bytes 98336 | tf_op jit(solution)/shard_map/qkv_weight_grad/ppermute | solution.py:1232
  268.4 2.1 unpack.1
  (170 shorter events, 23.2 us)
Async XLA Ops:
  7.2 12.3 %copy-start.18 = (s32[2,256]{1,0:T(2,128)S(1)}, s32[2,256]{1,0:T(2,128)}, u32[]{:S(2)}) copy-start(s32[2,256]{1,0:T(2,128)} %param.16) | copy-start | bytes 6148
  7.2 12.4 %copy-start.31 = (bf16[192]{0:T(256)(128)(2,1)S(1)}, bf16[192]{0:T(256)(128)(2,1)}, u32[]{:S(2)}) copy-start(bf16[192]{0:T(256)(128)(2,1)} %param.24) | copy-start | bytes 1156
  7.2 12.5 %copy-start.15 = (bf16[24,2304]{1,0:T(8,128)(2,1)S(1)}, bf16[24,2304]{1,0:T(8,128)(2,1)}, u32[]{:S(2)}) copy-start(bf16[24,2304]{1,0:T(8,128)(2,1)} %param.17) | copy-start | bytes 331780
  8.2 12.2 %collective-permute-start = (bf16[64,768]{1,0:T(8,128)(2,1)S(1)}, bf16[64,768]{1,0:T(8,128)(2,1)S(1)}, u32[]{:S(2)}, u32[]{:S(2)}) collective-permute-start(bf16[64,768]{1,0:T(8,128)(2,1)S(1)} %get-tuple-element.119), channel_id=1, source_target_pairs={{0,16},{16,0},{1,17},{17,1},{2,18},{18,2},{3,19},{19,3},{4,20},{20... | collective-permute-start | bytes 294920 | tf_op jit(solution)/shard_map/gather_tokens/ppermute | solution.py:998
  13.3 6.8 %copy-start.19 = (bf16[2,24]{1,0:T(2,128)(2,1)S(1)}, bf16[2,24]{1,0:T(2,128)(2,1)}, u32[]{:S(2)}) copy-start(bf16[2,24]{1,0:T(2,128)(2,1)} %param.18) | copy-start | bytes 292
  13.3 6.8 %copy-start.20 = (bf16[24]{0:T(256)(128)(2,1)S(1)}, bf16[24]{0:T(256)(128)(2,1)}, u32[]{:S(2)}) copy-start(bf16[24]{0:T(256)(128)(2,1)} %param.20) | copy-start | bytes 148
  13.3 6.8 %copy-start.21 = (bf16[24]{0:T(256)(128)(2,1)S(1)}, bf16[24]{0:T(256)(128)(2,1)}, u32[]{:S(2)}) copy-start(bf16[24]{0:T(256)(128)(2,1)} %param.21) | copy-start | bytes 148
  13.3 6.8 %copy-start.22 = (bf16[24]{0:T(256)(128)(2,1)S(1)}, bf16[24]{0:T(256)(128)(2,1)}, u32[]{:S(2)}) copy-start(bf16[24]{0:T(256)(128)(2,1)} %param.22) | copy-start | bytes 148
  13.3 6.8 %copy-start.23 = (bf16[24]{0:T(256)(128)(2,1)S(1)}, bf16[24]{0:T(256)(128)(2,1)}, u32[]{:S(2)}) copy-start(bf16[24]{0:T(256)(128)(2,1)} %param.26) | copy-start | bytes 148
  13.3 6.8 %copy-start.24 = (bf16[24]{0:T(256)(128)(2,1)S(1)}, bf16[24]{0:T(256)(128)(2,1)}, u32[]{:S(2)}) copy-start(bf16[24]{0:T(256)(128)(2,1)} %param.27) | copy-start | bytes 148
  13.3 6.8 %copy-start.25 = (bf16[24]{0:T(256)(128)(2,1)S(1)}, bf16[24]{0:T(256)(128)(2,1)}, u32[]{:S(2)}) copy-start(bf16[24]{0:T(256)(128)(2,1)} %param.28) | copy-start | bytes 148
  13.7 8.4 %collective-permute-start.2 = (bf16[96,384]{1,0:T(8,128)(2,1)S(1)}, bf16[96,384]{1,0:T(8,128)(2,1)S(1)}, u32[]{:S(2)}, u32[]{:S(2)}) collective-permute-start(bf16[96,384]{1,0:T(8,128)(2,1)S(1)} %bitcast.147), channel_id=1, source_target_pairs={{0,1},{1,0},{2,3},{3,2},{4,5},{5,4},{6,7},{7,6},{8,9},{9,8},{10,11... | collective-permute-start | bytes 221192 | tf_op jit(solution)/shard_map/gather_ff_weights/ppermute | solution.py:943
  15.6 13.0 %all-to-all-start = ((bf16[8,24,1152]{2,1,0:T(8,128)(2,1)}), bf16[8,24,1152]{2,1,0:T(8,128)(2,1)S(1)}, u32[]{:S(2)}, u32[]{:S(2)}) async-start(bf16[8,24,1152]{2,1,0:T(8,128)(2,1)} %spread.1), calls=%async_computation | async-start | bytes 884736 | tf_op jit(solution)/shard_map/gather_ff_weights/all_to_all | solution.py:938
  20.5 7.4 %collective-permute-start.1 = (bf16[2,64,768]{2,1,0:T(8,128)(2,1)S(1)}, bf16[2,64,768]{2,1,0:T(8,128)(2,1)S(1)}, u32[]{:S(2)}, u32[]{:S(2)}) collective-permute-start(bf16[2,64,768]{2,1,0:T(8,128)(2,1)S(1)} %maximum_select_fusion.4), channel_id=1, source_target_pairs={{0,8},{8,0},{1,9},{9,1},{2,10},{10,2},{3,11},{11,3},{4,12},{12,4},... | collective-permute-start | bytes 589832 | tf_op jit(solution)/shard_map/gather_tokens/ppermute | solution.py:1000
  30.0 12.0 %copy-start.3 = (bf16[2,2,64,768]{3,2,1,0:T(8,128)(2,1)S(1)}, bf16[2,2,64,768]{3,2,1,0:T(8,128)(2,1)}, u32[]{:S(2)}) copy-start(bf16[2,2,64,768]{3,2,1,0:T(8,128)(2,1)} %hold.11) | copy-start | bytes 1179652
  30.0 12.0 %collective-permute-start.3 = (bf16[2,2,64,768]{3,2,1,0:T(8,128)(2,1)}, bf16[2,2,64,768]{3,2,1,0:T(8,128)(2,1)S(1)}, u32[]{:S(2)}, u32[]{:S(2)}) collective-permute-start(bf16[2,2,64,768]{3,2,1,0:T(8,128)(2,1)} %hold.11), channel_id=1, source_target_pairs={{0,4},{4,0},{1,5},{5,1},{2,6},{6,2},{3,7},{7,3},{8,12},{12,8},{9,1... | collective-permute-start | bytes 1179656 | tf_op jit(solution)/shard_map/gather_tokens/ppermute | solution.py:1002
  33.2 11.6 %all-to-all-start.1 = ((bf16[8,24,640]{2,1,0:T(8,128)(2,1)}), bf16[8,24,640]{2,1,0:T(8,128)(2,1)S(1)}, u32[]{:S(2)}, u32[]{:S(2)}) async-start(bf16[8,24,640]{2,1,0:T(8,128)(2,1)} %bitcast.23), calls=%async_computation.1 | async-start | bytes 491520 | tf_op jit(solution)/shard_map/gather_qkv_weights/all_to_all | solution.py:993
  36.6 60.2 %all-gather.3.cloned.1.call-start = ((), (), s32[]{:S(2)}) async-start(), calls=%async_computation.9 | async-start | bytes 2949120 | tf_op jit(solution)/shard_map/gather_ff_weights/all_gather | solution.py:1031
  44.8 0.7 copy-start.5
  55.3 1.2 copy-start.4
  55.5 6.9 %copy-start.8 = (bf16[2,1,2,2,2,2,24,576]{7,6,5,4,3,2,0,1:T(8,128)(2,1)}, bf16[2,1,2,2,2,2,24,576]{7,6,5,4,3,2,0,1:T(8,128)(2,1)S(1)}, u32[]{:S(2)}) copy-start(bf16[2,1,2,2,2,2,24,576]{7,6,5,4,3,2,0,1:T(8,128)(2,1)S(1)} %copy.69) | copy-start | bytes 2654212
  57.9 4.5 %collective-permute-start.5 = (bf16[512,384]{1,0:T(8,128)(2,1)}, bf16[512,384]{1,0:T(8,128)(2,1)}, u32[]{:S(2)}, u32[]{:S(2)}) collective-permute-start(bf16[512,384]{1,0:T(8,128)(2,1)} %fusion.refs_0_.refs_1_), channel_id=1, source_target_pairs={{0,1},{1,0},{2,3},{3,2},{4,5},{5,4},{6,7},{7,6},{8,9},{9,8},{10,11... | collective-permute-start | bytes 1179656 | tf_op jit(solution)/shard_map/gather_kv/ppermute | solution.py:1051
  58.3 11.4 %collective-permute-start.4 = (bf16[512,384]{1,0:T(8,128)(2,1)}, bf16[512,384]{1,0:T(8,128)(2,1)S(1)}, u32[]{:S(2)}, u32[]{:S(2)}) collective-permute-start(bf16[512,384]{1,0:T(8,128)(2,1)} %fusion.refs_0_.refs_1_), channel_id=1, source_target_pairs={{0,2},{2,0},{1,3},{3,1},{4,6},{6,4},{5,7},{7,5},{8,10},{10,8},{9,1... | collective-permute-start | bytes 1179656 | tf_op jit(solution)/shard_map/gather_kv/ppermute | solution.py:1050
  69.7 0.7 copy-start.13
  70.4 4.5 %collective-permute-start.6 = (bf16[512,384]{1,0:T(8,128)(2,1)}, bf16[512,384]{1,0:T(8,128)(2,1)S(1)}, u32[]{:S(2)}, u32[]{:S(2)}) collective-permute-start(bf16[512,384]{1,0:T(8,128)(2,1)} %hold.13.refs_2_), channel_id=1, source_target_pairs={{0,1},{1,0},{2,3},{3,2},{4,5},{5,4},{6,7},{7,6},{8,9},{9,8},{10,11... | collective-permute-start | bytes 1179656 | tf_op jit(solution)/shard_map/attention/ppermute | solution.py:1086
  74.9 0.8 copy-start.28
  97.9 2.1 copy-start.11
  97.9 2.1 collective-permute-start.7
  99.9 0.8 copy-start.27
  103.8 0.9 copy-start.9
  103.8 14.3 %collective-permute-start.8 = (bf16[768,1536]{1,0:T(8,128)(2,1)}, bf16[768,1536]{1,0:T(8,128)(2,1)S(1)}, u32[]{:S(2)}, u32[]{:S(2)}) collective-permute-start(bf16[768,1536]{1,0:T(8,128)(2,1)} %hold.15.own_ref), channel_id=1, source_target_pairs={{0,1},{1,0},{2,3},{3,2},{4,5},{5,4},{6,7},{7,6},{8,9},{9,8},{10,11... | collective-permute-start | bytes 7077896 | tf_op jit(solution)/shard_map/first_norm/ppermute | solution.py:1106
  118.1 1.4 copy-start.26
  163.5 11.5 %all-to-all-start.4 = ((bf16[4,128,768]{2,1,0:T(8,128)(2,1)}), bf16[4,128,768]{2,1,0:T(8,128)(2,1)S(1)}, u32[]{:S(2)}, u32[]{:S(2)}) async-start(bf16[4,128,768]{2,1,0:T(8,128)(2,1)} %bitcast.134), calls=%async_computation.4 | async-start | bytes 1572864 | tf_op jit(solution)/shard_map/sum_hidden_grad/all_to_all | solution.py:856
  173.3 12.6 %collective-permute-start.10 = (bf16[768,1152]{1,0:T(8,128)(2,1)}, bf16[768,1152]{1,0:T(8,128)(2,1)S(1)}, u32[]{:S(2)}, u32[]{:S(2)}) collective-permute-start(bf16[768,1152]{1,0:T(8,128)(2,1)} %get-tuple-element.93), channel_id=1, source_target_pairs={{0,1},{1,0},{2,3},{3,2},{4,5},{5,4},{6,7},{7,6},{8,9},{9,8},{10,11... | collective-permute-start | bytes 5308424 | tf_op jit(solution)/shard_map/attn_weight_grad/ppermute | solution.py:848
  175.0 0.9 copy-start.10
  180.0 5.9 %copy-start.7 = (bf16[768,1152]{1,0:T(8,128)(2,1)S(1)}, bf16[768,1152]{1,0:T(8,128)(2,1)}, u32[]{:S(2)}) copy-start(bf16[768,1152]{1,0:T(8,128)(2,1)} %get-tuple-element.86._) | copy-start | bytes 5308420
  180.0 4.3 %collective-permute-start.9 = (bf16[768,512]{1,0:T(8,128)(2,1)}, bf16[768,512]{1,0:T(8,128)(2,1)}, u32[]{:S(2)}, u32[]{:S(2)}) collective-permute-start(bf16[768,512]{1,0:T(8,128)(2,1)} %get-tuple-element.92), channel_id=1, source_target_pairs={{0,1},{1,0},{2,3},{3,2},{4,5},{5,4},{6,7},{7,6},{8,9},{9,8},{10,11... | collective-permute-start | bytes 2359304 | tf_op jit(solution)/shard_map/attn_weight_grad/ppermute | solution.py:848
  180.0 13.9 %all-to-all-start.5 = ((bf16[8,64,192]{2,1,0:T(8,128)(2,1)}), bf16[8,64,192]{2,1,0:T(8,128)(2,1)}, u32[]{:S(2)}, u32[]{:S(2)}) async-start(bf16[8,64,192]{2,1,0:T(8,128)(2,1)} %get-tuple-element.88), calls=%async_computation.5 | async-start | bytes 524288 | tf_op jit(solution)/shard_map/send_out_grad/all_to_all | solution.py:1150
  184.2 59.6 %reduce-scatter.2.cloned.1.call-start = ((), (), s32[]{:S(2)}) async-start(), calls=%async_computation.10 | async-start | bytes 3194880 | tf_op jit(solution)/shard_map/attn_weight_grad/reduce_scatter | solution.py:1157
  193.9 10.5 %copy-start.17 = (f32[2,768]{1,0:T(2,128)S(1)}, f32[2,768]{1,0:T(2,128)}, u32[]{:S(2)}) copy-start(f32[2,768]{1,0:T(2,128)} %get-tuple-element.100) | copy-start | bytes 18436
  203.8 1.9 collective-permute-start.11
  205.1 8.0 %collective-permute-start.12 = (bf16[512,384]{1,0:T(8,128)(2,1)}, bf16[512,384]{1,0:T(8,128)(2,1)S(1)}, u32[]{:S(2)}, u32[]{:S(2)}) collective-permute-start(bf16[512,384]{1,0:T(8,128)(2,1)} %get-tuple-element.99), channel_id=1, source_target_pairs={{0,1},{1,0},{2,3},{3,2},{4,5},{5,4},{6,7},{7,6},{8,9},{9,8},{10,11... | collective-permute-start | bytes 1179656 | tf_op jit(solution)/shard_map/sum_kv_grads/ppermute | solution.py:1188
  206.8 1.4 copy-start.14
  206.9 11.2 %collective-permute-start.13 = (bf16[512,384]{1,0:T(8,128)(2,1)S(1)}, bf16[512,384]{1,0:T(8,128)(2,1)S(1)}, u32[]{:S(2)}, u32[]{:S(2)}) collective-permute-start(bf16[512,384]{1,0:T(8,128)(2,1)S(1)} %add_convert_fusion.3.refs_0_), channel_id=1, source_target_pairs={{0,2},{2,0},{1,3},{3,1},{4,6},{6,4},{5,7},{7,5},{8,10},{10,8},{9,1... | collective-permute-start | bytes 1179656 | tf_op jit(solution)/shard_map/sum_kv_grads/ppermute | solution.py:1189
  213.1 5.0 %copy-start.29 = (bf16[512,384]{1,0:T(8,128)(2,1)}, bf16[512,384]{1,0:T(8,128)(2,1)S(1)}, u32[]{:S(2)}) copy-start(bf16[512,384]{1,0:T(8,128)(2,1)S(1)} %collective-permute-done.12.c_ref) | copy-start | bytes 1179652
  218.1 0.8 copy-start.30
  222.6 2.1 collective-permute-start.14
  225.9 8.6 %copy-start.1 = (bf16[2,208,576]{2,1,0:T(8,128)(2,1)}, bf16[2,208,576]{2,1,0:T(8,128)(2,1)S(1)}, u32[]{:S(2)}) copy-start(bf16[2,208,576]{2,1,0:T(8,128)(2,1)S(1)} %add_convert_fusion.2.refs_1_) | copy-start | bytes 1437700
  226.0 8.5 %collective-permute-start.16 = (bf16[208,576]{1,0:T(8,128)(2,1)S(1)}, bf16[208,576]{1,0:T(8,128)(2,1)S(1)}, u32[]{:S(2)}, u32[]{:S(2)}) collective-permute-start(bf16[208,576]{1,0:T(8,128)(2,1)S(1)} %dynamic-slice_bitcast_fusion.1), channel_id=1, source_target_pairs={{0,2},{2,0},{1,3},{3,1},{4,6},{6,4},{5,7},{7,5},{8,10},{10,8},{9,1... | collective-permute-start | bytes 718856 | tf_op jit(solution)/shard_map/qkv_weight_grad/ppermute | solution.py:848
  230.5 11.5 %collective-permute-start.15 = (bf16[4,64,768]{2,1,0:T(8,128)(2,1)}, bf16[4,64,768]{2,1,0:T(8,128)(2,1)S(1)}, u32[]{:S(2)}, u32[]{:S(2)}) collective-permute-start(bf16[4,64,768]{2,1,0:T(8,128)(2,1)} %get-tuple-element.105), channel_id=1, source_target_pairs={{0,4},{4,0},{1,5},{5,1},{2,6},{6,2},{3,7},{7,3},{8,12},{12,8},{9,1... | collective-permute-start | bytes 1179656 | tf_op jit(solution)/shard_map/qkv_weight_grad/ppermute | solution.py:1210
  235.5 14.3 %all-to-all-start.6 = ((bf16[8,32,576]{2,1,0:T(8,128)(2,1)}), bf16[8,32,576]{2,1,0:T(8,128)(2,1)S(1)}, u32[]{:S(2)}, u32[]{:S(2)}) async-start(bf16[8,32,576]{2,1,0:T(8,128)(2,1)} %maximum_maximum_fusion.refs_1_), calls=%async_computation.7 | async-start | bytes 655360 | tf_op jit(solution)/shard_map/qkv_weight_grad/all_to_all | solution.py:1231
  243.8 13.7 %collective-permute-start.17 = (bf16[2,64,768]{2,1,0:T(8,128)(2,1)}, bf16[2,64,768]{2,1,0:T(8,128)(2,1)S(1)}, u32[]{:S(2)}, u32[]{:S(2)}) collective-permute-start(bf16[2,64,768]{2,1,0:T(8,128)(2,1)} %hold.18), channel_id=1, source_target_pairs={{0,8},{8,0},{1,9},{9,1},{2,10},{10,2},{3,11},{11,3},{4,12},{12,4},... | collective-permute-start | bytes 589832 | tf_op jit(solution)/shard_map/input_grad/ppermute | solution.py:1226
  245.3 12.3 %copy-start.2 = (f32[2,64,768]{2,1,0:T(8,128)S(1)}, f32[2,64,768]{2,1,0:T(8,128)}, u32[]{:S(2)}) copy-start(f32[2,64,768]{2,1,0:T(8,128)} %hold.17) | copy-start | bytes 1179652
  249.8 0.7 copy-start
  253.4 14.2 %all-to-all-start.7 = ((bf16[8,24,1280]{2,1,0:T(8,128)(2,1)}), bf16[8,24,1280]{2,1,0:T(8,128)(2,1)S(1)}, u32[]{:S(2)}, u32[]{:S(2)}) async-start(bf16[8,24,1280]{2,1,0:T(8,128)(2,1)} %bitcast.60.refs_1_), calls=%async_computation.8 | async-start | bytes 983040 | tf_op jit(solution)/shard_map/ff_weight_grads/all_to_all | solution.py:1266
  258.3 9.3 %collective-permute-start.19 = (bf16[96,384]{1,0:T(8,128)(2,1)S(1)}, bf16[96,384]{1,0:T(8,128)(2,1)S(1)}, u32[]{:S(2)}, u32[]{:S(2)}) collective-permute-start(bf16[96,384]{1,0:T(8,128)(2,1)S(1)} %get-tuple-element.120), channel_id=1, source_target_pairs={{0,1},{1,0},{2,3},{3,2},{4,5},{5,4},{6,7},{7,6},{8,9},{9,8},{10,11... | collective-permute-start | bytes 221192 | tf_op jit(solution)/shard_map/ff_weight_grads/ppermute | solution.py:1270
  258.6 8.0 %collective-permute-start.18 = (bf16[64,768]{1,0:T(8,128)(2,1)}, bf16[64,768]{1,0:T(8,128)(2,1)S(1)}, u32[]{:S(2)}, u32[]{:S(2)}) collective-permute-start(bf16[64,768]{1,0:T(8,128)(2,1)} %hold.19), channel_id=1, source_target_pairs={{0,16},{16,0},{1,17},{17,1},{2,18},{18,2},{3,19},{19,3},{4,20},{20... | collective-permute-start | bytes 294920 | tf_op jit(solution)/shard_map/qkv_weight_grad/ppermute | solution.py:1232
  258.7 8.0 %copy-start.12 = (f32[128,768]{1,0:T(8,128)S(1)}, f32[128,768]{1,0:T(8,128)}, u32[]{:S(2)}) copy-start(f32[128,768]{1,0:T(8,128)} %get-tuple-element.87) | copy-start | bytes 1179652
  267.5 0.6 copy-start.16
  267.5 0.8 copy-start.6
Sparse Core Ops, SparseCore 0:
  39.6 54.8 all-gather.2
  188.1 52.3 reduce-scatter.1
